TPU v7x, 32 devices: a whole 2x2x4 slice. The times are simulated.
32 devices in a mesh: seq: 4 (over x, core), rep: 8 (over z, y).
Axes of the slice: x: 2, y: 2, z: 4, core: 2. Of those that a mesh axis runs over, the one named last changes fastest.
Arguments:
- tokens: bfloat16 [8, 512, 2048], P('rep', 'seq'), may hold values from -6 to 6
- segment_ids: int32 [8, 512], P('rep', 'seq'), may hold values from 0 to 5, never falling along the last dimension, each value on 1 to 256 neighbouring positions
- cotangent: bfloat16 [8, 512, 2048], P('rep', 'seq'), may hold values from -6 to 6
- attn_gain: bfloat16 [2048], P(('seq', 'rep')), may hold values from 0.099609375 to 1.8984375
- w_qkv: bfloat16 [2048, 1920], P(('seq', 'rep')), may hold values from -0.125 to 0.125
- w_out: bfloat16 [2048, 1280], P(('seq', 'rep')), may hold values from -0.5 to 0.5
- ffn_gain: bfloat16 [2048], P(('seq', 'rep')), may hold values from 0.099609375 to 1.8984375
- w_gate: bfloat16 [2048, 3584], P(('seq', 'rep')), may hold values from -0.125 to 0.125
- w_up: bfloat16 [2048, 3584], P(('seq', 'rep')), may hold values from -0.125 to 0.125
- w_down: bfloat16 [2048, 3584], P(('seq', 'rep')), may hold values from -0.09375 to 0.09375
- q_gain: bfloat16 [64], replicated, may hold values from 0.099609375 to 1.8984375
- k_gain: bfloat16 [64], replicated, may hold values from 0.099609375 to 1.8984375
Outputs:
- activations: bfloat16 [8, 512, 2048], P('rep', 'seq')
- grad_tokens: float32 [8, 512, 2048], P('rep', 'seq')
- grad_attn_gain: float32 [2048], P(('seq', 'rep'))
- grad_qkv: float32 [2048, 1920], P(('seq', 'rep'))
- grad_out: float32 [2048, 1280], P(('seq', 'rep'))
- grad_ffn_gain: float32 [2048], P(('seq', 'rep'))
- grad_gate: float32 [2048, 3584], P(('seq', 'rep'))
- grad_up: float32 [2048, 3584], P(('seq', 'rep'))
- grad_down: float32 [2048, 3584], P(('seq', 'rep'))
- grad_q_gain: float32 [64], replicated
- grad_k_gain: float32 [64], replicated
All inputs are finite; a program needn't handle non-finite values.
Results may differ from a plain program's by a relative error of at most 0.015.
Values may be sent and summed in bfloat16 or wider, within the bound.
A program may use at most 384 MiB of HBM per device.

v0:
```python
import jax
import jax.numpy as jnp
from jax import lax
from jax.sharding import PartitionSpec as P

QH = 20
KVG = 5
HD = 64
QW = 1280
KW = 320


norm_eps = 1e-06
rope_base = 10000.0


def norm_rows(value_matrix, gain):
    return (
        value_matrix
        * lax.rsqrt(jnp.mean(value_matrix * value_matrix, axis=-1, keepdims=True) + norm_eps)
        * gain
    )


def rotate_heads(value_matrix, positions):
    half = value_matrix.shape[-1] // 2
    freqs = rope_base ** (-jnp.arange(half, dtype=jnp.float32) * 2.0 / value_matrix.shape[-1])
    angles = positions.astype(jnp.float32)[:, None] * freqs[None, :]
    cosine = jnp.cos(angles)[:, None, :]
    sine = jnp.sin(angles)[:, None, :]
    first = value_matrix[..., :half]
    second = value_matrix[..., half:]
    return jnp.concatenate(
        [first * cosine - second * sine, second * cosine + first * sine], axis=-1
    )


def heads_prep(qkv, q_scale, k_scale, positions):
    count = qkv.shape[0]
    query = qkv[:, :QW].reshape(count, QH, HD)
    key = qkv[:, QW : QW + KW].reshape(count, KVG, HD)
    value = qkv[:, QW + KW :].reshape(count, KVG, HD)
    query = rotate_heads(norm_rows(query, q_scale), positions)
    key = rotate_heads(norm_rows(key, k_scale), positions)
    return (query, key, value)


def times_rows(left, right):
    return lax.dot_general(
        left, right, (((1,), (1,)), ((), ())), preferred_element_type=jnp.float32
    )


def token_sum(left, right):
    return lax.dot_general(
        left, right, (((0,), (0,)), ((), ())), preferred_element_type=jnp.float32
    )


def block_scores(query_block, key_matrix, seg_row, start, score_scale):
    width = query_block.shape[1]
    length = key_matrix.shape[1]
    logit_scores = (
        jnp.einsum("zjfr,zyr->zfjy", query_block, key_matrix, preferred_element_type=jnp.float32)
        * score_scale
    )
    rows = start + jnp.arange(width, dtype=jnp.int32)
    cols = jnp.arange(length, dtype=jnp.int32)
    seg_blk = lax.dynamic_slice_in_dim(seg_row, start, width, 1)
    allowed = (cols[None, None, :] <= rows[None, :, None]) & (
        seg_row[:, None, :] == seg_blk[:, :, None]
    )
    return jnp.where(allowed[:, None], logit_scores, -1e30)


def attend_forward(query, key_matrix, value_matrix, seg_row, block):
    length = key_matrix.shape[1]
    score_scale = HD ** (-0.5)

    def one_block(start):
        query_block = lax.dynamic_slice_in_dim(query, start, block, 1)
        logit_scores = block_scores(query_block, key_matrix, seg_row, start, score_scale)
        top = jnp.max(logit_scores, axis=-1, keepdims=True)
        weights = jnp.exp(logit_scores - top)
        total = jnp.sum(weights, axis=-1, keepdims=True)
        attention_probabilities = (weights / total).astype(jnp.bfloat16)
        layer_result = jnp.einsum(
            "szjr,srn->sjzn",
            attention_probabilities,
            value_matrix,
            preferred_element_type=jnp.float32,
        )
        return (layer_result.astype(jnp.bfloat16), (top + jnp.log(total))[..., 0])

    starts = jnp.arange(0, length, block, dtype=jnp.int32)
    return lax.map(one_block, starts)


def attend_backward(query, key_matrix, value_matrix, seg_row, grads_out, lse, block):
    length = key_matrix.shape[1]
    score_scale = HD ** (-0.5)

    def one_block(carry, item):
        d_key, d_value = carry
        start, sums = item
        query_block = lax.dynamic_slice_in_dim(query, start, block, 1)
        gradient_block = lax.dynamic_slice_in_dim(grads_out, start, block, 1)
        logit_scores = block_scores(query_block, key_matrix, seg_row, start, score_scale)
        attention_probabilities = jnp.exp(logit_scores - sums[..., None])
        reduced_probabilities = attention_probabilities.astype(jnp.bfloat16)
        d_value = d_value + jnp.einsum(
            "syer,seyo->sro",
            reduced_probabilities,
            gradient_block,
            preferred_element_type=jnp.float32,
        )
        probability_gradient = jnp.einsum(
            "zjfr,zyr->zfjy", gradient_block, value_matrix, preferred_element_type=jnp.float32
        )
        inner = jnp.sum(attention_probabilities * probability_gradient, axis=-1, keepdims=True)
        score_gradient = (attention_probabilities * (probability_gradient - inner)).astype(
            jnp.bfloat16
        )
        d_query = (
            jnp.einsum(
                "szjr,srn->sjzn", score_gradient, key_matrix, preferred_element_type=jnp.float32
            )
            * score_scale
        )
        d_key = (
            d_key
            + jnp.einsum(
                "syer,seyo->sro", score_gradient, query_block, preferred_element_type=jnp.float32
            )
            * score_scale
        )
        return ((d_key, d_value), d_query)

    starts = jnp.arange(0, length, block, dtype=jnp.int32)
    zeros = jnp.zeros(key_matrix.shape, jnp.float32)
    carry, d_query = lax.scan(one_block, (zeros, zeros), (starts, lse))
    return (d_query, carry[0], carry[1])


def shards(
    tokens,
    segment_ids,
    cotangent,
    attn_gain,
    w_qkv,
    w_out,
    ffn_gain,
    w_gate,
    w_up,
    w_down,
    q_gain,
    k_gain,
):
    groups = lax.axis_size("seq")
    rows_dev, len_dev, width = tokens.shape
    count = rows_dev * len_dev
    per_group = QH // KVG
    places = (KVG + groups - 1) // groups * groups
    place_dev = places // groups
    length = len_dev * groups
    block = min(512, length)
    items = rows_dev * place_dev
    gain_one, qkv_w, out_w, gain_two, gate_w, up_w, down_w = (
        lax.all_gather(attn_gain, ("seq", "rep"), axis=0, tiled=True),
        lax.all_gather(w_qkv, ("seq", "rep"), axis=0, tiled=True),
        lax.all_gather(w_out, ("seq", "rep"), axis=0, tiled=True),
        lax.all_gather(ffn_gain, ("seq", "rep"), axis=0, tiled=True),
        lax.all_gather(w_gate, ("seq", "rep"), axis=0, tiled=True),
        lax.all_gather(w_up, ("seq", "rep"), axis=0, tiled=True),
        lax.all_gather(w_down, ("seq", "rep"), axis=0, tiled=True),
    )
    row_seg = lax.all_gather(segment_ids, "seq", axis=1, tiled=True)
    offset = lax.axis_index("seq") * len_dev
    earlier = jnp.sum((row_seg[:, None, :] < segment_ids[:, :, None]).astype(jnp.int32), axis=2)
    positions = (offset + jnp.arange(len_dev, dtype=jnp.int32)[None, :] - earlier).reshape(count)
    seg_items = jnp.repeat(row_seg, place_dev, axis=0)
    x_rows = tokens.reshape(count, width).astype(jnp.float32)
    gain_a = gain_one.astype(jnp.float32)
    gain_b = gain_two.astype(jnp.float32)
    q_scale = q_gain.astype(jnp.float32)
    k_scale = k_gain.astype(jnp.float32)
    normed = norm_rows(x_rows, gain_a).astype(jnp.bfloat16)
    qkv = jnp.dot(normed, qkv_w, preferred_element_type=jnp.float32)
    query, key, value = heads_prep(qkv, q_scale, k_scale, positions)
    packed = jnp.concatenate(
        [query.reshape(count, KVG, per_group * HD), key, value], axis=2
    ).astype(jnp.bfloat16)
    packed = jnp.pad(packed, ((0, 0), (0, places - KVG), (0, 0))).reshape(
        rows_dev, len_dev, places, -1
    )
    arrived = lax.all_to_all(packed, "seq", split_axis=2, concat_axis=1, tiled=True)
    arrived = arrived.transpose(0, 2, 1, 3).reshape(items, length, -1)
    q_heads = arrived[..., : per_group * HD].reshape(items, length, per_group, HD)
    k_heads = arrived[..., per_group * HD : (per_group + 1) * HD]
    v_heads = arrived[..., (per_group + 1) * HD :]
    outs, lse = attend_forward(q_heads, k_heads, v_heads, seg_items, block)
    attended = (
        outs.transpose(1, 0, 2, 3, 4)
        .reshape(rows_dev, place_dev, length, per_group * HD)
        .transpose(0, 2, 1, 3)
    )
    returned = lax.all_to_all(attended, "seq", split_axis=1, concat_axis=2, tiled=True)
    mixed = returned[:, :, :KVG].reshape(count, QW)
    hidden = x_rows + times_rows(mixed, out_w)
    normed_two = norm_rows(hidden, gain_b).astype(jnp.bfloat16)
    d_result = cotangent.reshape(count, width).astype(jnp.float32)
    gate = jnp.dot(normed_two, gate_w, preferred_element_type=jnp.float32)
    upward = jnp.dot(normed_two, up_w, preferred_element_type=jnp.float32)
    active = (jax.nn.silu(gate) * upward).astype(jnp.bfloat16)
    layer_result = hidden + times_rows(active, down_w)
    d_branch = d_result.astype(jnp.bfloat16)
    d_active = jnp.dot(d_branch, down_w, preferred_element_type=jnp.float32)
    grad_down = token_sum(d_branch, active)
    swiglu_out, swiglu_back = jax.vjp(
        lambda gate_in, up_in: jax.nn.silu(gate_in) * up_in, gate, upward
    )
    d_gate, d_up = swiglu_back(d_active)
    d_gate = d_gate.astype(jnp.bfloat16)
    d_up = d_up.astype(jnp.bfloat16)
    grad_gate = token_sum(normed_two, d_gate)
    grad_up = token_sum(normed_two, d_up)
    d_normed_two = times_rows(d_gate, gate_w) + times_rows(d_up, up_w)
    activations = layer_result.astype(jnp.bfloat16).reshape(rows_dev, len_dev, width)
    second_out, second_back = jax.vjp(norm_rows, hidden, gain_b)
    d_hidden, grad_gain_b = second_back(d_normed_two)
    d_hidden = d_hidden + d_result
    d_attn = d_hidden.astype(jnp.bfloat16)
    grad_out = token_sum(d_attn, mixed)
    d_mixed = jnp.dot(d_attn, out_w, preferred_element_type=jnp.float32).astype(jnp.bfloat16)
    d_pack = jnp.pad(
        d_mixed.reshape(count, KVG, per_group * HD), ((0, 0), (0, places - KVG), (0, 0))
    )
    d_pack = d_pack.reshape(rows_dev, len_dev, places, -1)
    d_arrived = lax.all_to_all(d_pack, "seq", split_axis=2, concat_axis=1, tiled=True)
    d_items = d_arrived.transpose(0, 2, 1, 3).reshape(items, length, per_group, HD)
    d_query, d_key, d_value = attend_backward(
        q_heads, k_heads, v_heads, seg_items, d_items, lse, block
    )
    d_query = d_query.transpose(1, 0, 2, 3, 4).reshape(items, length, per_group * HD)
    d_heads = jnp.concatenate([d_query, d_key, d_value], axis=2).astype(jnp.bfloat16)
    d_heads = d_heads.reshape(rows_dev, place_dev, length, -1).transpose(0, 2, 1, 3)
    d_back = lax.all_to_all(d_heads, "seq", split_axis=1, concat_axis=2, tiled=True)
    d_back = d_back[:, :, :KVG].reshape(count, KVG, -1).astype(jnp.float32)
    d_q_rows = d_back[..., : per_group * HD].reshape(count, QH, HD)
    d_k_rows = d_back[..., per_group * HD : (per_group + 1) * HD]
    d_v_rows = d_back[..., (per_group + 1) * HD :]
    prep_out, prep_back = jax.vjp(
        lambda qkv_in, qs_in, ks_in: heads_prep(qkv_in, qs_in, ks_in, positions),
        qkv,
        q_scale,
        k_scale,
    )
    d_qkv, grad_q_scale, grad_k_scale = prep_back((d_q_rows, d_k_rows, d_v_rows))
    d_qkv = d_qkv.astype(jnp.bfloat16)
    grad_qkv = token_sum(normed, d_qkv)
    d_normed = times_rows(d_qkv, qkv_w)
    first_out, first_back = jax.vjp(norm_rows, x_rows, gain_a)
    d_tokens, grad_gain_a = first_back(d_normed)
    d_tokens = d_tokens + d_hidden
    head_sums = lax.psum((grad_q_scale, grad_k_scale), ("seq", "rep"))
    parts = (
        lax.psum_scatter(grad_gain_a, ("seq", "rep"), scatter_dimension=0, tiled=True),
        lax.psum_scatter(grad_qkv, ("seq", "rep"), scatter_dimension=0, tiled=True),
        lax.psum_scatter(grad_out, ("seq", "rep"), scatter_dimension=0, tiled=True),
        lax.psum_scatter(grad_gain_b, ("seq", "rep"), scatter_dimension=0, tiled=True),
        lax.psum_scatter(grad_gate, ("seq", "rep"), scatter_dimension=0, tiled=True),
        lax.psum_scatter(grad_up, ("seq", "rep"), scatter_dimension=0, tiled=True),
        lax.psum_scatter(grad_down, ("seq", "rep"), scatter_dimension=0, tiled=True),
    )
    return (
        activations,
        d_tokens.reshape(rows_dev, len_dev, width),
        parts[0],
        parts[1],
        parts[2],
        parts[3],
        parts[4],
        parts[5],
        parts[6],
        head_sums[0],
        head_sums[1],
    )


def solution(mesh):
    in_specs = (
        P("rep", "seq", None),
        P("rep", "seq"),
        P("rep", "seq", None),
        P(("seq", "rep")),
        P(("seq", "rep"), None),
        P(("seq", "rep"), None),
        P(("seq", "rep")),
        P(("seq", "rep"), None),
        P(("seq", "rep"), None),
        P(("seq", "rep"), None),
        P(),
        P(),
    )
    out_specs = (
        P("rep", "seq", None),
        P("rep", "seq", None),
        P(("seq", "rep")),
        P(("seq", "rep"), None),
        P(("seq", "rep"), None),
        P(("seq", "rep")),
        P(("seq", "rep"), None),
        P(("seq", "rep"), None),
        P(("seq", "rep"), None),
        P(),
        P(),
    )
    return jax.shard_map(shards, mesh=mesh, in_specs=in_specs, out_specs=out_specs, check_vma=False)
```

profile of v0, /device:TPU:1, one launch (start us, length us, event | category | flops | bytes accessed | tf_op | source)
XLA Modules:
  0.0 2787.8 jit_solution(13718362793096273126)
XLA Ops:
  13.6 41.7 %all-reduce.14 = (bf16[2048]{0:T(1024)(128)(2,1)S(1)}, bf16[2048]{0:T(1024)(128)(2,1)S(1)}) all-reduce(bf16[2048]{0:T(1024)(128)(2,1)S(1)} %dynamic-update-slice, bf16[2048]{0:T(1024)(128)(2,1)S(1)} %dynamic-update-slice.1), channel_id=1, replica_groups=mesh['seq'=4,'rep'=8] {'seq','rep'}, use_global_device_ids=true, to_apply=%add.9 | all-reduce | flops 4096 | bytes 16384
  55.3 6.0 all_gather.26
  64.0 25.1 all-gather.6.cloned.1.call-done
  100.0 11.3 all-to-all-done
  123.0 7.5 all-to-all-done.1
  130.8 26.1 all-gather.8.cloned.1.call-done
  161.5 102.5 %all-gather.12.cloned.1.call-done = bf16[2048,3584]{1,0:T(8,128)(2,1)} async-done(((bf16[64,3584]{1,0:T(8,128)(2,1)}), bf16[2048,3584]{1,0:T(8,128)(2,1)}) %all-gather.12.cloned.1.call-update) | async-done | bytes 14680080 | tf_op jit(solution)/shard_map/all_gather | solution.py:174
  264.0 8.5 fusion.65
  272.5 97.8 %all-gather.10.cloned.1.call-done = bf16[2048,3584]{1,0:T(8,128)(2,1)} async-done(((bf16[64,3584]{1,0:T(8,128)(2,1)}), bf16[2048,3584]{1,0:T(8,128)(2,1)}) %all-gather.10.cloned.1.call-update) | async-done | bytes 14680080 | tf_op jit(solution)/shard_map/all_gather | solution.py:173
  370.3 8.5 fusion.64
  378.8 97.8 %all-gather.14.cloned.1.call-done = bf16[2048,3584]{1,0:T(8,128)(2,1)} async-done(((bf16[64,3584]{1,0:T(8,128)(2,1)}), bf16[2048,3584]{1,0:T(8,128)(2,1)}) %all-gather.14.cloned.1.call-update) | async-done | bytes 14680080 | tf_op jit(solution)/shard_map/all_gather | solution.py:175
  476.6 9.9 multiply_convert_fusion
  486.5 10.6 fusion.66
  497.1 10.3 multiply_reduce_fusion
  507.8 5.5 fusion.50
  525.5 8.1 all-to-all-done.2
  535.5 4.8 fusion.31
  541.2 5.5 fusion
  564.9 15.1 all_to_all.72
  588.5 7.8 fusion.53
  596.4 15.2 convolution_bitcast_fusion
  611.6 27.7 copy.112
  639.4 12.9 fusion.68
  652.7 12.9 fusion.67
  665.6 11.2 fusion.10
  676.8 6.1 fusion.36
  682.9 47.6 %all-reduce.13 = (f32[2048]{0:T(1024)S(1)}, f32[2048]{0:T(1024)S(1)}, f32[64]{0:T(128)}, f32[64]{0:T(128)}) all-reduce(f32[2048]{0:T(1024)S(1)} %get-tuple-element.125, f32[2048]{0:T(1024)S(1)} %get-tuple-element.123, f32[64]{0:T(128)S(1)} %copy-done.16, ...), channel_id=2, replica_groups=mesh['seq'=4,'rep'=8] {'seq','rep'}, use_global_device_ids=true, to_apply=%region_13.14.clone | all-reduce | flops 4224 | bytes 33792
  733.0 7.3 reduce-scatter.10.cloned.1.call-done
  740.3 175.2 %reduce-scatter.8.cloned.1.call-done = f32[64,1920]{1,0:T(8,128)} async-done(((f32[2048,1920]{1,0:T(8,128)}), f32[64,1920]{1,0:T(8,128)}) %reduce-scatter.8.cloned.1.call-update) | async-done | bytes 491536 | tf_op jit(solution)/shard_map/reduce_scatter | solution.py:268
  915.4 621.9 %reduce-scatter.16.cloned.1.call-done = f32[64,3584]{1,0:T(8,128)} async-done(((f32[2048,3584]{1,0:T(8,128)}), f32[64,3584]{1,0:T(8,128)}) %reduce-scatter.16.cloned.1.call-update) | async-done | bytes 917520
  1537.3 621.7 %reduce-scatter.14.cloned.1.call-done = f32[64,3584]{1,0:T(8,128)} async-done(((f32[2048,3584]{1,0:T(8,128)}), f32[64,3584]{1,0:T(8,128)}) %reduce-scatter.14.cloned.1.call-update) | async-done | bytes 917520 | tf_op jit(solution)/shard_map/reduce_scatter | solution.py:272
  2159.0 621.5 %reduce-scatter.12.cloned.1.call-done = f32[64,3584]{1,0:T(8,128)} async-done(((f32[2048,3584]{1,0:T(8,128)}), f32[64,3584]{1,0:T(8,128)}) %reduce-scatter.12.cloned.1.call-update) | async-done | bytes 917520 | tf_op jit(solution)/shard_map/reduce_scatter | solution.py:271
  (139 shorter events, 81.1 us)
Async XLA Ops:
  7.2 81.9 %all-gather.6.cloned.1.call-start = ((), (), s32[]{:S(2)}) async-start(), calls=%async_computation.9 | async-start | bytes 8110080 | tf_op jit(solution)/shard_map/all_gather | solution.py:170
  7.9 149.0 %all-gather.8.cloned.1.call-start = ((), (), s32[]{:S(2)}) async-start(), calls=%async_computation.10 | async-start | bytes 5406720 | tf_op jit(solution)/shard_map/all_gather | solution.py:171
  8.7 255.4 %all-gather.12.cloned.1.call-start = ((), (), s32[]{:S(2)}) async-start(), calls=%async_computation.12 | async-start | bytes 15138816 | tf_op jit(solution)/shard_map/all_gather | solution.py:174
  9.4 360.9 %all-gather.10.cloned.1.call-start = ((), (), s32[]{:S(2)}) async-start(), calls=%async_computation.11 | async-start | bytes 15138816 | tf_op jit(solution)/shard_map/all_gather | solution.py:173
  10.0 466.6 %all-gather.14.cloned.1.call-start = ((), (), s32[]{:S(2)}) async-start(), calls=%async_computation.13 | async-start | bytes 15138816 | tf_op jit(solution)/shard_map/all_gather | solution.py:175
  63.3 0.5 copy-start.17
  94.4 19.8 copy-start.3
  95.9 15.4 all-to-all-start
  112.6 2.9 copy-start.8
  112.7 1.6 copy-start.6
  114.3 3.3 copy-start
  115.5 41.4 %copy-start.2 = (bf16[1,128,2048]{2,1,0:T(8,128)(2,1)S(1)}, bf16[1,128,2048]{2,1,0:T(8,128)(2,1)}, u32[]{:S(2)}) copy-start(bf16[1,128,2048]{2,1,0:T(8,128)(2,1)} %param.12) | copy-start | bytes 1572868
  118.7 11.8 all-to-all-start.1
  122.5 617.8 %reduce-scatter.10.cloned.1.call-start = ((), (), s32[]{:S(2)}) async-start(), calls=%async_computation.15 | async-start | bytes 10813440 | tf_op jit(solution)/shard_map/reduce_scatter | solution.py:269
  130.8 30.5 %copy-start.11 = (bf16[1,128,5,256]{1,3,2,0:T(8,128)(2,1)}, bf16[1,128,5,256]{1,3,2,0:T(8,128)(2,1)S(1)}, u32[]{:S(2)}) copy-start(bf16[1,128,5,256]{1,3,2,0:T(8,128)(2,1)S(1)} %copy.92) | copy-start | bytes 983044
  486.5 20.9 copy-start.9
  486.5 20.9 copy-start.10
  497.1 10.4 copy-start.13
  497.1 10.7 copy-start.12
  521.2 12.4 all-to-all-start.2
  525.5 389.9 %reduce-scatter.8.cloned.1.call-start = ((), (), s32[]{:S(2)}) async-start(), calls=%async_computation.14 | async-start | bytes 16220160 | tf_op jit(solution)/shard_map/reduce_scatter | solution.py:268
  534.7 0.8 copy-start.7
  551.4 1.9 copy-start.1
  584.0 3.7 copy-start.14
  587.7 0.8 copy-start.4
  596.4 941.0 %reduce-scatter.16.cloned.1.call-start = ((), (), s32[]{:S(2)}) async-start(), calls=%async_computation.18 | async-start | bytes 30277632
  639.3 1519.7 %reduce-scatter.14.cloned.1.call-start = ((), (), s32[]{:S(2)}) async-start(), calls=%async_computation.17 | async-start | bytes 30277632 | tf_op jit(solution)/shard_map/reduce_scatter | solution.py:272
  652.4 2128.2 %reduce-scatter.12.cloned.1.call-start = ((), (), s32[]{:S(2)}) async-start(), calls=%async_computation.16 | async-start | bytes 30277632 | tf_op jit(solution)/shard_map/reduce_scatter | solution.py:271
  665.6 11.2 copy-start.5
  665.6 11.2 copy-start.15
  676.8 6.2 copy-start.16
  676.8 55.0 %copy-start.18 = (f32[128]{0:T(128)S(1)}, f32[128]{0:T(128)}, u32[]{:S(2)}) copy-start(f32[128]{0:T(128)} %copy-done.17) | copy-start | bytes 1540
Sparse Core Ops, SparseCore 0:
  10.9 78.0 all-gather.5
  91.9 65.0 all-gather.7
  159.8 104.2 all-gather.11
  266.8 103.5 all-gather.9
  373.0 103.5 all-gather.13
  513.5 226.7 reduce-scatter.9
  746.8 168.5 reduce-scatter.7
  918.3 618.9 reduce-scatter.15
  1540.2 618.7 reduce-scatter.13
  2161.8 618.7 reduce-scatter.11
where the time goes:
time: 2800 us; the launch traced here: 2790 us
  waiting for transfers between devices  2430 us (87%)
  matrix products  152 us (5%)
  blocking collectives  110 us (4%)
  local copies, waits for them, and re-layouts  50.1 us (2%)
    unnamed x11, waiting for transfers between devices  625 us
    reduce_scatter x1, waiting for transfers between devices, shards(): lax.psum_scatter(grad_up, ('seq', 'rep'), scatter_dimension=0, tiled=True)  622 us
    reduce_scatter x1, waiting for transfers between devices, shards(): lax.psum_scatter(grad_gate, ('seq', 'rep'), scatter_dimension=0, tiled=True)  622 us
    reduce_scatter x1, waiting for transfers between devices, shards(): lax.psum_scatter(grad_qkv, ('seq', 'rep'), scatter_dimension=0, tiled=True)  175 us
    all_gather x1, waiting for transfers between devices, shards(): lax.all_gather(w_up, ('seq', 'rep'), axis=0, tiled=True)  103 us
    all_gather x1, waiting for transfers between devices, shards(): lax.all_gather(w_gate, ('seq', 'rep'), axis=0, tiled=True)  97.8 us
    all_gather x1, waiting for transfers between devices, shards(): lax.all_gather(w_down, ('seq', 'rep'), axis=0, tiled=True)  97.8 us
    unnamed x2, blocking collectives  89.3 us
  transfers between devices with their start and end apart: 13, of which 13 were waited for; matrix products, arithmetic and copies ran while one was open for 6% of the time, Pallas kernels for 0%

commit v1 on v0

--- a/solution.py
+++ b/solution.py
@@ -1,6 +1,8 @@
 import jax
 import jax.numpy as jnp
 from jax import lax
+from jax.experimental import pallas as pl
+from jax.experimental.pallas import tpu as pltpu
 from jax.sharding import PartitionSpec as P
 
 QH = 20
@@ -287,6 +289,743 @@
     )
 
 
+MESH = pl.DeviceIdType.MESH
+BF = jnp.bfloat16
+F32 = jnp.float32
+EPS = norm_eps
+NEG = -1e30
+VMEM_BYTES = 60 * 2**20
+
+
+def place():
+    s = lax.axis_index("seq")
+    r = lax.axis_index("rep")
+    return lax.div(s, 2), lax.rem(s, 2), lax.div(r, 2), lax.rem(r, 2)
+
+
+def dev(x, c, z, y):
+    return {"seq": 2 * x + c, "rep": 2 * z + y}
+
+
+def flip(v, by):
+    return v if by == 0 else 1 - v
+
+
+def send(src, dst, send_sem, recv_sem, target):
+    copy = pltpu.make_async_remote_copy(
+        src_ref=src,
+        dst_ref=dst,
+        send_sem=send_sem,
+        recv_sem=recv_sem,
+        device_id=target,
+        device_id_type=MESH,
+    )
+    copy.start()
+    return copy
+
+
+def arrived(ref, sem):
+    pltpu.make_async_copy(ref, ref, sem).wait()
+
+
+def rows_of(ref, index, size):
+    return ref.at[pl.ds(pl.multiple_of(index * size, size), size)]
+
+
+def greet(targets):
+    barrier = pltpu.get_barrier_semaphore()
+    for target in targets:
+        pl.semaphore_signal(barrier, inc=1, device_id=target, device_id_type=MESH)
+    pl.semaphore_wait(barrier, len(targets))
+
+
+def plane_targets(x, c, z, y):
+    found = []
+    for dx in range(2):
+        for dy in range(2):
+            for dc in range(2):
+                if dx or dy or dc:
+                    found.append(dev(flip(x, dx), flip(c, dc), z, flip(y, dy)))
+    return found
+
+
+def column_targets(x, c, z, y):
+    found = []
+    for dz in range(1, DZ):
+        for dx in range(2):
+            for dy in range(2):
+                found.append(
+                    dev(flip(x, dx), c, lax.rem(z + dz, DZ), flip(y, dy))
+                )
+    return found
+
+
+def spread_start(src, full, send_sems, recv_sems):
+    x, c, z, y = place()
+    slot = 2 * x + c
+    spot = rows_of(full, slot, BLK)
+    for k, (dx, dy) in enumerate(((1, 1), (1, 0), (0, 1))):
+        send(
+            src, spot, send_sems.at[k], recv_sems.at[slot], dev(flip(x, dx), y, z, flip(y, dy))
+        )
+
+    @pl.when(c == y)
+    def _():
+        pltpu.make_async_copy(src, spot, recv_sems.at[slot]).start()
+
+    @pl.when(c != y)
+    def _():
+        send(src, spot, send_sems.at[3], recv_sems.at[slot], dev(x, y, z, y))
+
+
+def spread_wait(full, recv_sems):
+    for j in range(4):
+        arrived(rows_of(full, j, BLK), recv_sems.at[j])
+
+
+def spread_sent(src, send_sems):
+    x, c, z, y = place()
+    for k in range(3):
+        arrived(src, send_sems.at[k])
+
+    @pl.when(c != y)
+    def _():
+        arrived(src, send_sems.at[3])
+
+
+BLOCK_ORDER = ((1, 1), (1, 0), (0, 1), (0, 0))
+
+
+def block_at(order):
+    x, c, z, y = place()
+    dx, dc = BLOCK_ORDER[order]
+    return 2 * flip(x, dx) + flip(c, dc)
+
+
+def collect_start(order, partial, inbox, send_sems, recv_sems):
+    x, c, z, y = place()
+    dx, dc = BLOCK_ORDER[order]
+    src = rows_of(partial, block_at(order), BLK)
+    slot = 2 * x + y
+    spot = inbox.at[slot]
+    target = dev(flip(x, dx), flip(c, dc), z, c)
+    if dx or dc:
+        send(src, spot, send_sems.at[order], recv_sems.at[slot], target)
+        return
+
+    @pl.when(c == y)
+    def _():
+        pltpu.make_async_copy(src, spot, recv_sems.at[slot]).start()
+
+    @pl.when(c != y)
+    def _():
+        send(src, spot, send_sems.at[order], recv_sems.at[slot], target)
+
+
+def collect_wait(inbox, recv_sems):
+    for j in range(4):
+        arrived(inbox.at[j], recv_sems.at[j])
+
+
+def collect_sent(inbox, send_sems):
+    x, c, z, y = place()
+    for k in range(3):
+        arrived(inbox.at[0], send_sems.at[k])
+
+    @pl.when(c == y)
+    def _():
+        pass
+
+    @pl.when(c != y)
+    def _():
+        arrived(inbox.at[0], send_sems.at[3])
+
+
+def inbox_sum(inbox):
+    return (inbox[0].astype(F32) + inbox[1].astype(F32)) + (
+        inbox[2].astype(F32) + inbox[3].astype(F32)
+    )
+
+
+def mm(left, right):
+    return lax.dot_general(left, right, (((1,), (0,)), ((), ())), preferred_element_type=F32)
+
+
+def mm_nt(left, right):
+    return lax.dot_general(left, right, (((1,), (1,)), ((), ())), preferred_element_type=F32)
+
+
+def mm_tn(left, right):
+    return lax.dot_general(left, right, (((0,), (0,)), ((), ())), preferred_element_type=F32)
+
+
+def mask_of(seg_ref):
+    seg_col = seg_ref[:, 0:1].astype(F32)
+    seg_row = jnp.transpose(seg_ref[...].astype(F32))[0:1, :]
+    key_at = lax.broadcasted_iota(jnp.int32, (LEN4, LEN4), 0)
+    query_at = lax.broadcasted_iota(jnp.int32, (LEN4, LEN4), 1)
+    return seg_col, seg_row, (key_at <= query_at) & (seg_col == seg_row)
+
+
+def group_of(local_head):
+    x, c, z, y = place()
+    shard = 2 * x + y
+    return jnp.where(local_head + shard >= 4, 1, 0)
+
+
+def k1_body(
+    tok, cot, seg, wa, wg, wu, wd, gq, gk, fr,
+    w3_o, wa_o, dyf_o, hid_o, n2_o, qt_o, kt_o, k_o, vt_o, v_o, qkvt_o, lse_o, att_o, n1_o, cs_o, grow_o, segf_o,
+    xf, wav, attt, part, inbox,
+    tok_ss, tok_rs, cot_ss, cot_rs, seg_ss, seg_rs, out_ss, out_rs, w_ss, w_rs, c_ss, c_rs, loc,
+):
+    x, c, z, y = place()
+    me = (2 * x + c) * 2 * DZ + 2 * z + y
+    source = (2 * x + y) * DZ + z
+    greet(plane_targets(x, c, z, y) + column_targets(x, c, z, y))
+
+    def weight_piece(m, shard):
+        wide = pl.ds(pl.multiple_of(shard * FFS, 128), FFS)
+        if m == 0:
+            return wa.at[shard]
+        return (wg, wu, wd)[m - 1].at[:, wide]
+
+    def weight_view(m, first, count):
+        rows = pl.ds(pl.multiple_of(first, count), count)
+        if m == 0:
+            return wav.at[rows]
+        return w3_o.at[rows, pl.ds((m - 1) * FFS, FFS)]
+
+    def weights_start(m):
+        for dz in range(DZ):
+            for dx in range(2):
+                for dy in range(2):
+                    tx, ty, tz = flip(x, dx), flip(y, dy), lax.rem(z + dz, DZ)
+                    src = weight_piece(m, 2 * tx + ty)
+                    spot = weight_view(m, me * BR, BR)
+                    k = (dz * 2 + dx) * 2 + dy
+                    if k == 0:
+                        pltpu.make_async_copy(src, spot, w_rs.at[m, source]).start()
+                    else:
+                        send(src, spot, w_ss.at[m, k], w_rs.at[m, source], dev(tx, c, tz, ty))
+
+    def weights_sent(m):
+        for k in range(1, 4 * DZ):
+            arrived(weight_view(m, 0, BR), w_ss.at[m, k])
+
+    def weights_swap(m):
+        for k in range(4 * DZ):
+            arrived(weight_view(m, 0, BR), w_rs.at[m, k])
+        for tx in range(2):
+            half = weight_view(m, (2 * tx + c) * HALF, HALF)
+            send(half, half, c_ss.at[m, tx], c_rs.at[m, tx], dev(x, 1 - c, z, y))
+
+    def weights_wait(m):
+        for tx in range(2):
+            arrived(weight_view(m, 0, HALF), c_rs.at[m, tx])
+
+    def swap_sent(m):
+        for tx in range(2):
+            arrived(weight_view(m, 0, HALF), c_ss.at[m, tx])
+
+    spread_start(seg, segf_o, seg_ss, seg_rs)
+    spread_start(tok, xf, tok_ss, tok_rs)
+    weights_start(0)
+    spread_wait(segf_o, seg_rs)
+    seg_col, seg_row, allowed = mask_of(segf_o)
+    earlier = jnp.sum(jnp.where(seg_col < seg_row, 1.0, 0.0), axis=0, keepdims=True)
+    index = lax.broadcasted_iota(jnp.int32, (1, LEN4), 1).astype(F32)
+    angles = fr[...] * (index - earlier)
+    cos, sin = jnp.cos(angles), jnp.sin(angles)
+    cs_o[0:32, :] = cos
+    cs_o[32:64, :] = sin
+    spread_wait(xf, tok_rs)
+    weights_swap(0)
+    weights_wait(0)
+    for m in range(1, 4):
+        weights_start(m)
+    spread_start(cot, dyf_o, cot_ss, cot_rs)
+    keep = pltpu.make_async_copy(wav, wa_o, loc.at[0])
+    keep.start()
+    gains = jnp.transpose(wav[:, 512:640].astype(F32))[64:72, :]
+    grow_o[...] = gains
+    gain_a, gain_b = grow_o[0:1, :], grow_o[1:2, :]
+
+    @pl.loop(0, 4)
+    def _(j):
+        rows = pl.ds(pl.multiple_of(j * BLK, BLK), BLK)
+        v = xf[rows, :].astype(F32)
+        n1_o[rows, :] = (
+            v * lax.rsqrt(jnp.mean(v * v, axis=1, keepdims=True) + EPS) * gain_a
+        ).astype(BF)
+
+    @pl.loop(0, 5)
+    def _(j):
+        wide = pl.ds(pl.multiple_of(j * 128, 128), 128)
+        qkvt_o[wide, :] = jnp.transpose(mm(n1_o[...], wav[:, wide]))
+
+    def rotated(v, gain):
+        v = v * lax.rsqrt(jnp.mean(v * v, axis=0, keepdims=True) + EPS) * gain
+        first, second = v[0:32, :], v[32:64, :]
+        return first * cos - second * sin, second * cos + first * sin
+
+    for h in range(QS):
+        first, second = rotated(qkvt_o[h * 64 : h * 64 + 64, :], gq[...])
+        qt_o[h, 0:32, :] = first.astype(BF)
+        qt_o[h, 32:64, :] = second.astype(BF)
+    for g in range(2):
+        base = QS * 64 + g * 64
+        first, second = rotated(qkvt_o[base : base + 64, :], gk[...])
+        both = jnp.concatenate([first, second], axis=0)
+        kt_o[g] = both.astype(BF)
+        k_o[g] = jnp.transpose(both).astype(BF)
+        value = qkvt_o[base + 128 : base + 192, :]
+        vt_o[g] = value.astype(BF)
+        v_o[g] = jnp.transpose(value).astype(BF)
+    lse_o[...] = jnp.zeros_like(lse_o)
+    attt[QS * 64 :, :] = jnp.zeros((384 - QS * 64, LEN4), F32)
+    for h in range(QS):
+        g = group_of(h)
+        scores = jnp.where(allowed, mm(k_o[g], qt_o[h]) * SCALE, NEG)
+        top = jnp.max(scores, axis=0, keepdims=True)
+        weights = jnp.exp(scores - top)
+        total = jnp.sum(weights, axis=0, keepdims=True)
+        lse_o[h : h + 1, :] = top + jnp.log(total)
+        attt[h * 64 : h * 64 + 64, :] = mm(vt_o[g], (weights / total).astype(BF))
+    att_o[...] = jnp.transpose(attt[...]).astype(BF)
+    for order in range(4):
+        rows = pl.ds(pl.multiple_of(block_at(order) * BLK, BLK), BLK)
+        part[rows, :] = mm_nt(att_o[rows, :], wav[:, 640:1024]).astype(BF)
+        collect_start(order, part, inbox, out_ss, out_rs)
+    collect_wait(inbox, out_rs)
+    hidden = tok[...].astype(F32) + inbox_sum(inbox)
+    hid_o[...] = hidden
+    n2_o[...] = (
+        hidden * lax.rsqrt(jnp.mean(hidden * hidden, axis=1, keepdims=True) + EPS) * gain_b
+    ).astype(BF)
+    for m in range(1, 4):
+        weights_swap(m)
+    spread_wait(dyf_o, cot_rs)
+    spread_sent(seg, seg_ss)
+    spread_sent(tok, tok_ss)
+    spread_sent(cot, cot_ss)
+    collect_sent(inbox, out_ss)
+    for m in range(4):
+        weights_sent(m)
+        swap_sent(m)
+    for m in range(1, 4):
+        weights_wait(m)
+    keep.wait()
+
+
+def k2_body(
+    n2, dyf_h, w3_h, hid, cot, grow,
+    act_o, dhid_o, dab_o, g_o, gp_o,
+    n2f, dyf, w3, dact, active, dgu, part, inbox, inbox_y, gsend, grecv,
+    n_ss, n_rs, d_ss, d_rs, y_ss, y_rs, g_ss, g_rs, loc,
+):
+    x, c, z, y = place()
+    greet(plane_targets(x, c, z, y))
+    spread_start(n2, n2f, n_ss, n_rs)
+    loads = (
+        pltpu.make_async_copy(dyf_h, dyf, loc.at[0]),
+        pltpu.make_async_copy(w3_h.at[:, pl.ds(2 * FFS, FFS)], w3.at[:, pl.ds(2 * FFS, FFS)], loc.at[1]),
+        pltpu.make_async_copy(w3_h.at[:, pl.ds(0, 2 * FFS)], w3.at[:, pl.ds(0, 2 * FFS)], loc.at[2]),
+    )
+    for load in loads:
+        load.start()
+    loads[0].wait()
+    loads[1].wait()
+    tiles = FF_TILES
+    for lo, wide in tiles:
+        dact[:, lo : lo + wide] = mm(dyf[...], w3[:, 2 * FFS + lo : 2 * FFS + lo + wide])
+    loads[2].wait()
+    spread_wait(n2f, n_rs)
+    for lo, wide in tiles:
+        gate = mm(n2f[...], w3[:, lo : lo + wide])
+        upward = mm(n2f[...], w3[:, FFS + lo : FFS + lo + wide])
+        sig = 1.0 / (1.0 + jnp.exp(-gate))
+        silu = gate * sig
+        grad = dact[:, lo : lo + wide]
+        active[:, lo : lo + wide] = (silu * upward).astype(BF)
+        dgu[:, lo : lo + wide] = (grad * upward * (sig * (1.0 + gate * (1.0 - sig)))).astype(BF)
+        dgu[:, FFS + lo : FFS + lo + wide] = (grad * silu).astype(BF)
+    for order in range(4):
+        rows = pl.ds(pl.multiple_of(block_at(order) * BLK, BLK), BLK)
+
+        @pl.loop(0, 4)
+        def _(j):
+            wide = pl.ds(pl.multiple_of(j * 512, 512), 512)
+            part[0, rows, wide] = mm_nt(dgu[rows, :], w3[wide, 0 : 2 * FFS]).astype(BF)
+
+        collect_start(order, part.at[0], inbox, d_ss, d_rs)
+    for order in range(4):
+        rows = pl.ds(pl.multiple_of(block_at(order) * BLK, BLK), BLK)
+
+        @pl.loop(0, 4)
+        def _(j):
+            wide = pl.ds(pl.multiple_of(j * 512, 512), 512)
+            part[1, rows, wide] = mm_nt(active[rows, :], w3[wide, 2 * FFS : 3 * FFS]).astype(BF)
+
+        collect_start(order, part.at[1], inbox_y, y_ss, y_rs)
+
+    def grads(core, row):
+        first = (2 * lax.div(row, 2) + core) * HALF + lax.rem(row, 2) * 256
+        wide = pl.ds(pl.multiple_of(first, 256), 256)
+        return mm_tn(n2f[:, wide], dgu[...]), mm_tn(dyf[:, wide], active[...])
+
+    @pl.loop(0, 4)
+    def _(j):
+        gu, down = grads(1 - c, j)
+        rows = pl.ds(pl.multiple_of(j * 256, 256), 256)
+        gsend[rows, 0 : 2 * FFS] = gu.astype(BF)
+        gsend[rows, 2 * FFS : 3 * FFS] = down.astype(BF)
+
+    swap = send(gsend, grecv, g_ss, g_rs, dev(x, 1 - c, z, y))
+    collect_wait(inbox, d_rs)
+    dn = inbox_sum(inbox)
+    h = hid[...]
+    r = lax.rsqrt(jnp.mean(h * h, axis=1, keepdims=True) + EPS)
+    gp_o[...] = jnp.broadcast_to(jnp.sum(dn * h * r, axis=0, keepdims=True), gp_o.shape)
+    a = dn * grow[1:2, :]
+    dh = cot[...].astype(F32) + r * (a - h * (r * r * jnp.mean(a * h, axis=1, keepdims=True)))
+    dhid_o[...] = dh
+    dab_o[...] = dh.astype(BF)
+    swap.wait_recv()
+
+    @pl.loop(0, 4)
+    def _(j):
+        gu, down = grads(c, j)
+        rows = pl.ds(pl.multiple_of(j * 256, 256), 256)
+        g_o[rows, 0 : 2 * FFS] = (gu + grecv[rows, 0 : 2 * FFS].astype(F32)).astype(BF)
+        g_o[rows, 2 * FFS : 3 * FFS] = (down + grecv[rows, 2 * FFS : 3 * FFS].astype(F32)).astype(BF)
+
+    collect_wait(inbox_y, y_rs)
+    act_o[...] = (hid[...] + inbox_sum(inbox_y)).astype(BF)
+    swap.wait_send()
+    spread_sent(n2, n_ss)
+    collect_sent(inbox, d_ss)
+    collect_sent(inbox_y, y_ss)
+
+
+def k3_body(
+    g_h, dab, dhid, tok, wa_h, qt, kt, k, vt, v, qkvt, lse, att, n1, cs, grow, seg, gp2, gq, gk,
+    dtok_o, gr_o, ar_o, vr_o,
+    dabf, wav, dot_s, dqkvt, dqkv, part, inbox, asend, arecv, aown, vec, vecr, vecs, dkt, dvt,
+    b_ss, b_rs, t_ss, t_rs, w_ss, w_rs, a_ss, a_rs, v_ss, v_rs, c_ss, c_rs, loc,
+):
+    x, c, z, y = place()
+    source = (2 * x + y) * DZ + z
+    greet(plane_targets(x, c, z, y) + column_targets(x, c, z, y))
+
+    def owners_start(src, dst, send_sems, recv_sems):
+        for dz in range(DZ):
+            for dx in range(2):
+                for dy in range(2):
+                    tx, ty, tz = flip(x, dx), flip(y, dy), lax.rem(z + dz, DZ)
+                    piece = src((tx * DZ + tz) * 2 + ty)
+                    k_at = (dz * 2 + dx) * 2 + dy
+                    if k_at == 0:
+                        pltpu.make_async_copy(piece, dst.at[source], recv_sems.at[source]).start()
+                    else:
+                        send(
+                            piece, dst.at[source], send_sems.at[k_at], recv_sems.at[source], dev(tx, c, tz, ty)
+                        )
+
+    def owners_wait(dst, send_sems, recv_sems):
+        for i in range(1, 4 * DZ):
+            arrived(dst.at[0], send_sems.at[i])
+        for i in range(4 * DZ):
+            arrived(dst.at[i], recv_sems.at[i])
+
+    spread_start(dab, dabf, b_ss, b_rs)
+    load = pltpu.make_async_copy(wa_h, wav, loc.at[0])
+    load.start()
+    owners_start(lambda i: rows_of(g_h, i, BR), gr_o, w_ss, w_rs)
+    seg_col, seg_row, allowed = mask_of(seg)
+    cos, sin = cs[0:32, :], cs[32:64, :]
+    load.wait()
+    spread_wait(dabf, b_rs)
+    dot_s[...] = jnp.transpose(mm(dabf[...], wav[:, 640:1024]).astype(BF).astype(F32)).astype(BF)
+    dkt[...] = jnp.zeros_like(dkt)
+    dvt[...] = jnp.zeros_like(dvt)
+
+    def unrotated(first, second, raw, gain):
+        d_first = first * cos + second * sin
+        d_second = second * cos - first * sin
+        d = jnp.concatenate([d_first, d_second], axis=0)
+        r = lax.rsqrt(jnp.mean(raw * raw, axis=0, keepdims=True) + EPS)
+        d_gain = jnp.sum(d * raw * r, axis=1, keepdims=True)
+        a = d * gain
+        return r * (a - raw * (r * r * jnp.mean(a * raw, axis=0, keepdims=True))), d_gain
+
+    dq_gain = jnp.zeros((64, 1), F32)
+    for h in range(QS):
+        g = group_of(h)
+        scores = mm(k[g], qt[h]) * SCALE
+        p = jnp.where(allowed, jnp.exp(scores - lse[h : h + 1, :]), 0.0)
+        d_out = dot_s[h * 64 : h * 64 + 64, :]
+        dvt[g] += mm_nt(d_out, p.astype(BF))
+        dp = mm(v[g], d_out)
+        ds = (p * (dp - jnp.sum(p * dp, axis=0, keepdims=True))).astype(BF)
+        dkt[g] += mm_nt(qt[h], ds) * SCALE
+        dq = (mm(kt[g], ds) * SCALE).astype(BF).astype(F32)
+        d, more = unrotated(dq[0:32, :], dq[32:64, :], qkvt[h * 64 : h * 64 + 64, :], gq[...])
+        dq_gain = dq_gain + more
+        dqkvt[h * 64 : h * 64 + 64, :] = d
+    dk_gain = jnp.zeros((64, 1), F32)
+    for g in range(2):
+        base = QS * 64 + g * 64
+        dk = dkt[g].astype(BF).astype(F32)
+        d, more = unrotated(dk[0:32, :], dk[32:64, :], qkvt[base : base + 64, :], gk[...])
+        dk_gain = dk_gain + more
+        dqkvt[base : base + 64, :] = d
+        dqkvt[base + 128 : base + 192, :] = dvt[g]
+    dqkvt[576:640, :] = jnp.zeros((64, LEN4), F32)
+    dqkv[...] = jnp.transpose(dqkvt[...]).astype(BF)
+    for order in range(4):
+        rows = pl.ds(pl.multiple_of(block_at(order) * BLK, BLK), BLK)
+        part[rows, :] = mm_nt(dqkv[rows, :], wav[:, 0:640]).astype(BF)
+        collect_start(order, part, inbox, t_ss, t_rs)
+
+    def grads(core, row):
+        first = (2 * lax.div(row, 2) + core) * HALF + lax.rem(row, 2) * 256
+        wide = pl.ds(pl.multiple_of(first, 256), 256)
+        return mm_tn(n1[:, wide], dqkv[...]), mm_tn(dabf[:, wide], att[...])
+
+    @pl.loop(0, 4)
+    def _(j):
+        one, two = grads(1 - c, j)
+        rows = pl.ds(pl.multiple_of(j * 256, 256), 256)
+        asend[rows, 0:640] = one.astype(BF)
+        asend[rows, 640:1024] = two.astype(BF)
+
+    swap = send(asend, arecv, c_ss.at[0], c_rs.at[0], dev(x, 1 - c, z, y))
+    swap.wait_recv()
+
+    @pl.loop(0, 4)
+    def _(j):
+        one, two = grads(c, j)
+        rows = pl.ds(pl.multiple_of(j * 256, 256), 256)
+        aown[rows, 0:640] = (one + arecv[rows, 0:640].astype(F32)).astype(BF)
+        aown[rows, 640:1024] = (two + arecv[rows, 640:1024].astype(F32)).astype(BF)
+
+    owners_start(lambda i: rows_of(aown, i, BR), ar_o, a_ss, a_rs)
+    collect_wait(inbox, t_rs)
+    dn = inbox_sum(inbox)
+    xv = tok[...].astype(F32)
+    r = lax.rsqrt(jnp.mean(xv * xv, axis=1, keepdims=True) + EPS)
+    gain_a = jnp.sum(dn * xv * r, axis=0, keepdims=True)
+    b = dn * grow[0:1, :]
+    dtok_o[...] = dhid[...] + r * (b - xv * (r * r * jnp.mean(b * xv, axis=1, keepdims=True)))
+    qk = jnp.transpose(jnp.concatenate([jnp.broadcast_to(dq_gain, (64, 128)), jnp.broadcast_to(dk_gain, (64, 128))], axis=0))
+    gain_b = gp2[0:1, :]
+    for i in range(4 * DZ):
+        for half in range(2):
+            at = (((i // (2 * DZ)) * 2 + half) * 2 * DZ + i % (2 * DZ)) * BR
+            rows4 = jnp.concatenate(
+                [gain_a[:, at : at + BR], gain_b[:, at : at + BR], qk[0:1, 0:64], qk[0:1, 64:128]], axis=0
+            )
+            vec[half, i, 0:4, 0:64] = rows4
+
+    vecs[...] = vec[c]
+    swap_v = send(vec.at[1 - c], vecr, c_ss.at[1], c_rs.at[1], dev(x, 1 - c, z, y))
+    swap_v.wait_recv()
+    vecs[...] += vecr[...]
+    owners_start(lambda i: vecs.at[i], vr_o, v_ss, v_rs)
+    owners_wait(gr_o, w_ss, w_rs)
+    owners_wait(ar_o, a_ss, a_rs)
+    owners_wait(vr_o, v_ss, v_rs)
+    swap.wait_send()
+    swap_v.wait_send()
+    spread_sent(dab, b_ss)
+    collect_sent(inbox, t_ss)
+
+
+QS = 5
+DZ = 4
+BLK = 128
+LEN4 = 512
+FFS = 896
+BR = 64
+HALF = 512
+SCALE = HD ** (-0.5)
+FF_TILES = ((0, 256), (256, 256), (512, 256), (768, 128))
+ANY = pl.ANY
+VM = pltpu.VMEM
+
+
+def kernel_call(body, args, kinds, outs, scratch, cid):
+    params = pltpu.CompilerParams(
+        collective_id=cid, has_side_effects=True, vmem_limit_bytes=VMEM_BYTES
+    )
+    return pl.pallas_call(
+        body,
+        out_shape=[jax.ShapeDtypeStruct(shape, kind) for shape, kind, _ in outs],
+        in_specs=[pl.BlockSpec(memory_space=ANY if kind == "h" else VM) for kind in kinds],
+        out_specs=[pl.BlockSpec(memory_space=ANY if where == "h" else VM) for _, _, where in outs],
+        scratch_shapes=scratch,
+        compiler_params=params,
+    )(*args)
+
+
+def plane_plan(
+    tokens, segment_ids, cotangent, attn_gain, w_qkv, w_out, ffn_gain, w_gate, w_up, w_down, q_gain, k_gain
+):
+    width = tokens.shape[-1]
+    tok = tokens.reshape(BLK, width)
+    cot = cotangent.reshape(BLK, width)
+    seg = jnp.broadcast_to(segment_ids.reshape(BLK, 1).astype(BF), (BLK, 128))
+    gains = jnp.concatenate(
+        [attn_gain[:, None], ffn_gain[:, None], jnp.zeros((BR, 62), BF)], axis=1
+    )
+    tail = jnp.zeros((BR, 64), BF)
+    wa = jnp.stack(
+        [
+            jnp.concatenate(
+                [
+                    w_qkv[:, 320 * t : 320 * t + 320],
+                    w_qkv[:, QW + 64 * t : QW + 64 * t + 128],
+                    w_qkv[:, QW + KW + 64 * t : QW + KW + 64 * t + 128],
+                    gains,
+                    w_out[:, 320 * t : 320 * t + 320],
+                    tail,
+                ],
+                axis=1,
+            )
+            for t in range(4)
+        ]
+    )
+    gq = q_gain.astype(F32).reshape(64, 1)
+    gk = k_gain.astype(F32).reshape(64, 1)
+    fr = (rope_base ** (-jnp.arange(32, dtype=jnp.float32) * 2.0 / 64)).reshape(32, 1)
+    sem = pltpu.SemaphoreType.DMA
+    vm = pltpu.VMEM
+    (
+        w3, wah, dyf, hid, n2, qt, kt, k, vt, v, qkvt, lse, att, n1, cs, grow, segf
+    ) = kernel_call(
+        k1_body,
+        (tok, cot, seg, wa, w_gate, w_up, w_down, gq, gk, fr),
+        "vhhhhhhvvv",
+        [
+            ((2048, 3 * FFS), BF, "h"),
+            ((2048, 1024), BF, "h"),
+            ((LEN4, width), BF, "h"),
+            ((BLK, width), F32, "v"),
+            ((BLK, width), BF, "v"),
+            ((QS, 64, LEN4), BF, "v"),
+            ((2, 64, LEN4), BF, "v"),
+            ((2, LEN4, 64), BF, "v"),
+            ((2, 64, LEN4), BF, "v"),
+            ((2, LEN4, 64), BF, "v"),
+            ((640, LEN4), F32, "v"),
+            ((8, LEN4), F32, "v"),
+            ((LEN4, 384), BF, "v"),
+            ((LEN4, width), BF, "v"),
+            ((64, LEN4), F32, "v"),
+            ((8, width), F32, "v"),
+            ((LEN4, 128), BF, "v"),
+        ],
+        [
+            vm((LEN4, width), BF),
+            vm((2048, 1024), BF),
+            vm((384, LEN4), F32),
+            vm((LEN4, width), BF),
+            vm((4, BLK, width), BF),
+            sem((4,)), sem((4,)), sem((4,)), sem((4,)), sem((4,)), sem((4,)), sem((4,)), sem((4,)),
+            sem((4, 4 * DZ)), sem((4, 4 * DZ)), sem((4, 2)), sem((4, 2)), sem((1,)),
+        ],
+        0,
+    )
+    act, dhid, dab, g, gp = kernel_call(
+        k2_body,
+        (n2, dyf, w3, hid, cot, grow),
+        "hhhvvv",
+        [
+            ((BLK, width), BF, "v"),
+            ((BLK, width), F32, "v"),
+            ((BLK, width), BF, "v"),
+            ((1024, 3 * FFS), BF, "v"),
+            ((8, width), F32, "v"),
+        ],
+        [
+            vm((LEN4, width), BF),
+            vm((LEN4, width), BF),
+            vm((2048, 3 * FFS), BF),
+            vm((LEN4, FFS), F32),
+            vm((LEN4, FFS), BF),
+            vm((LEN4, 2 * FFS), BF),
+            vm((2, LEN4, width), BF),
+            vm((4, BLK, width), BF),
+            vm((4, BLK, width), BF),
+            vm((1024, 3 * FFS), BF),
+            vm((1024, 3 * FFS), BF),
+            sem((4,)), sem((4,)), sem((4,)), sem((4,)), sem((4,)), sem((4,)), sem, sem, sem((3,)),
+        ],
+        1,
+    )
+    dtok, gr, ar, vr = kernel_call(
+        k3_body,
+        (g, dab, dhid, tok, wah, qt, kt, k, vt, v, qkvt, lse, att, n1, cs, grow, segf, gp, gq, gk),
+        "hhvvhvvvvvvvvvvvvvvv",
+        [
+            ((BLK, width), F32, "v"),
+            ((4 * DZ, BR, 3 * FFS), BF, "h"),
+            ((4 * DZ, BR, 1024), BF, "h"),
+            ((4 * DZ, 8, 128), F32, "h"),
+        ],
+        [
+            vm((LEN4, width), BF),
+            vm((2048, 1024), BF),
+            vm((384, LEN4), BF),
+            vm((640, LEN4), F32),
+            vm((LEN4, 640), BF),
+            vm((LEN4, width), BF),
+            vm((4, BLK, width), BF),
+            vm((1024, 1024), BF),
+            vm((1024, 1024), BF),
+            vm((1024, 1024), BF),
+            vm((2, 4 * DZ, 8, 128), F32),
+            vm((4 * DZ, 8, 128), F32),
+            vm((4 * DZ, 8, 128), F32),
+            vm((2, 64, LEN4), F32),
+            vm((2, 64, LEN4), F32),
+            sem((4,)), sem((4,)), sem((4,)), sem((4,)),
+            sem((4 * DZ,)), sem((4 * DZ,)), sem((4 * DZ,)), sem((4 * DZ,)), sem((4 * DZ,)), sem((4 * DZ,)),
+            sem((2,)), sem((2,)), sem((1,)),
+        ],
+        2,
+    )
+    ffn = jnp.sum(gr.reshape(4, DZ, BR, 3, FFS).astype(F32), axis=1)
+    ffn = ffn.transpose(2, 1, 0, 3).reshape(3, BR, 4 * FFS)
+    att_w = jnp.sum(ar.reshape(4, DZ, BR, 1024).astype(F32), axis=1)
+    none = jnp.zeros((BR, 64), F32)
+
+    def groups(at):
+        first = jnp.concatenate([att_w[t][:, at : at + 64] for t in range(4)] + [none], axis=1)
+        second = jnp.concatenate([none] + [att_w[t][:, at + 64 : at + 128] for t in range(4)], axis=1)
+        return first + second
+
+    g_qkv = jnp.concatenate(
+        [att_w[t][:, 0:320] for t in range(4)] + [groups(320), groups(448)], axis=1
+    )
+    g_out = jnp.concatenate([att_w[t][:, 640:960] for t in range(4)], axis=1)
+    vec = jnp.sum(vr, axis=0)
+    return (
+        act.reshape(tokens.shape),
+        dtok.reshape(tokens.shape),
+        vec[0, :64],
+        g_qkv,
+        g_out,
+        vec[1, :64],
+        ffn[0],
+        ffn[1],
+        ffn[2],
+        vec[2, :64],
+        vec[3, :64],
+    )
+
+
 def solution(mesh):
     in_specs = (
         P("rep", "seq", None),
@@ -315,4 +1054,6 @@
         P(),
         P(),
     )
-    return jax.shard_map(shards, mesh=mesh, in_specs=in_specs, out_specs=out_specs, check_vma=False)
+    planes = mesh.shape["seq"] == 4 and mesh.shape["rep"] == 8
+    body = plane_plan if planes else shards
+    return jax.shard_map(body, mesh=mesh, in_specs=in_specs, out_specs=out_specs, check_vma=False)

time: 2800 us -> 518 us (0.18)
  waiting for transfers between devices: 2430 us -> 0 us
  Pallas kernels: 0 us -> 461 us
  matrix products: 152 us -> 0 us
  blocking collectives: 110 us -> 0 us
    reduce_scatter x4 -> x0, waiting for transfers between devices: 1430 us -> none  [the longest x1 622 us: shards(): lax.psum_scatter(grad_up, ('seq', 'rep'), scatter_dimension=0, tiled=True)]
    unnamed x11 -> x0, waiting for transfers between devices: 625 us -> none
    pallas_call x0 -> x3, Pallas kernels: none -> 461 us  [kernel_call(): pl.pallas_call(body, out_shape=[jax.ShapeDtypeStruct(shape, kind) for sha...]
    all_gather x5 -> x0, waiting for transfers between devices: 349 us -> none  [the longest x1 103 us: shards(): lax.all_gather(w_up, ('seq', 'rep'), axis=0, tiled=True)]
    dot_general x21 -> x0, matrix products: 152 us -> none  [the longest x5 54.3 us: token_sum(): lax.dot_general(left, right, (((0,), (0,)), ((), ())), preferred_element_...]
    unnamed x2 -> x0, blocking collectives: 89.3 us -> none
    unnamed x45 -> x13, local copies, waits for them, and re-layouts: 35.1 us -> 4.75 us
  transfers between devices with their start and end apart: 13 -> 0, of which waited for: 13 -> 0; matrix products, arithmetic and copies ran while one was open for 6% -> 0% of each run, Pallas kernels for 0% -> 0%
where the time goes in v1:
time: 518 us; the launch traced here: 516 us
  Pallas kernels  461 us (89%)
  local copies, waits for them, and re-layouts  38.7 us (7%)
  other arithmetic  15 us (3%)
    pallas_call x3, Pallas kernels, kernel_call(): pl.pallas_call(body, out_shape=[jax.ShapeDtypeStruct(shape, kind) for sha...  461 us
    convert_element_type x1, local copies, waits for them, and re-layouts, plane_plan(): ffn = jnp.sum(gr.reshape(4, DZ, BR, 3, FFS).astype(F32), axis=1)  15.7 us
    reduce_sum x1, other arithmetic, plane_plan(): ffn = jnp.sum(gr.reshape(4, DZ, BR, 3, FFS).astype(F32), axis=1)  11.1 us

profile of v1, /device:TPU:1, one launch (start us, length us, event | category | flops | bytes accessed | tf_op | source)
XLA Modules:
  0.0 515.7 jit_solution(8737401864455516894)
XLA Ops:
  0.6 1.1 fusion.10
  1.8 1.1 fusion.9
  2.8 0.8 copy.59
  3.6 0.8 copy.60
  4.4 0.1 concatenate.35
  4.5 0.1 concatenate.36
  4.9 0.9 pad_maximum_fusion.wa
  5.7 0.7 bitcast_convert_fusion.1
  6.4 0.7 copy.67.gq
  7.1 0.7 bitcast_convert_fusion
  7.8 0.7 copy.68.gk
  8.5 0.7 convert_bitcast_fusion
  9.1 0.7 broadcast_in_dim.20.seg
  9.8 0.6 multiply_power_fusion.fr
  10.5 193.2 %shard_map.203 = (bf16[2048,2688]{1,0:T(8,128)(2,1)}, bf16[2048,1024]{1,0:T(8,128)(2,1)}, bf16[512,2048]{1,0:T(8,128)(2,1)}, f32[128,2048]{1,0:T(8,128)}, bf16[1...) custom-call(bf16[128,2048]{1,0:T(8,128)(2,1)} %bitcast.51, ...), custom_call_target="tpu_custom_call" | custom-call | tf_op jit(solution)/shard_map/pallas_call | solution.py:862
  203.6 86.9 %shard_map.204 = (bf16[128,2048]{1,0:T(8,128)(2,1)}, f32[128,2048]{1,0:T(8,128)}, bf16[128,2048]{1,0:T(8,128)(2,1)}, bf16[1024,2688]{1,0:T(8,128)(2,1)}, f32[8,2048]{1,0:T(8,128)}) custom-call(bf16[128,2048]{1,0:T(8,128)(2,1)} %get-tuple-element.37.n2, bf16[512,2048]{1,0:T(8,128)(2,1)} %get-tuple-element.38.dyf_h, ...), custom_call_target="tpu_custom_call" | custom-call | tf_op jit(solution)/shard_map/pallas_call | solution.py:862
  290.5 181.0 %shard_map.205 = (f32[128,2048]{1,0:T(8,128)}, bf16[16,64,2688]{2,1,0:T(8,128)(2,1)}, bf16[16,64,1024]{2,1,0:T(8,128)(2,1)}, f32[16,8,128]{2,1,0:T(8,128)}) custom-call(bf16[1024,2688]{1,0:T(8,128)(2,1)} %get-tuple-element.43.g_h, bf16[128,2048]{1,0:T(8,128)(2,1)} %get-tuple-element.44.dab, f32[128,2048]{1,0:T(8,128)} %get-tuple-element.45.dhid, ...), custom_call_target="tpu_custom_call" | custom-call | tf_op jit(solution)/shard_map/pallas_call | solution.py:862
  471.6 15.7 %reshape.93 = f32[4,4,64,3,896]{4,3,2,1,0:T(4,128)} reshape(bf16[16,64,2688]{2,1,0:T(8,128)(2,1)} %get-tuple-element.62) | data formatting | bytes 16515072 | tf_op jit(solution)/shard_map/convert_element_type | solution.py:999
  487.3 11.1 %reduce_sum.29 = f32[4,64,3,896]{3,2,1,0:T(4,128)} reduce(f32[4,4,64,3,896]{4,3,2,1,0:T(4,128)} %reshape.93, f32[]{:T(128)} %constant.2.clone.1), dimensions={1}, to_apply=%region_2.0 | reduce | flops 2064384 | bytes 13762564 | tf_op jit(solution)/shard_map/reduce_sum | solution.py:999
  498.4 7.0 %fusion = (f32[1,64,4,896]{3,0,1,2:T(1,128)S(1)}, f32[1,64,4,896]{3,0,1,2:T(1,128)S(1)}, f32[1,64,4,896]{3,0,1,2:T(1,128)S(1)}) fusion(f32[3,64,4,896]{3,0,1,2:T(4,128)} %bitcast.47), kind=kLoop, calls=%fused_computation.14 | loop fusion | bytes 5505024 | tf_op jit(solution)/shard_map/slice | solution.py:1023
  505.4 0.6 copy.71
  506.0 1.0 copy.74
  507.0 0.6 copy.72
  507.6 1.0 copy.75
  508.6 0.6 copy.73
  509.2 1.0 copy.76
  510.2 0.4 convert_reduce_fusion
  510.8 0.8 concatenate.44
  512.4 0.9 concatenate.43
  513.4 0.5 slice_bitcast_fusion.4
  513.9 0.8 copy.79
  514.7 1.0 copy.80
  (29 shorter events, 1.2 us)
Async XLA Ops:
  507.0 3.2 copy-start
  510.6 2.8 copy-start.3
  510.6 3.3 copy-start.2
  510.7 4.0 copy-start.1

commit v2 on v0

--- a/solution.py
+++ b/solution.py
@@ -1,6 +1,8 @@
 import jax
 import jax.numpy as jnp
 from jax import lax
+from jax.experimental import pallas as pl
+from jax.experimental.pallas import tpu as pltpu
 from jax.sharding import PartitionSpec as P
 
 QH = 20
@@ -287,6 +289,870 @@
     )
 
 
+MESH = pl.DeviceIdType.MESH
+BF = jnp.bfloat16
+F32 = jnp.float32
+NEG = -1e30
+VMEM_BYTES = 61 * 2**20
+QS = 5
+DZ = 4
+BLK = 128
+LEN4 = 512
+FFS = 896
+BR = 64
+HALF = 512
+AW = 1024
+QKV_W = 640
+SCALE = HD ** (-0.5)
+FF_TILES = ((0, 256), (256, 256), (512, 256), (768, 128))
+QKV_M, OUT_M, DOWN_M, GATE_M, UP_M = range(5)
+FF_AT = {DOWN_M: 2 * FFS, GATE_M: 0, UP_M: FFS}
+
+
+def place():
+    s = lax.axis_index("seq")
+    r = lax.axis_index("rep")
+    return lax.div(s, 2), lax.rem(s, 2), lax.div(r, 2), lax.rem(r, 2)
+
+
+def dev(x, c, z, y):
+    return {"seq": 2 * x + c, "rep": 2 * z + y}
+
+
+def flip(v, by):
+    return v if by == 0 else 1 - v
+
+
+def near(z):
+    return z + 1 - 2 * lax.rem(z, 2)
+
+
+def inner(z):
+    return (z == 1) | (z == 2)
+
+
+def send(src, dst, send_sem, recv_sem, target):
+    pltpu.make_async_remote_copy(
+        src_ref=src,
+        dst_ref=dst,
+        send_sem=send_sem,
+        recv_sem=recv_sem,
+        device_id=target,
+        device_id_type=MESH,
+    ).start()
+
+
+def arrived(ref, sem):
+    pltpu.make_async_copy(ref, ref, sem).wait()
+
+
+def many(first, count):
+    return pl.ds(pl.multiple_of(first, count), count)
+
+
+def rows_of(ref, index, size):
+    return ref.at[many(index * size, size)]
+
+
+def greet(x, c, z, y):
+    found = []
+    for dz in range(DZ):
+        for dx in range(2):
+            for dy in range(2):
+                for dc in range(2):
+                    if (dx or dy or dc) if dz == 0 else dc == 0:
+                        found.append(
+                            dev(flip(x, dx), flip(c, dc), lax.rem(z + dz, DZ), flip(y, dy))
+                        )
+    barrier = pltpu.get_barrier_semaphore()
+    for target in found:
+        pl.semaphore_signal(barrier, inc=1, device_id=target, device_id_type=MESH)
+    pl.semaphore_wait(barrier, len(found))
+
+
+def spread_start(src, spot, ss, rs):
+    x, c, z, y = place()
+    slot = 2 * x + c
+    for k, (dx, dy) in enumerate(((1, 1), (1, 0), (0, 1))):
+        send(src, spot, ss.at[k], rs.at[slot], dev(flip(x, dx), y, z, flip(y, dy)))
+
+    @pl.when(c == y)
+    def _():
+        pltpu.make_async_copy(src, spot, rs.at[slot]).start()
+
+    @pl.when(c != y)
+    def _():
+        send(src, spot, ss.at[3], rs.at[slot], dev(x, y, z, y))
+
+
+def spread_wait(block, rs):
+    for j in range(4):
+        arrived(block, rs.at[j])
+
+
+def spread_sent(src, ss):
+    x, c, z, y = place()
+    for k in range(3):
+        arrived(src, ss.at[k])
+
+    @pl.when(c != y)
+    def _():
+        arrived(src, ss.at[3])
+
+
+BLOCK_ORDER = ((1, 1), (1, 0), (0, 1), (0, 0))
+
+
+def block_at(order):
+    x, c, z, y = place()
+    dx, dc = BLOCK_ORDER[order]
+    return 2 * flip(x, dx) + flip(c, dc)
+
+
+def collect_start(order, partial, inbox, ss, rs):
+    x, c, z, y = place()
+    dx, dc = BLOCK_ORDER[order]
+    src = rows_of(partial, block_at(order), BLK)
+    slot = 2 * x + y
+    spot = inbox.at[slot]
+    target = dev(flip(x, dx), flip(c, dc), z, c)
+    if dx or dc:
+        send(src, spot, ss.at[order], rs.at[slot], target)
+        return
+
+    @pl.when(c == y)
+    def _():
+        pltpu.make_async_copy(src, spot, rs.at[slot]).start()
+
+    @pl.when(c != y)
+    def _():
+        send(src, spot, ss.at[order], rs.at[slot], target)
+
+
+def collect_wait(inbox, rs):
+    for j in range(4):
+        arrived(inbox.at[j], rs.at[j])
+
+
+def collect_sent(inbox, ss):
+    x, c, z, y = place()
+    for k in range(3):
+        arrived(inbox.at[0], ss.at[k])
+
+    @pl.when(c != y)
+    def _():
+        arrived(inbox.at[0], ss.at[3])
+
+
+def inbox_sum(inbox):
+    return (inbox[0].astype(F32) + inbox[1].astype(F32)) + (
+        inbox[2].astype(F32) + inbox[3].astype(F32)
+    )
+
+
+def mm(left, right):
+    return lax.dot_general(left, right, (((1,), (0,)), ((), ())), preferred_element_type=F32)
+
+
+def mm_nt(left, right):
+    return lax.dot_general(left, right, (((1,), (1,)), ((), ())), preferred_element_type=F32)
+
+
+def mm_tn(left, right):
+    return lax.dot_general(left, right, (((0,), (0,)), ((), ())), preferred_element_type=F32)
+
+
+def group_of(local_head):
+    x, c, z, y = place()
+    return jnp.where(local_head + 2 * x + y >= 4, 1, 0)
+
+
+def layer_body(
+    tok, cot, small, wq, wo, wg, wu, wd,
+    act_o, dtok_o, gate_o, up_o, down_o, ga_o, vec_o, gr,
+    wap, smallf, xf, n1, wav, w3, dyf, n2f, part, inbox, dact, active, dgu,
+    qkvt, dqkvt, dqkv, qt, kt, kk, vt, vv, lse, att, cs, grow, hid, blk, dot_s, dkt, dvt,
+    help_f, help_a, arecv, ar, vec, vecr, vr, gp2,
+    sp_ss, sp_rs, co_ss, co_rs, w_ss, w_rs, f_ss, c_ss, c_rs, g_ss, g_rs, h_ss, h_rs, o_ss, o_rs, v_ss, v_rs, loc,
+    ready,
+):
+    x, c, z, y = place()
+    shard = 2 * x + y
+    me = (2 * x + c) * 2 * DZ + 2 * z + y
+    mid = inner(z)
+    sibling = dev(x, 1 - c, z, y)
+    pair, across = near(z), DZ - 1 - z
+    SMALL, TOK, COT, N2, DAB = range(5)
+    OUT, DN, YY, DT = range(4)
+
+    def own_piece(m, to_shard):
+        if m == QKV_M:
+            return wap.at[to_shard, :, pl.ds(0, QKV_W)]
+        if m == OUT_M:
+            return wap.at[to_shard, :, pl.ds(QKV_W, AW - QKV_W)]
+        return {DOWN_M: wd, GATE_M: wg, UP_M: wu}[m].at[
+            :, pl.ds(pl.multiple_of(to_shard * FFS, 128), FFS)
+        ]
+
+    def held(m, first, count):
+        rows = many(first, count)
+        if m == QKV_M:
+            return wav.at[rows, pl.ds(0, QKV_W)]
+        if m == OUT_M:
+            return wav.at[rows, pl.ds(QKV_W, AW - QKV_W)]
+        return w3.at[rows, pl.ds(FF_AT[m], FFS)]
+
+    def weights_start(m):
+        def to_plane(tz, base):
+            for dx in range(2):
+                for dy in range(2):
+                    tx, ty = flip(x, dx), flip(y, dy)
+                    send(
+                        own_piece(m, 2 * tx + ty),
+                        held(m, me * BR, BR),
+                        w_ss.at[m, base + 2 * dx + dy],
+                        w_rs.at[m, z * 4 + shard],
+                        dev(tx, c, tz, ty),
+                    )
+
+        to_plane(pair, 4)
+
+        @pl.when(mid)
+        def _():
+            to_plane(across, 8)
+
+        for dx in range(2):
+            for dy in range(2):
+                src = own_piece(m, 2 * flip(x, dx) + flip(y, dy))
+                spot = held(m, me * BR, BR)
+                sem = w_rs.at[m, z * 4 + shard]
+                if dx or dy:
+                    send(src, spot, w_ss.at[m, 2 * dx + dy], sem, dev(flip(x, dx), c, z, flip(y, dy)))
+                else:
+                    pltpu.make_async_copy(src, spot, sem).start()
+
+    def pass_on(m, from_plane, to_plane, base):
+        for tx in range(2):
+            for ty in range(2):
+                k = 2 * tx + ty
+                sem = w_rs.at[m, from_plane * 4 + k]
+                piece = held(m, ((2 * tx + c) * 2 * DZ + 2 * from_plane + ty) * BR, BR)
+                arrived(piece, sem)
+                send(piece, piece, f_ss.at[m, base + k], sem, dev(x, c, to_plane, y))
+
+    def weights_pass_near(m):
+        @pl.when(mid)
+        def _():
+            pass_on(m, pair, across, 0)
+            pass_on(m, across, pair, 4)
+
+    def weights_pass_far(m):
+        @pl.when(mid)
+        def _():
+            pass_on(m, DZ - 1 - pair, pair, 8)
+
+    def weights_swap(m):
+        @pl.when(jnp.logical_not(mid))
+        def _():
+            for i in range(4 * DZ):
+                arrived(held(m, 0, BR), w_rs.at[m, i])
+
+        @pl.when(mid)
+        def _():
+            for k in range(4):
+                arrived(held(m, 0, BR), w_rs.at[m, z * 4 + k])
+
+        for tx in range(2):
+            half = held(m, (2 * tx + c) * HALF, HALF)
+            send(half, half, c_ss.at[m, tx], c_rs.at[m, tx], sibling)
+
+    def weights_wait(m):
+        for tx in range(2):
+            arrived(held(m, 0, HALF), c_rs.at[m, tx])
+
+    def weights_sent(m):
+        for k in range(1, 8):
+            arrived(held(m, 0, BR), w_ss.at[m, k])
+
+        @pl.when(mid)
+        def _():
+            for k in range(8, 12):
+                arrived(held(m, 0, BR), w_ss.at[m, k])
+            for k in range(12):
+                arrived(held(m, 0, BR), f_ss.at[m, k])
+
+        for tx in range(2):
+            arrived(held(m, 0, HALF), c_ss.at[m, tx])
+
+    def slot_of(to_plane):
+        return shard * 3 + z - jnp.where(to_plane >= 2, 1, 0)
+
+    def grads_to_plane(kind, piece, inbox_at, tz, base):
+        spot = inbox_at(slot_of(tz))
+        for dx in range(2):
+            for dy in range(2):
+                tx, ty = flip(x, dx), flip(y, dy)
+                send(
+                    piece(tz, tx, ty),
+                    spot,
+                    o_ss.at[kind, base + 2 * dx + dy],
+                    o_rs.at[kind, slot_of(tz)],
+                    dev(tx, c, tz, ty),
+                )
+
+    def grads_start(kind, piece, inbox_at, pair_rows, help_ref):
+        @pl.when(jnp.logical_not(mid))
+        def _():
+            for i, tz in enumerate((DZ - 1 - pair, DZ - 1 - z)):
+                for tx in range(2):
+                    send(
+                        pair_rows(tx, tz),
+                        help_ref.at[i, pl.ds(tx * 2 * BR, 2 * BR)],
+                        h_ss.at[kind, 2 * i + tx],
+                        h_rs.at[kind, 2 * i + tx],
+                        dev(x, c, pair, y),
+                    )
+
+        grads_to_plane(kind, piece, inbox_at, pair, 4)
+        spot = inbox_at(slot_of(z))
+        sem = o_rs.at[kind, slot_of(z)]
+        for dx in range(2):
+            for dy in range(2):
+                tx, ty = flip(x, dx), flip(y, dy)
+                if dx or dy:
+                    send(piece(z, tx, ty), spot, o_ss.at[kind, 2 * dx + dy], sem, dev(tx, c, z, ty))
+                else:
+                    pltpu.make_async_copy(piece(z, x, y), spot, sem).start()
+
+    def grads_join(kind, piece, inbox_at, pair_rows, help_ref):
+        @pl.when(mid)
+        def _():
+            for i, tz in enumerate((across, DZ - 1 - pair)):
+                for tx in range(2):
+                    rows = pair_rows(tx, tz)
+                    arrived(rows, h_rs.at[kind, 2 * i + tx])
+                    rows[...] = (
+                        rows[...].astype(F32)
+                        + help_ref[i, tx * 2 * BR : (tx + 1) * 2 * BR, :].astype(F32)
+                    ).astype(BF)
+                grads_to_plane(kind, piece, inbox_at, tz, 8 + 4 * i)
+
+    def grads_wait(kind, inbox_at, pair_rows):
+        for k in range(12):
+            arrived(inbox_at(0), o_rs.at[kind, k])
+        for k in range(1, 8):
+            arrived(inbox_at(0), o_ss.at[kind, k])
+
+        @pl.when(mid)
+        def _():
+            for k in range(8, 16):
+                arrived(inbox_at(0), o_ss.at[kind, k])
+
+        @pl.when(jnp.logical_not(mid))
+        def _():
+            for k in range(4):
+                arrived(pair_rows(0, 0), h_ss.at[kind, k])
+
+    def grad_refs(ref, first_row, lo, width, inbox, helper):
+        lanes = pl.ds(lo, width)
+
+        def piece(tz, tx, ty):
+            return ref.at[many(first_row + ((tx * DZ + tz) * 2 + ty) * BR, BR), lanes]
+
+        def inbox_at(slot):
+            return inbox.at[many(slot * BR, BR), lanes]
+
+        def pair_rows(tx, tz):
+            return ref.at[many(first_row + (tx * DZ + tz) * 2 * BR, 2 * BR), lanes]
+
+        return piece, inbox_at, pair_rows, helper
+
+    ffn_refs = [
+        grad_refs(w3, 1024, j * FFS, FFS, gr, help_f.at[j]) for j in range(3)
+    ]
+    out_refs = grad_refs(arecv, 0, QKV_W, AW - QKV_W, ar, help_a.at[:, :, pl.ds(QKV_W, AW - QKV_W)])
+    qkv_refs = grad_refs(arecv, 0, 0, QKV_W, ar, help_a.at[:, :, pl.ds(0, QKV_W)])
+    kind_refs = ffn_refs + [out_refs, qkv_refs]
+
+    def join(kind):
+        grads_join(kind, *kind_refs[kind])
+
+    def start(kind):
+        grads_start(kind, *kind_refs[kind])
+
+    greet(x, c, z, y)
+    spot = smallf.at[:, many((2 * x + c) * BLK, BLK)]
+    spread_start(small, spot, sp_ss.at[SMALL], sp_rs.at[SMALL])
+    spread_start(tok, rows_of(xf, 2 * x + c, BLK), sp_ss.at[TOK], sp_rs.at[TOK])
+    turned = jnp.transpose(small[...])
+    lane = lax.broadcasted_iota(jnp.int32, (BR, 64), 1)
+    gains = jnp.where(lane == 0, turned[0:64, 0:1], jnp.where(lane == 1, turned[0:64, 1:2], 0.0))
+    gq, gk, fr = turned[0:64, 2:3], turned[0:64, 3:4], turned[0:32, 5:6]
+    for t in range(4):
+        wap[t, :, 0:320] = wq[:, 320 * t : 320 * t + 320]
+        wap[t, :, 320:448] = wq[:, QW + 64 * t : QW + 64 * t + 128]
+        wap[t, :, 448:576] = wq[:, QW + KW + 64 * t : QW + KW + 64 * t + 128]
+        wap[t, :, 576:640] = gains.astype(BF)
+        wap[t, :, 640:960] = wo[:, 320 * t : 320 * t + 320]
+        wap[t, :, 960:1024] = jnp.zeros((BR, 64), BF)
+    weights_start(QKV_M)
+    weights_start(OUT_M)
+    spread_wait(spot, sp_rs.at[SMALL])
+    seg_row = smallf[4:5, :]
+    seg_col = jnp.transpose(smallf[...])[:, 4:5]
+    key_at = lax.broadcasted_iota(jnp.int32, (LEN4, LEN4), 0)
+    query_at = lax.broadcasted_iota(jnp.int32, (LEN4, LEN4), 1)
+    allowed = (key_at <= query_at) & (seg_col == seg_row)
+    earlier = jnp.sum(jnp.where(seg_col < seg_row, 1.0, 0.0), axis=0, keepdims=True)
+    index = lax.broadcasted_iota(jnp.int32, (1, LEN4), 1).astype(F32)
+    angles = fr * (index - earlier)
+    cs[0:32, :] = jnp.cos(angles)
+    cs[32:64, :] = jnp.sin(angles)
+    spread_wait(rows_of(xf, 0, BLK), sp_rs.at[TOK])
+    weights_pass_near(QKV_M)
+    weights_pass_far(QKV_M)
+    weights_pass_near(OUT_M)
+    weights_pass_far(OUT_M)
+    for m in (DOWN_M, GATE_M, UP_M):
+        weights_start(m)
+    spread_start(cot, rows_of(dyf, 2 * x + c, BLK), sp_ss.at[COT], sp_rs.at[COT])
+    weights_swap(QKV_M)
+    weights_swap(OUT_M)
+    weights_wait(QKV_M)
+    grow[...] = jnp.transpose(wav[:, 512:640].astype(F32))[64:72, :]
+
+    @pl.loop(0, 4)
+    def _(j):
+        rows = many(j * BLK, BLK)
+        v = xf[rows, :].astype(F32)
+        n1[rows, :] = (
+            v * lax.rsqrt(jnp.mean(v * v, axis=1, keepdims=True) + norm_eps) * grow[0:1, :]
+        ).astype(BF)
+
+    @pl.loop(0, 5)
+    def _(j):
+        wide = many(j * 128, 128)
+        qkvt[wide, :] = jnp.transpose(mm(n1[...], wav[:, wide]))
+
+    def rotated(v, gain):
+        cos, sin = cs[0:32, :], cs[32:64, :]
+        v = v * lax.rsqrt(jnp.mean(v * v, axis=0, keepdims=True) + norm_eps) * gain
+        first, second = v[0:32, :], v[32:64, :]
+        return first * cos - second * sin, second * cos + first * sin
+
+    for h in range(QS):
+        first, second = rotated(qkvt[h * 64 : h * 64 + 64, :], gq)
+        qt[h, 0:32, :] = first.astype(BF)
+        qt[h, 32:64, :] = second.astype(BF)
+    for g in range(2):
+        base = QS * 64 + g * 64
+        first, second = rotated(qkvt[base : base + 64, :], gk)
+        both = jnp.concatenate([first, second], axis=0)
+        kt[g] = both.astype(BF)
+        kk[g] = jnp.transpose(both).astype(BF)
+        value = qkvt[base + 128 : base + 192, :]
+        vt[g] = value.astype(BF)
+        vv[g] = jnp.transpose(value).astype(BF)
+    dqkvt[QS * 64 : 384, :] = jnp.zeros((384 - QS * 64, LEN4), F32)
+    for h in range(QS):
+        g = group_of(h)
+        scores = jnp.where(allowed, mm(kk[g], qt[h]) * SCALE, NEG)
+        top = jnp.max(scores, axis=0, keepdims=True)
+        weights = jnp.exp(scores - top)
+        total = jnp.sum(weights, axis=0, keepdims=True)
+        lse[h : h + 1, :] = top + jnp.log(total)
+        dqkvt[h * 64 : h * 64 + 64, :] = mm(vt[g], (weights / total).astype(BF))
+    att[...] = jnp.transpose(dqkvt[0:384, :]).astype(BF)
+    weights_wait(OUT_M)
+    for order in range(4):
+        rows = many(block_at(order) * BLK, BLK)
+        part[0, rows, :] = mm_nt(att[rows, :], wav[:, QKV_W:AW]).astype(BF)
+        collect_start(order, part.at[0], inbox.at[0], co_ss.at[OUT], co_rs.at[OUT])
+    for m in (DOWN_M, GATE_M, UP_M):
+        weights_pass_near(m)
+    collect_wait(inbox.at[0], co_rs.at[OUT])
+    hidden = tok[...].astype(F32) + inbox_sum(inbox.at[0])
+    hid[...] = hidden
+    blk[0] = (
+        hidden
+        * lax.rsqrt(jnp.mean(hidden * hidden, axis=1, keepdims=True) + norm_eps)
+        * grow[1:2, :]
+    ).astype(BF)
+    spread_start(blk.at[0], rows_of(n2f, 2 * x + c, BLK), sp_ss.at[N2], sp_rs.at[N2])
+    for m in (DOWN_M, GATE_M, UP_M):
+        weights_pass_far(m)
+    weights_swap(DOWN_M)
+    spread_wait(rows_of(dyf, 0, BLK), sp_rs.at[COT])
+    weights_wait(DOWN_M)
+    for lo, wide in FF_TILES:
+        dact[:, lo : lo + wide] = mm(dyf[...], w3[:, 2 * FFS + lo : 2 * FFS + lo + wide])
+    weights_swap(GATE_M)
+    weights_swap(UP_M)
+    spread_wait(rows_of(n2f, 0, BLK), sp_rs.at[N2])
+    weights_wait(GATE_M)
+    weights_wait(UP_M)
+    for lo, wide in FF_TILES:
+        gate = mm(n2f[...], w3[:, lo : lo + wide])
+        upward = mm(n2f[...], w3[:, FFS + lo : FFS + lo + wide])
+        sig = 1.0 / (1.0 + jnp.exp(-gate))
+        silu = gate * sig
+        grad = dact[:, lo : lo + wide]
+        active[:, lo : lo + wide] = (silu * upward).astype(BF)
+        dgu[:, lo : lo + wide] = (grad * upward * (sig * (1.0 + gate * (1.0 - sig)))).astype(BF)
+        dgu[:, FFS + lo : FFS + lo + wide] = (grad * silu).astype(BF)
+    for order in range(4):
+        rows = many(block_at(order) * BLK, BLK)
+
+        @pl.loop(0, 4)
+        def _(j):
+            wide = many(j * 512, 512)
+            part[1, rows, wide] = mm_nt(dgu[rows, :], w3[wide, 0 : 2 * FFS]).astype(BF)
+
+        collect_start(order, part.at[1], inbox.at[1], co_ss.at[DN], co_rs.at[DN])
+    collect_sent(inbox.at[0], co_ss.at[OUT])
+    for order in range(4):
+        rows = many(block_at(order) * BLK, BLK)
+
+        @pl.loop(0, 4)
+        def _(j):
+            wide = many(j * 512, 512)
+            part[0, rows, wide] = mm_nt(active[rows, :], w3[wide, 2 * FFS : 3 * FFS]).astype(BF)
+
+        collect_start(order, part.at[0], inbox.at[0], co_ss.at[YY], co_rs.at[YY])
+    for m in range(5):
+        weights_sent(m)
+    pl.semaphore_signal(ready, inc=1, device_id=sibling, device_id_type=MESH)
+
+    def ffn_grads(core, row, j):
+        first = (2 * lax.div(row, 2) + core) * HALF + lax.rem(row, 2) * 256
+        wide = many(first, 256)
+        if j < 2:
+            return mm_tn(n2f[:, wide], dgu[:, j * FFS : (j + 1) * FFS])
+        return mm_tn(dyf[:, wide], active[...])
+
+    for j in range(3):
+        lanes = pl.ds(j * FFS, FFS)
+
+        @pl.loop(0, 4)
+        def _(row):
+            w3[many(row * 256, 256), lanes] = ffn_grads(1 - c, row, j).astype(BF)
+
+        if j == 0:
+            pl.semaphore_wait(ready, 1)
+        send(
+            w3.at[pl.ds(0, 1024), lanes], w3.at[pl.ds(1024, 1024), lanes], g_ss.at[j], g_rs.at[j], sibling
+        )
+    collect_wait(inbox.at[1], co_rs.at[DN])
+    dn = inbox_sum(inbox.at[1])
+    h = hid[...]
+    r = lax.rsqrt(jnp.mean(h * h, axis=1, keepdims=True) + norm_eps)
+    gp2[...] = jnp.broadcast_to(jnp.sum(dn * h * r, axis=0, keepdims=True), gp2.shape)
+    a = dn * grow[1:2, :]
+    dh = cot[...].astype(F32) + r * (a - h * (r * r * jnp.mean(a * h, axis=1, keepdims=True)))
+    dtok_o[...] = dh
+    blk[1] = dh.astype(BF)
+    spread_start(blk.at[1], rows_of(xf, 2 * x + c, BLK), sp_ss.at[DAB], sp_rs.at[DAB])
+    for j in range(3):
+        lanes = pl.ds(j * FFS, FFS)
+        arrived(w3.at[pl.ds(1024, 1024), lanes], g_rs.at[j])
+
+        @pl.loop(0, 4)
+        def _(row):
+            rows = many(1024 + row * 256, 256)
+            w3[rows, lanes] = (ffn_grads(c, row, j) + w3[rows, lanes].astype(F32)).astype(BF)
+
+        start(j)
+    collect_wait(inbox.at[0], co_rs.at[YY])
+    act_o[...] = (hid[...] + inbox_sum(inbox.at[0])).astype(BF)
+    spread_wait(rows_of(xf, 0, BLK), sp_rs.at[DAB])
+    dot_s[...] = jnp.transpose(mm(xf[...], wav[:, QKV_W:AW]).astype(BF).astype(F32)).astype(BF)
+    dkt[...] = jnp.zeros_like(dkt)
+    dvt[...] = jnp.zeros_like(dvt)
+
+    def unrotated(first, second, raw, gain):
+        cos, sin = cs[0:32, :], cs[32:64, :]
+        d_first = first * cos + second * sin
+        d_second = second * cos - first * sin
+        d = jnp.concatenate([d_first, d_second], axis=0)
+        r = lax.rsqrt(jnp.mean(raw * raw, axis=0, keepdims=True) + norm_eps)
+        d_gain = jnp.sum(d * raw * r, axis=1, keepdims=True)
+        a = d * gain
+        return r * (a - raw * (r * r * jnp.mean(a * raw, axis=0, keepdims=True))), d_gain
+
+    dq_gain = jnp.zeros((64, 1), F32)
+    for h in range(QS):
+        g = group_of(h)
+        scores = mm(kk[g], qt[h]) * SCALE
+        p = jnp.where(allowed, jnp.exp(scores - lse[h : h + 1, :]), 0.0)
+        d_out = dot_s[h * 64 : h * 64 + 64, :]
+        dvt[g] += mm_nt(d_out, p.astype(BF))
+        dp = mm(vv[g], d_out)
+        ds = (p * (dp - jnp.sum(p * dp, axis=0, keepdims=True))).astype(BF)
+        dkt[g] += mm_nt(qt[h], ds) * SCALE
+        dq = (mm(kt[g], ds) * SCALE).astype(BF).astype(F32)
+        d, more = unrotated(dq[0:32, :], dq[32:64, :], qkvt[h * 64 : h * 64 + 64, :], gq)
+        dq_gain = dq_gain + more
+        dqkvt[h * 64 : h * 64 + 64, :] = d
+        if h in JOIN_AFTER:
+            join(JOIN_AFTER[h])
+    dk_gain = jnp.zeros((64, 1), F32)
+    for g in range(2):
+        base = QS * 64 + g * 64
+        dk = dkt[g].astype(BF).astype(F32)
+        d, more = unrotated(dk[0:32, :], dk[32:64, :], qkvt[base : base + 64, :], gk)
+        dk_gain = dk_gain + more
+        dqkvt[base : base + 64, :] = d
+        dqkvt[base + 128 : base + 192, :] = dvt[g]
+    dqkvt[576:640, :] = jnp.zeros((64, LEN4), F32)
+    dqkv[...] = jnp.transpose(dqkvt[...]).astype(BF)
+    collect_sent(inbox.at[1], co_ss.at[DN])
+    for order in range(4):
+        rows = many(block_at(order) * BLK, BLK)
+        part[1, rows, :] = mm_nt(dqkv[rows, :], wav[:, 0:QKV_W]).astype(BF)
+        collect_start(order, part.at[1], inbox.at[1], co_ss.at[DT], co_rs.at[DT])
+
+    def att_grads(core, row, kind):
+        first = (2 * lax.div(row, 2) + core) * HALF + lax.rem(row, 2) * 256
+        wide = many(first, 256)
+        if kind == 4:
+            return mm_tn(n1[:, wide], dqkv[...])
+        return mm_tn(xf[:, wide], att[...])
+
+    att_lanes = {k: pl.ds(ATT_LO[k], ATT_WIDE[k]) for k in (3, 4)}
+    for kind in (3, 4):
+
+        @pl.loop(0, 4)
+        def _(row):
+            side = lax.div(row, 2) * AW + ATT_LO[kind]
+            dyf[many(lax.rem(row, 2) * 256, 256), pl.ds(pl.multiple_of(side, 128), ATT_WIDE[kind])] = (
+                att_grads(1 - c, row, kind).astype(BF)
+            )
+
+        for side in range(2):
+            send(
+                dyf.at[:, pl.ds(side * AW + ATT_LO[kind], ATT_WIDE[kind])],
+                arecv.at[pl.ds(side * HALF, HALF), att_lanes[kind]],
+                g_ss.at[2 * kind - 3 + side],
+                g_rs.at[2 * kind - 3 + side],
+                sibling,
+            )
+    for kind in (3, 4):
+        for side in range(2):
+            arrived(arecv.at[pl.ds(0, HALF), att_lanes[kind]], g_rs.at[2 * kind - 3 + side])
+
+        @pl.loop(0, 4)
+        def _(row):
+            rows = many(row * 256, 256)
+            arecv[rows, att_lanes[kind]] = (
+                att_grads(c, row, kind) + arecv[rows, att_lanes[kind]].astype(F32)
+            ).astype(BF)
+
+        start(kind)
+    collect_wait(inbox.at[1], co_rs.at[DT])
+    dn = inbox_sum(inbox.at[1])
+    xv = tok[...].astype(F32)
+    r = lax.rsqrt(jnp.mean(xv * xv, axis=1, keepdims=True) + norm_eps)
+    gain_a = jnp.sum(dn * xv * r, axis=0, keepdims=True)
+    b = dn * grow[0:1, :]
+    dtok_o[...] += r * (b - xv * (r * r * jnp.mean(b * xv, axis=1, keepdims=True)))
+    qk = jnp.transpose(
+        jnp.concatenate(
+            [jnp.broadcast_to(dq_gain, (64, 128)), jnp.broadcast_to(dk_gain, (64, 128))], axis=0
+        )
+    )
+    gain_b = gp2[0:1, :]
+    vec[...] = jnp.zeros_like(vec)
+    for i in range(4 * DZ):
+        for half in range(2):
+            at = (((i // (2 * DZ)) * 2 + half) * 2 * DZ + i % (2 * DZ)) * BR
+            vec[half, i, 0:4, 0:64] = jnp.concatenate(
+                [gain_a[:, at : at + BR], gain_b[:, at : at + BR], qk[0:1, 0:64], qk[0:1, 64:128]], axis=0
+            )
+    send(vec.at[1 - c], vecr, g_ss.at[7], g_rs.at[7], sibling)
+    arrived(vecr, g_rs.at[7])
+    vecr[...] += vec[c]
+    source = shard * DZ + z
+    for dz in range(DZ):
+        for dx in range(2):
+            for dy in range(2):
+                tx, ty, tz = flip(x, dx), flip(y, dy), lax.rem(z + dz, DZ)
+                src = vecr.at[(tx * DZ + tz) * 2 + ty]
+                k = (dz * 2 + dx) * 2 + dy
+                if k == 0:
+                    pltpu.make_async_copy(src, vr.at[source], v_rs.at[source]).start()
+                else:
+                    send(src, vr.at[source], v_ss.at[k], v_rs.at[source], dev(tx, c, tz, ty))
+    join(3)
+    join(4)
+    for j in range(3):
+        grads_wait(j, *kind_refs[j][1:3])
+    for j in range(3):
+        arrived(w3.at[pl.ds(0, 1024), pl.ds(j * FFS, FFS)], g_ss.at[j])
+    load = pltpu.make_async_copy(gr, w3.at[pl.ds(0, 12 * BR)], loc.at[0])
+    load.start()
+    load.wait()
+
+    def three(ref, t, lo, width):
+        lanes = pl.ds(lo, width)
+        at = t * 3 * BR
+        return (
+            ref[at : at + BR, lanes].astype(F32) + ref[at + BR : at + 2 * BR, lanes].astype(F32)
+        ) + ref[at + 2 * BR : at + 3 * BR, lanes].astype(F32)
+
+    leave = []
+    for j, out in enumerate((gate_o, up_o, down_o)):
+        for t in range(4):
+            rows = pl.ds((j % 2) * 4 * BR + t * BR, BR)
+            if j == 2:
+                leave[t].wait()
+            dact[rows, :] = three(w3, t, j * FFS, FFS)
+            leave.append(
+                pltpu.make_async_copy(
+                    dact.at[rows], out.at[:, pl.ds(t * FFS, FFS)], loc.at[1 + 4 * j + t]
+                )
+            )
+            leave[-1].start()
+    for j in (3, 4):
+        grads_wait(j, *kind_refs[j][1:3])
+    for t in range(4):
+        ga_o[t] = three(ar, t, 0, AW)
+    for i in range(4 * DZ):
+        arrived(vr.at[0], v_rs.at[i])
+    for i in range(1, 4 * DZ):
+        arrived(vr.at[0], v_ss.at[i])
+    for copy in leave[4:]:
+        copy.wait()
+    vec_o[...] = jnp.sum(vr[...], axis=0)
+    for j in (3, 4):
+        for side in range(2):
+            arrived(arecv.at[pl.ds(0, HALF), att_lanes[j]], g_ss.at[2 * j - 3 + side])
+    arrived(vecr, g_ss.at[7])
+    spread_sent(small, sp_ss.at[SMALL])
+    spread_sent(tok, sp_ss.at[TOK])
+    spread_sent(cot, sp_ss.at[COT])
+    spread_sent(blk.at[0], sp_ss.at[N2])
+    spread_sent(blk.at[1], sp_ss.at[DAB])
+    collect_sent(inbox.at[0], co_ss.at[YY])
+    collect_sent(inbox.at[1], co_ss.at[DT])
+
+
+JOIN_AFTER = {1: 0, 3: 1, 4: 2}
+ATT_LO = {3: QKV_W, 4: 0}
+ATT_WIDE = {3: AW - QKV_W, 4: QKV_W}
+
+
+def plane_plan(
+    tokens, segment_ids, cotangent, attn_gain, w_qkv, w_out, ffn_gain, w_gate, w_up, w_down, q_gain, k_gain
+):
+    width = tokens.shape[-1]
+    freqs = rope_base ** (-jnp.arange(32, dtype=jnp.float32) * 2.0 / HD)
+
+    def lanes(v):
+        v = v.astype(F32).reshape(1, -1)
+        return jnp.pad(v, ((0, 0), (0, BLK - v.shape[1])))
+
+    small = jnp.concatenate(
+        [lanes(v) for v in (attn_gain, ffn_gain, q_gain, k_gain, segment_ids, freqs)]
+        + [jnp.zeros((2, BLK), F32)],
+        axis=0,
+    )
+    dma = pltpu.SemaphoreType.DMA
+    vm = pltpu.VMEM
+    far, close = pl.BlockSpec(memory_space=pl.ANY), pl.BlockSpec(memory_space=pltpu.VMEM)
+    act, dtok, gate, up, down, ga, vec, _ = pl.pallas_call(
+        layer_body,
+        out_shape=[
+            jax.ShapeDtypeStruct((BLK, width), BF),
+            jax.ShapeDtypeStruct((BLK, width), F32),
+            jax.ShapeDtypeStruct((BR, 4 * FFS), F32),
+            jax.ShapeDtypeStruct((BR, 4 * FFS), F32),
+            jax.ShapeDtypeStruct((BR, 4 * FFS), F32),
+            jax.ShapeDtypeStruct((4, BR, AW), F32),
+            jax.ShapeDtypeStruct((8, BLK), F32),
+            jax.ShapeDtypeStruct((12 * BR, 3 * FFS), BF),
+        ],
+        in_specs=[close] * 5 + [far] * 3,
+        out_specs=[close] * 2 + [far] * 3 + [close] * 2 + [far],
+        scratch_shapes=[
+            vm((4, BR, AW), BF),
+            vm((8, LEN4), F32),
+            vm((LEN4, width), BF),
+            vm((LEN4, width), BF),
+            vm((2048, AW), BF),
+            vm((2048, 3 * FFS), BF),
+            vm((LEN4, width), BF),
+            vm((LEN4, width), BF),
+            vm((2, LEN4, width), BF),
+            vm((2, 4, BLK, width), BF),
+            vm((LEN4, FFS), F32),
+            vm((LEN4, FFS), BF),
+            vm((LEN4, 2 * FFS), BF),
+            vm((QKV_W, LEN4), F32),
+            vm((QKV_W, LEN4), F32),
+            vm((LEN4, QKV_W), BF),
+            vm((QS, 64, LEN4), BF),
+            vm((2, 64, LEN4), BF),
+            vm((2, LEN4, 64), BF),
+            vm((2, 64, LEN4), BF),
+            vm((2, LEN4, 64), BF),
+            vm((8, LEN4), F32),
+            vm((LEN4, 384), BF),
+            vm((64, LEN4), F32),
+            vm((8, width), F32),
+            vm((BLK, width), F32),
+            vm((2, BLK, width), BF),
+            vm((384, LEN4), BF),
+            vm((2, 64, LEN4), F32),
+            vm((2, 64, LEN4), F32),
+            vm((3, 2, 4 * BR, FFS), BF),
+            vm((2, 4 * BR, AW), BF),
+            vm((1024, AW), BF),
+            vm((12 * BR, AW), BF),
+            vm((2, 4 * DZ, 8, BLK), F32),
+            vm((4 * DZ, 8, BLK), F32),
+            vm((4 * DZ, 8, BLK), F32),
+            vm((8, width), F32),
+            dma((5, 4)), dma((5, 4)),
+            dma((4, 4)), dma((4, 4)),
+            dma((5, 12)), dma((5, 16)), dma((5, 12)),
+            dma((5, 2)), dma((5, 2)),
+            dma((8,)), dma((8,)),
+            dma((5, 4)), dma((5, 4)),
+            dma((5, 16)), dma((5, 12)),
+            dma((16,)), dma((16,)),
+            dma((13,)),
+            pltpu.SemaphoreType.REGULAR,
+        ],
+        compiler_params=pltpu.CompilerParams(
+            collective_id=0, has_side_effects=True, vmem_limit_bytes=VMEM_BYTES
+        ),
+    )(
+        tokens.reshape(BLK, width), cotangent.reshape(BLK, width), small, w_qkv, w_out, w_gate, w_up, w_down
+    )
+    none = jnp.zeros((BR, 64), F32)
+
+    def groups(at):
+        first = jnp.concatenate([ga[t][:, at : at + 64] for t in range(4)] + [none], axis=1)
+        second = jnp.concatenate([none] + [ga[t][:, at + 64 : at + 128] for t in range(4)], axis=1)
+        return first + second
+
+    g_qkv = jnp.concatenate([ga[t][:, 0:320] for t in range(4)] + [groups(320), groups(448)], axis=1)
+    g_out = jnp.concatenate([ga[t][:, 640:960] for t in range(4)], axis=1)
+    return (
+        act.reshape(tokens.shape),
+        dtok.reshape(tokens.shape),
+        vec[0, :64],
+        g_qkv,
+        g_out,
+        vec[1, :64],
+        gate,
+        up,
+        down,
+        vec[2, :64],
+        vec[3, :64],
+    )
+
+
 def solution(mesh):
     in_specs = (
         P("rep", "seq", None),
@@ -315,4 +1181,6 @@
         P(),
         P(),
     )
-    return jax.shard_map(shards, mesh=mesh, in_specs=in_specs, out_specs=out_specs, check_vma=False)
+    planes = mesh.shape["seq"] == 4 and mesh.shape["rep"] == 8
+    body = plane_plan if planes else shards
+    return jax.shard_map(body, mesh=mesh, in_specs=in_specs, out_specs=out_specs, check_vma=False)

time: 2800 us -> 379 us (0.14)
  waiting for transfers between devices: 2430 us -> 0 us
  Pallas kernels: 0 us -> 354 us
  matrix products: 152 us -> 0 us
  blocking collectives: 110 us -> 0 us
  local copies, waits for them, and re-layouts: 50.1 us -> 15.6 us
    reduce_scatter x4 -> x0, waiting for transfers between devices: 1430 us -> none  [the longest x1 622 us: shards(): lax.psum_scatter(grad_up, ('seq', 'rep'), scatter_dimension=0, tiled=True)]
    unnamed x11 -> x0, waiting for transfers between devices: 625 us -> none
    pallas_call x0 -> x1, Pallas kernels: none -> 354 us  [plane_plan(): pl.pallas_call(layer_body, out_shape=[jax.ShapeDtypeStruct((BLK, width),...]
    all_gather x5 -> x0, waiting for transfers between devices: 349 us -> none  [the longest x1 103 us: shards(): lax.all_gather(w_up, ('seq', 'rep'), axis=0, tiled=True)]
    dot_general x21 -> x0, matrix products: 152 us -> none  [the longest x5 54.3 us: token_sum(): lax.dot_general(left, right, (((0,), (0,)), ((), ())), preferred_element_...]
    unnamed x2 -> x0, blocking collectives: 89.3 us -> none
    unnamed x45 -> x15, local copies, waits for them, and re-layouts: 35.1 us -> 5.79 us
  transfers between devices with their start and end apart: 13 -> 0, of which waited for: 13 -> 0; matrix products, arithmetic and copies ran while one was open for 6% -> 0% of each run, Pallas kernels for 0% -> 0%
where the time goes in v2:
time: 379 us; the launch traced here: 374 us
  Pallas kernels  354 us (93%)
  local copies, waits for them, and re-layouts  15.6 us (4%)
    pallas_call x1, Pallas kernels, plane_plan(): pl.pallas_call(layer_body, out_shape=[jax.ShapeDtypeStruct((BLK, width),...  354 us

profile of v2, /device:TPU:1, one launch (start us, length us, event | category | flops | bytes accessed | tf_op | source)
XLA Modules:
  0.0 374.0 jit_solution(13220315050673561982)
XLA Ops:
  0.6 0.7 pad_convert_fusion
  1.3 0.7 pad_convert_fusion.2
  2.0 0.7 convert_element_type.14
  2.7 0.6 concatenate.21.small
  3.3 354.4 %shard_map.203 = (bf16[128,2048]{1,0:T(8,128)(2,1)}, f32[128,2048]{1,0:T(8,128)}, f32[64,3584]{1,0:T(8,128)}, f32[64,3584]{1,0:T(8,128)}, f32[64,3584]{1,0:T(8,1...) custom-call(bf16[128,2048]{1,0:T(8,128)(2,1)} %bitcast.26, bf16[128,2048]{1,0:T(8,128)(2,1)} %bitcast.27, ...), custom_call_target="tpu_custom_call" | custom-call | tf_op jit(solution)/shard_map/pallas_call | solution.py:1062
  357.7 0.0 copy-start.4
  357.7 1.3 slice_bitcast_fusion
  359.0 0.1 fusion.4
  359.1 0.1 fusion.5
  359.2 0.1 fusion.6
  359.3 0.1 fusion.7
  359.4 0.1 concatenate.25
  359.4 0.1 concatenate.24
  359.5 0.7 add.17
  360.2 0.1 concatenate.23
  360.3 0.1 concatenate.22
  360.4 0.7 add.16
  361.1 0.7 fusion
  361.7 0.7 fusion.1
  362.4 0.7 fusion.2
  363.1 0.7 fusion.3
  363.8 2.1 concatenate.26
  365.9 1.9 concatenate.27
  367.7 0.0 copy-done.4
  367.7 0.5 slice_bitcast_fusion.4
  368.3 0.8 copy.28
  369.1 0.0 copy-done
  369.1 1.0 copy.29
  370.0 2.2 copy.30
  372.2 0.0 copy-done.2
  372.2 0.9 copy.31
  373.1 0.9 copy.32
  (10 shorter events, 0.0 us)
Async XLA Ops:
  357.7 10.1 %copy-start.4 = (f32[8,128]{1,0:T(8,128)S(1)}, f32[8,128]{1,0:T(8,128)}, u32[]{:S(2)}) copy-start(f32[8,128]{1,0:T(8,128)} %get-tuple-element.20) | copy-start | bytes 12292
  357.7 10.6 %copy-start.3 = (bf16[128,2048]{1,0:T(8,128)(2,1)S(1)}, bf16[128,2048]{1,0:T(8,128)(2,1)}, u32[]{:S(2)}) copy-start(bf16[128,2048]{1,0:T(8,128)(2,1)} %get-tuple-element.18) | copy-start | bytes 1572868
  359.0 10.1 %copy-start = (f32[128,2048]{1,0:T(8,128)S(1)}, f32[128,2048]{1,0:T(8,128)}, u32[]{:S(2)}) copy-start(f32[128,2048]{1,0:T(8,128)} %get-tuple-element.19) | copy-start | bytes 3145732
  361.0 11.1 %copy-start.2 = (f32[64,3584]{1,0:T(8,128)S(1)}, f32[64,3584]{1,0:T(8,128)}, u32[]{:S(2)}) copy-start(f32[64,3584]{1,0:T(8,128)} %get-tuple-element.79) | copy-start | bytes 2752516
  363.8 9.4 %copy-start.1 = (f32[64,3584]{1,0:T(8,128)S(1)}, f32[64,3584]{1,0:T(8,128)}, u32[]{:S(2)}) copy-start(f32[64,3584]{1,0:T(8,128)} %get-tuple-element.80) | copy-start | bytes 2752516

commit v3 on v2

--- a/solution.py
+++ b/solution.py
@@ -293,7 +293,7 @@
 BF = jnp.bfloat16
 F32 = jnp.float32
 NEG = -1e30
-VMEM_BYTES = 61 * 2**20
+VMEM_BYTES = 63 * 2**20
 QS = 5
 DZ = 4
 BLK = 128
@@ -304,9 +304,8 @@
 AW = 1024
 QKV_W = 640
 SCALE = HD ** (-0.5)
-FF_TILES = ((0, 256), (256, 256), (512, 256), (768, 128))
-QKV_M, OUT_M, DOWN_M, GATE_M, UP_M = range(5)
-FF_AT = {DOWN_M: 2 * FFS, GATE_M: 0, UP_M: FFS}
+CHUNKS = ((0, 384), (384, 512))
+QKV_M, OUT_M, F0_M, F1_M = range(4)
 
 
 def place():
@@ -367,7 +366,7 @@
     barrier = pltpu.get_barrier_semaphore()
     for target in found:
         pl.semaphore_signal(barrier, inc=1, device_id=target, device_id_type=MESH)
-    pl.semaphore_wait(barrier, len(found))
+    return lambda: pl.semaphore_wait(barrier, len(found))
 
 
 def spread_start(src, spot, ss, rs):
@@ -469,11 +468,11 @@
 
 def layer_body(
     tok, cot, small, wq, wo, wg, wu, wd,
-    act_o, dtok_o, gate_o, up_o, down_o, ga_o, vec_o, gr,
-    wap, smallf, xf, n1, wav, w3, dyf, n2f, part, inbox, dact, active, dgu,
+    act_o, dtok_o, ga_o, gqkv_o, go_o, gf_o, gate_o, up_o, down_o, gq_o, gk_o,
+    wap, smallf, xf, n1, wav, w3, dyf, n2f, part, inbox, stage, active, dgu,
     qkvt, dqkvt, dqkv, qt, kt, kk, vt, vv, lse, att, cs, grow, hid, blk, dot_s, dkt, dvt,
-    help_f, help_a, arecv, ar, vec, vecr, vr, gp2,
-    sp_ss, sp_rs, co_ss, co_rs, w_ss, w_rs, f_ss, c_ss, c_rs, g_ss, g_rs, h_ss, h_rs, o_ss, o_rs, v_ss, v_rs, loc,
+    help_f, come_f, end_f, help_a, come_a, end_a, arecv, vec, vecr, vr, gp2,
+    sp_ss, sp_rs, co_ss, co_rs, w_ss, w_rs, l_ss, l_rs, c_ss, c_rs, g_ss, g_rs, h_ss, h_rs, o_ss, o_rs, p_ss, p_rs, v_ss, v_rs, loc,
     ready,
 ):
     x, c, z, y = place()
@@ -482,17 +481,24 @@
     mid = inner(z)
     sibling = dev(x, 1 - c, z, y)
     pair, across = near(z), DZ - 1 - z
+    far = DZ - 1 - pair
     SMALL, TOK, COT, N2, DAB = range(5)
     OUT, DN, YY, DT = range(4)
 
-    def own_piece(m, to_shard):
+    def own_pieces(m, to_shard):
         if m == QKV_M:
-            return wap.at[to_shard, :, pl.ds(0, QKV_W)]
+            return [wap.at[to_shard, :, pl.ds(0, QKV_W)]]
         if m == OUT_M:
-            return wap.at[to_shard, :, pl.ds(QKV_W, AW - QKV_W)]
-        return {DOWN_M: wd, GATE_M: wg, UP_M: wu}[m].at[
-            :, pl.ds(pl.multiple_of(to_shard * FFS, 128), FFS)
-        ]
+            return [wap.at[to_shard, :, pl.ds(QKV_W, AW - QKV_W)]]
+        lo, wide = CHUNKS[m - F0_M]
+        lanes = pl.ds(pl.multiple_of(to_shard * FFS + lo, 128), wide)
+        return [ref.at[:, lanes] for ref in (wg, wu, wd)]
+
+    def spots(m, rows):
+        if m < F0_M:
+            return [held(m, rows, BR)]
+        lo, wide = CHUNKS[m - F0_M]
+        return [w3.at[many(rows, BR), pl.ds(3 * lo + j * wide, wide)] for j in range(3)]
 
     def held(m, first, count):
         rows = many(first, count)
@@ -500,67 +506,55 @@
             return wav.at[rows, pl.ds(0, QKV_W)]
         if m == OUT_M:
             return wav.at[rows, pl.ds(QKV_W, AW - QKV_W)]
-        return w3.at[rows, pl.ds(FF_AT[m], FFS)]
+        lo, wide = CHUNKS[m - F0_M]
+        return w3.at[rows, pl.ds(3 * lo, 3 * wide)]
 
     def weights_start(m):
-        def to_plane(tz, base):
-            for dx in range(2):
-                for dy in range(2):
-                    tx, ty = flip(x, dx), flip(y, dy)
-                    send(
-                        own_piece(m, 2 * tx + ty),
-                        held(m, me * BR, BR),
-                        w_ss.at[m, base + 2 * dx + dy],
-                        w_rs.at[m, z * 4 + shard],
-                        dev(tx, c, tz, ty),
-                    )
-
-        to_plane(pair, 4)
+        for dx, dy in ((1, 1), (1, 0), (0, 1), (0, 0)):
+            tx, ty = flip(x, dx), flip(y, dy)
+            for src, spot in zip(own_pieces(m, 2 * tx + ty), spots(m, me * BR)):
+                if dx or dy:
+                    send(src, spot, w_ss.at[m, 2 * dx + dy - 1], w_rs.at[m, shard], dev(tx, c, z, ty))
+                else:
+                    pltpu.make_async_copy(src, spot, w_rs.at[m, shard]).start()
+
+    def line(m, from_plane, to_plane, k):
+        for tx in range(2):
+            slab = held(m, ((2 * tx + c) * DZ + from_plane) * 2 * BR, 2 * BR)
+            send(slab, slab, l_ss.at[m, 2 * k + tx], l_rs.at[m, 2 * from_plane + tx], dev(x, c, to_plane, y))
+
+    def line_wait(m, plane):
+        for tx in range(2):
+            arrived(held(m, 0, 2 * BR), l_rs.at[m, 2 * plane + tx])
+
+    def weights_line(m):
+        for k in range(4):
+            arrived(held(m, 0, BR), w_rs.at[m, k])
+        line(m, z, pair, 0)
 
         @pl.when(mid)
         def _():
-            to_plane(across, 8)
-
-        for dx in range(2):
-            for dy in range(2):
-                src = own_piece(m, 2 * flip(x, dx) + flip(y, dy))
-                spot = held(m, me * BR, BR)
-                sem = w_rs.at[m, z * 4 + shard]
-                if dx or dy:
-                    send(src, spot, w_ss.at[m, 2 * dx + dy], sem, dev(flip(x, dx), c, z, flip(y, dy)))
-                else:
-                    pltpu.make_async_copy(src, spot, sem).start()
-
-    def pass_on(m, from_plane, to_plane, base):
-        for tx in range(2):
-            for ty in range(2):
-                k = 2 * tx + ty
-                sem = w_rs.at[m, from_plane * 4 + k]
-                piece = held(m, ((2 * tx + c) * 2 * DZ + 2 * from_plane + ty) * BR, BR)
-                arrived(piece, sem)
-                send(piece, piece, f_ss.at[m, base + k], sem, dev(x, c, to_plane, y))
+            line(m, z, across, 1)
 
     def weights_pass_near(m):
         @pl.when(mid)
         def _():
-            pass_on(m, pair, across, 0)
-            pass_on(m, across, pair, 4)
+            line_wait(m, pair)
+            line(m, pair, across, 2)
+            line_wait(m, across)
+            line(m, across, pair, 3)
 
     def weights_pass_far(m):
         @pl.when(mid)
         def _():
-            pass_on(m, DZ - 1 - pair, pair, 8)
+            line_wait(m, far)
+            line(m, far, pair, 4)
 
     def weights_swap(m):
         @pl.when(jnp.logical_not(mid))
         def _():
-            for i in range(4 * DZ):
-                arrived(held(m, 0, BR), w_rs.at[m, i])
-
-        @pl.when(mid)
-        def _():
-            for k in range(4):
-                arrived(held(m, 0, BR), w_rs.at[m, z * 4 + k])
+            for plane in (pair, far, across):
+                line_wait(m, plane)
 
         for tx in range(2):
             half = held(m, (2 * tx + c) * HALF, HALF)
@@ -571,119 +565,119 @@
             arrived(held(m, 0, HALF), c_rs.at[m, tx])
 
     def weights_sent(m):
-        for k in range(1, 8):
+        for k in range(3):
             arrived(held(m, 0, BR), w_ss.at[m, k])
+        for k in range(2):
+            arrived(held(m, 0, 2 * BR), l_ss.at[m, k])
 
         @pl.when(mid)
         def _():
-            for k in range(8, 12):
-                arrived(held(m, 0, BR), w_ss.at[m, k])
-            for k in range(12):
-                arrived(held(m, 0, BR), f_ss.at[m, k])
+            for k in range(2, 10):
+                arrived(held(m, 0, 2 * BR), l_ss.at[m, k])
 
         for tx in range(2):
             arrived(held(m, 0, HALF), c_ss.at[m, tx])
 
-    def slot_of(to_plane):
-        return shard * 3 + z - jnp.where(to_plane >= 2, 1, 0)
-
-    def grads_to_plane(kind, piece, inbox_at, tz, base):
-        spot = inbox_at(slot_of(tz))
-        for dx in range(2):
-            for dy in range(2):
-                tx, ty = flip(x, dx), flip(y, dy)
-                send(
-                    piece(tz, tx, ty),
-                    spot,
-                    o_ss.at[kind, base + 2 * dx + dy],
-                    o_rs.at[kind, slot_of(tz)],
-                    dev(tx, c, tz, ty),
-                )
-
-    def grads_start(kind, piece, inbox_at, pair_rows, help_ref):
+    class Grad:
+        pass
+
+    def grad(kind, ref, first_row, lo, width, helped, come, final):
+        g = Grad()
+        lanes = pl.ds(lo, width)
+        g.slab = lambda tx, plane: ref.at[many(first_row + (tx * DZ + plane) * 2 * BR, 2 * BR), lanes]
+        g.helped, g.come, g.final, g.kind = helped, come, final, kind
+        return g
+
+    def start(g):
+        k = g.kind
+
         @pl.when(jnp.logical_not(mid))
         def _():
-            for i, tz in enumerate((DZ - 1 - pair, DZ - 1 - z)):
+            for i, plane in enumerate((far, across)):
                 for tx in range(2):
                     send(
-                        pair_rows(tx, tz),
-                        help_ref.at[i, pl.ds(tx * 2 * BR, 2 * BR)],
-                        h_ss.at[kind, 2 * i + tx],
-                        h_rs.at[kind, 2 * i + tx],
+                        g.slab(tx, plane), g.helped(i, tx), h_ss.at[k, 2 * i + tx], h_rs.at[k, 2 * i + tx],
                         dev(x, c, pair, y),
                     )
 
-        grads_to_plane(kind, piece, inbox_at, pair, 4)
-        spot = inbox_at(slot_of(z))
-        sem = o_rs.at[kind, slot_of(z)]
-        for dx in range(2):
-            for dy in range(2):
-                tx, ty = flip(x, dx), flip(y, dy)
-                if dx or dy:
-                    send(piece(z, tx, ty), spot, o_ss.at[kind, 2 * dx + dy], sem, dev(tx, c, z, ty))
-                else:
-                    pltpu.make_async_copy(piece(z, x, y), spot, sem).start()
-
-    def grads_join(kind, piece, inbox_at, pair_rows, help_ref):
+        for tx in range(2):
+            send(g.slab(tx, pair), g.come(0, tx), o_ss.at[k, tx], o_rs.at[k, tx], dev(x, c, pair, y))
+
+    def join(g, i):
+        k = g.kind
+        plane = (across, far)[i]
+
         @pl.when(mid)
         def _():
-            for i, tz in enumerate((across, DZ - 1 - pair)):
+            for _ in range(1):
                 for tx in range(2):
-                    rows = pair_rows(tx, tz)
-                    arrived(rows, h_rs.at[kind, 2 * i + tx])
-                    rows[...] = (
-                        rows[...].astype(F32)
-                        + help_ref[i, tx * 2 * BR : (tx + 1) * 2 * BR, :].astype(F32)
-                    ).astype(BF)
-                grads_to_plane(kind, piece, inbox_at, tz, 8 + 4 * i)
-
-    def grads_wait(kind, inbox_at, pair_rows):
-        for k in range(12):
-            arrived(inbox_at(0), o_rs.at[kind, k])
-        for k in range(1, 8):
-            arrived(inbox_at(0), o_ss.at[kind, k])
+                    rows, more = g.slab(tx, plane), g.helped(i, tx)
+                    arrived(more, h_rs.at[k, 2 * i + tx])
+                    rows[...] = (rows[...].astype(F32) + more[...].astype(F32)).astype(BF)
+                    send(
+                        rows, g.come(1, tx), o_ss.at[k, 2 + 2 * i + tx], o_rs.at[k, 2 + tx], dev(x, c, plane, y)
+                    )
+
+    def finish(g):
+        k = g.kind
+        for tx in range(2):
+            rows = g.slab(tx, z)
+            for i in range(2):
+                arrived(rows, o_rs.at[k, 2 * i + tx])
+            rows[...] = (
+                rows[...].astype(F32) + g.come(0, tx)[...].astype(F32) + g.come(1, tx)[...].astype(F32)
+            ).astype(BF)
+        for dx, dy in ((1, 1), (1, 0), (0, 1), (0, 0)):
+            tx, ty = flip(x, dx), flip(y, dy)
+            src = g.slab(tx, z).at[many(ty * BR, BR)]
+            if dx or dy:
+                send(src, g.final(shard), p_ss.at[k, 2 * dx + dy - 1], p_rs.at[k, shard], dev(tx, c, z, ty))
+            else:
+                pltpu.make_async_copy(src, g.final(shard), p_rs.at[k, shard]).start()
+
+    def final_wait(g):
+        for t in range(4):
+            arrived(g.final(0), p_rs.at[g.kind, t])
+
+    def grad_sent(g):
+        k = g.kind
+        for i in range(3):
+            arrived(g.final(0), p_ss.at[k, i])
+        for i in range(2):
+            arrived(g.slab(0, 0), o_ss.at[k, i])
 
         @pl.when(mid)
         def _():
-            for k in range(8, 16):
-                arrived(inbox_at(0), o_ss.at[kind, k])
+            for i in range(2, 6):
+                arrived(g.slab(0, 0), o_ss.at[k, i])
 
         @pl.when(jnp.logical_not(mid))
         def _():
-            for k in range(4):
-                arrived(pair_rows(0, 0), h_ss.at[kind, k])
-
-    def grad_refs(ref, first_row, lo, width, inbox, helper):
-        lanes = pl.ds(lo, width)
-
-        def piece(tz, tx, ty):
-            return ref.at[many(first_row + ((tx * DZ + tz) * 2 + ty) * BR, BR), lanes]
-
-        def inbox_at(slot):
-            return inbox.at[many(slot * BR, BR), lanes]
-
-        def pair_rows(tx, tz):
-            return ref.at[many(first_row + (tx * DZ + tz) * 2 * BR, 2 * BR), lanes]
-
-        return piece, inbox_at, pair_rows, helper
-
-    ffn_refs = [
-        grad_refs(w3, 1024, j * FFS, FFS, gr, help_f.at[j]) for j in range(3)
-    ]
-    out_refs = grad_refs(arecv, 0, QKV_W, AW - QKV_W, ar, help_a.at[:, :, pl.ds(QKV_W, AW - QKV_W)])
-    qkv_refs = grad_refs(arecv, 0, 0, QKV_W, ar, help_a.at[:, :, pl.ds(0, QKV_W)])
-    kind_refs = ffn_refs + [out_refs, qkv_refs]
-
-    def join(kind):
-        grads_join(kind, *kind_refs[kind])
-
-    def start(kind):
-        grads_start(kind, *kind_refs[kind])
-
-    greet(x, c, z, y)
-    spot = smallf.at[:, many((2 * x + c) * BLK, BLK)]
-    spread_start(small, spot, sp_ss.at[SMALL], sp_rs.at[SMALL])
-    spread_start(tok, rows_of(xf, 2 * x + c, BLK), sp_ss.at[TOK], sp_rs.at[TOK])
+            for i in range(4):
+                arrived(g.slab(0, 0), h_ss.at[k, i])
+
+    def ffn_grad(j):
+        lo, wide = CHUNKS[j]
+        lanes = pl.ds(3 * lo, 3 * wide)
+        return grad(
+            j, w3, 1024, 3 * lo, 3 * wide,
+            lambda i, tx: help_f.at[i, pl.ds(tx * 2 * BR, 2 * BR), lanes],
+            lambda i, tx: come_f.at[i, pl.ds(tx * 2 * BR, 2 * BR), lanes],
+            lambda t: end_f.at[t, :, lanes],
+        )
+
+    def att_grad(kind):
+        lanes = pl.ds(ATT_LO[kind], ATT_WIDE[kind])
+        return grad(
+            kind, arecv, 0, ATT_LO[kind], ATT_WIDE[kind],
+            lambda i, tx: help_a.at[i, pl.ds(tx * 2 * BR, 2 * BR), lanes],
+            lambda i, tx: come_a.at[i, pl.ds(tx * 2 * BR, 2 * BR), lanes],
+            lambda t: end_a.at[t, :, lanes],
+        )
+
+    F0, F1, GO, GQ = ffn_grad(0), ffn_grad(1), att_grad(2), att_grad(3)
+
+    everyone_here = greet(x, c, z, y)
     turned = jnp.transpose(small[...])
     lane = lax.broadcasted_iota(jnp.int32, (BR, 64), 1)
     gains = jnp.where(lane == 0, turned[0:64, 0:1], jnp.where(lane == 1, turned[0:64, 1:2], 0.0))
@@ -695,8 +689,16 @@
         wap[t, :, 576:640] = gains.astype(BF)
         wap[t, :, 640:960] = wo[:, 320 * t : 320 * t + 320]
         wap[t, :, 960:1024] = jnp.zeros((BR, 64), BF)
+    everyone_here()
     weights_start(QKV_M)
+    spot = smallf.at[:, many((2 * x + c) * BLK, BLK)]
+    spread_start(small, spot, sp_ss.at[SMALL], sp_rs.at[SMALL])
     weights_start(OUT_M)
+    spread_start(tok, rows_of(xf, 2 * x + c, BLK), sp_ss.at[TOK], sp_rs.at[TOK])
+    weights_start(F0_M)
+    weights_start(F1_M)
+    weights_line(QKV_M)
+    weights_line(OUT_M)
     spread_wait(spot, sp_rs.at[SMALL])
     seg_row = smallf[4:5, :]
     seg_col = jnp.transpose(smallf[...])[:, 4:5]
@@ -708,16 +710,15 @@
     angles = fr * (index - earlier)
     cs[0:32, :] = jnp.cos(angles)
     cs[32:64, :] = jnp.sin(angles)
+    weights_pass_near(QKV_M)
+    weights_pass_near(OUT_M)
+    weights_pass_far(QKV_M)
+    weights_pass_far(OUT_M)
+    weights_line(F0_M)
+    weights_line(F1_M)
+    weights_swap(QKV_M)
     spread_wait(rows_of(xf, 0, BLK), sp_rs.at[TOK])
-    weights_pass_near(QKV_M)
-    weights_pass_far(QKV_M)
-    weights_pass_near(OUT_M)
-    weights_pass_far(OUT_M)
-    for m in (DOWN_M, GATE_M, UP_M):
-        weights_start(m)
     spread_start(cot, rows_of(dyf, 2 * x + c, BLK), sp_ss.at[COT], sp_rs.at[COT])
-    weights_swap(QKV_M)
-    weights_swap(OUT_M)
     weights_wait(QKV_M)
     grow[...] = jnp.transpose(wav[:, 512:640].astype(F32))[64:72, :]
 
@@ -753,6 +754,7 @@
         value = qkvt[base + 128 : base + 192, :]
         vt[g] = value.astype(BF)
         vv[g] = jnp.transpose(value).astype(BF)
+    weights_swap(OUT_M)
     dqkvt[QS * 64 : 384, :] = jnp.zeros((384 - QS * 64, LEN4), F32)
     for h in range(QS):
         g = group_of(h)
@@ -763,13 +765,14 @@
         lse[h : h + 1, :] = top + jnp.log(total)
         dqkvt[h * 64 : h * 64 + 64, :] = mm(vt[g], (weights / total).astype(BF))
     att[...] = jnp.transpose(dqkvt[0:384, :]).astype(BF)
+    weights_pass_near(F0_M)
     weights_wait(OUT_M)
     for order in range(4):
         rows = many(block_at(order) * BLK, BLK)
         part[0, rows, :] = mm_nt(att[rows, :], wav[:, QKV_W:AW]).astype(BF)
         collect_start(order, part.at[0], inbox.at[0], co_ss.at[OUT], co_rs.at[OUT])
-    for m in (DOWN_M, GATE_M, UP_M):
-        weights_pass_near(m)
+    weights_pass_near(F1_M)
+    weights_pass_far(F0_M)
     collect_wait(inbox.at[0], co_rs.at[OUT])
     hidden = tok[...].astype(F32) + inbox_sum(inbox.at[0])
     hid[...] = hidden
@@ -779,69 +782,113 @@
         * grow[1:2, :]
     ).astype(BF)
     spread_start(blk.at[0], rows_of(n2f, 2 * x + c, BLK), sp_ss.at[N2], sp_rs.at[N2])
-    for m in (DOWN_M, GATE_M, UP_M):
-        weights_pass_far(m)
-    weights_swap(DOWN_M)
+    weights_pass_far(F1_M)
+    weights_swap(F0_M)
     spread_wait(rows_of(dyf, 0, BLK), sp_rs.at[COT])
-    weights_wait(DOWN_M)
-    for lo, wide in FF_TILES:
-        dact[:, lo : lo + wide] = mm(dyf[...], w3[:, 2 * FFS + lo : 2 * FFS + lo + wide])
-    weights_swap(GATE_M)
-    weights_swap(UP_M)
     spread_wait(rows_of(n2f, 0, BLK), sp_rs.at[N2])
-    weights_wait(GATE_M)
-    weights_wait(UP_M)
-    for lo, wide in FF_TILES:
-        gate = mm(n2f[...], w3[:, lo : lo + wide])
-        upward = mm(n2f[...], w3[:, FFS + lo : FFS + lo + wide])
-        sig = 1.0 / (1.0 + jnp.exp(-gate))
-        silu = gate * sig
-        grad = dact[:, lo : lo + wide]
-        active[:, lo : lo + wide] = (silu * upward).astype(BF)
-        dgu[:, lo : lo + wide] = (grad * upward * (sig * (1.0 + gate * (1.0 - sig)))).astype(BF)
-        dgu[:, FFS + lo : FFS + lo + wide] = (grad * silu).astype(BF)
+    weights_wait(F0_M)
+
+    def hidden_units(j):
+        first, width = CHUNKS[j]
+        base = 3 * first
+        for lo in range(0, width, 256):
+            wide = min(256, width - lo)
+            gate = mm(n2f[...], w3[:, base + lo : base + lo + wide])
+            upward = mm(n2f[...], w3[:, base + width + lo : base + width + lo + wide])
+            grad_in = mm(dyf[...], w3[:, base + 2 * width + lo : base + 2 * width + lo + wide])
+            sig = 1.0 / (1.0 + jnp.exp(-gate))
+            silu = gate * sig
+            active[:, first + lo : first + lo + wide] = (silu * upward).astype(BF)
+            at = 2 * first + lo
+            dgu[:, at : at + wide] = (grad_in * upward * (sig * (1.0 + gate * (1.0 - sig)))).astype(BF)
+            at = at + width
+            dgu[:, at : at + wide] = (grad_in * silu).astype(BF)
+
+    def dn_part(j, rows, wide):
+        first, width = CHUNKS[j]
+        return mm_nt(dgu[rows, 2 * first : 2 * first + 2 * width], w3[wide, 3 * first : 3 * first + 2 * width])
+
+    def y_part(j, rows, wide):
+        first, width = CHUNKS[j]
+        at = 3 * first + 2 * width
+        return mm_nt(active[rows, first : first + width], w3[wide, at : at + width])
+
+    def ffn_grads(j, core, row):
+        first, width = CHUNKS[j]
+        wide = many((2 * lax.div(row, 2) + core) * HALF + lax.rem(row, 2) * 256, 256)
+        return (
+            mm_tn(n2f[:, wide], dgu[:, 2 * first : 2 * first + 2 * width]),
+            mm_tn(dyf[:, wide], active[:, first : first + width]),
+        )
+
+    def chunk_lanes(j):
+        first, width = CHUNKS[j]
+        return pl.ds(3 * first, 2 * width), pl.ds(3 * first + 2 * width, width), pl.ds(3 * first, 3 * width)
+
+    def grads_swap(j):
+        two, one, both = chunk_lanes(j)
+        weights_sent(F0_M + j)
+        pl.semaphore_signal(ready.at[j], inc=1, device_id=sibling, device_id_type=MESH)
+
+        @pl.loop(0, 4)
+        def _(row):
+            rows = many(row * 256, 256)
+            gu, down = ffn_grads(j, 1 - c, row)
+            w3[rows, two] = gu.astype(BF)
+            w3[rows, one] = down.astype(BF)
+
+        pl.semaphore_wait(ready.at[j], 1)
+        send(
+            w3.at[pl.ds(0, 1024), both], w3.at[pl.ds(1024, 1024), both], g_ss.at[j], g_rs.at[j], sibling
+        )
+
+    def grads_own(j):
+        two, one, both = chunk_lanes(j)
+        arrived(w3.at[pl.ds(1024, 1024), both], g_rs.at[j])
+
+        @pl.loop(0, 4)
+        def _(row):
+            rows = many(1024 + row * 256, 256)
+            gu, down = ffn_grads(j, c, row)
+            w3[rows, two] = (gu + w3[rows, two].astype(F32)).astype(BF)
+            w3[rows, one] = (down + w3[rows, one].astype(F32)).astype(BF)
+
+    every = slice(0, LEN4)
+    hidden_units(0)
+    collect_sent(inbox.at[0], co_ss.at[OUT])
+
+    @pl.loop(0, 8)
+    def _(j):
+        wide = many(j * 256, 256)
+        part[1, :, wide] = dn_part(0, every, wide).astype(BF)
+        part[0, :, wide] = y_part(0, every, wide).astype(BF)
+
+    grads_swap(0)
+    grads_own(0)
+    start(F0)
+    weights_swap(F1_M)
+    weights_wait(F1_M)
+    hidden_units(1)
     for order in range(4):
         rows = many(block_at(order) * BLK, BLK)
 
         @pl.loop(0, 4)
         def _(j):
             wide = many(j * 512, 512)
-            part[1, rows, wide] = mm_nt(dgu[rows, :], w3[wide, 0 : 2 * FFS]).astype(BF)
+            part[1, rows, wide] = (part[1, rows, wide].astype(F32) + dn_part(1, rows, wide)).astype(BF)
 
         collect_start(order, part.at[1], inbox.at[1], co_ss.at[DN], co_rs.at[DN])
-    collect_sent(inbox.at[0], co_ss.at[OUT])
-    for order in range(4):
-        rows = many(block_at(order) * BLK, BLK)
-
-        @pl.loop(0, 4)
-        def _(j):
-            wide = many(j * 512, 512)
-            part[0, rows, wide] = mm_nt(active[rows, :], w3[wide, 2 * FFS : 3 * FFS]).astype(BF)
-
-        collect_start(order, part.at[0], inbox.at[0], co_ss.at[YY], co_rs.at[YY])
-    for m in range(5):
-        weights_sent(m)
-    pl.semaphore_signal(ready, inc=1, device_id=sibling, device_id_type=MESH)
-
-    def ffn_grads(core, row, j):
-        first = (2 * lax.div(row, 2) + core) * HALF + lax.rem(row, 2) * 256
-        wide = many(first, 256)
-        if j < 2:
-            return mm_tn(n2f[:, wide], dgu[:, j * FFS : (j + 1) * FFS])
-        return mm_tn(dyf[:, wide], active[...])
-
-    for j in range(3):
-        lanes = pl.ds(j * FFS, FFS)
-
-        @pl.loop(0, 4)
-        def _(row):
-            w3[many(row * 256, 256), lanes] = ffn_grads(1 - c, row, j).astype(BF)
-
-        if j == 0:
-            pl.semaphore_wait(ready, 1)
-        send(
-            w3.at[pl.ds(0, 1024), lanes], w3.at[pl.ds(1024, 1024), lanes], g_ss.at[j], g_rs.at[j], sibling
-        )
+
+    @pl.loop(0, 8)
+    def _(j):
+        wide = many(j * 256, 256)
+        part[0, :, wide] = (part[0, :, wide].astype(F32) + y_part(1, every, wide)).astype(BF)
+
+    grads_swap(1)
+    join(F0, 0)
+    grads_own(1)
+    start(F1)
+    join(F0, 1)
     collect_wait(inbox.at[1], co_rs.at[DN])
     dn = inbox_sum(inbox.at[1])
     h = hid[...]
@@ -852,20 +899,51 @@
     dtok_o[...] = dh
     blk[1] = dh.astype(BF)
     spread_start(blk.at[1], rows_of(xf, 2 * x + c, BLK), sp_ss.at[DAB], sp_rs.at[DAB])
-    for j in range(3):
-        lanes = pl.ds(j * FFS, FFS)
-        arrived(w3.at[pl.ds(1024, 1024), lanes], g_rs.at[j])
-
+    for order in range(4):
+        collect_start(order, part.at[0], inbox.at[0], co_ss.at[YY], co_rs.at[YY])
+    finish(F0)
+    join(F1, 0)
+    def att_grads(core, row, kind):
+        wide = many((2 * lax.div(row, 2) + core) * HALF + lax.rem(row, 2) * 256, 256)
+        if kind == 3:
+            return mm_tn(n1[:, wide], dqkv[...])
+        return mm_tn(xf[:, wide], att[...])
+
+    att_lanes = {k: pl.ds(ATT_LO[k], ATT_WIDE[k]) for k in (2, 3)}
+
+    def att_grads_swap(kind):
         @pl.loop(0, 4)
         def _(row):
-            rows = many(1024 + row * 256, 256)
-            w3[rows, lanes] = (ffn_grads(c, row, j) + w3[rows, lanes].astype(F32)).astype(BF)
-
-        start(j)
-    collect_wait(inbox.at[0], co_rs.at[YY])
-    act_o[...] = (hid[...] + inbox_sum(inbox.at[0])).astype(BF)
+            side = lax.div(row, 2) * AW + ATT_LO[kind]
+            dyf[many(lax.rem(row, 2) * 256, 256), pl.ds(pl.multiple_of(side, 128), ATT_WIDE[kind])] = (
+                att_grads(1 - c, row, kind).astype(BF)
+            )
+
+        for side in range(2):
+            send(
+                dyf.at[:, pl.ds(side * AW + ATT_LO[kind], ATT_WIDE[kind])],
+                arecv.at[pl.ds(side * HALF, HALF), att_lanes[kind]],
+                g_ss.at[2 * kind - 2 + side],
+                g_rs.at[2 * kind - 2 + side],
+                sibling,
+            )
+
+    def att_grads_own(kind):
+        for side in range(2):
+            arrived(arecv.at[pl.ds(0, HALF), att_lanes[kind]], g_rs.at[2 * kind - 2 + side])
+
+        @pl.loop(0, 4)
+        def _(row):
+            rows = many(row * 256, 256)
+            arecv[rows, att_lanes[kind]] = (
+                att_grads(c, row, kind) + arecv[rows, att_lanes[kind]].astype(F32)
+            ).astype(BF)
+
     spread_wait(rows_of(xf, 0, BLK), sp_rs.at[DAB])
+    att_grads_swap(2)
     dot_s[...] = jnp.transpose(mm(xf[...], wav[:, QKV_W:AW]).astype(BF).astype(F32)).astype(BF)
+    att_grads_own(2)
+    start(GO)
     dkt[...] = jnp.zeros_like(dkt)
     dvt[...] = jnp.zeros_like(dvt)
 
@@ -893,8 +971,8 @@
         d, more = unrotated(dq[0:32, :], dq[32:64, :], qkvt[h * 64 : h * 64 + 64, :], gq)
         dq_gain = dq_gain + more
         dqkvt[h * 64 : h * 64 + 64, :] = d
-        if h in JOIN_AFTER:
-            join(JOIN_AFTER[h])
+        for g_at, i in JOIN_AFTER.get(h, ()):
+            join((F0, F1, GO, GQ)[g_at], i)
     dk_gain = jnp.zeros((64, 1), F32)
     for g in range(2):
         base = QS * 64 + g * 64
@@ -911,43 +989,14 @@
         part[1, rows, :] = mm_nt(dqkv[rows, :], wav[:, 0:QKV_W]).astype(BF)
         collect_start(order, part.at[1], inbox.at[1], co_ss.at[DT], co_rs.at[DT])
 
-    def att_grads(core, row, kind):
-        first = (2 * lax.div(row, 2) + core) * HALF + lax.rem(row, 2) * 256
-        wide = many(first, 256)
-        if kind == 4:
-            return mm_tn(n1[:, wide], dqkv[...])
-        return mm_tn(xf[:, wide], att[...])
-
-    att_lanes = {k: pl.ds(ATT_LO[k], ATT_WIDE[k]) for k in (3, 4)}
-    for kind in (3, 4):
-
-        @pl.loop(0, 4)
-        def _(row):
-            side = lax.div(row, 2) * AW + ATT_LO[kind]
-            dyf[many(lax.rem(row, 2) * 256, 256), pl.ds(pl.multiple_of(side, 128), ATT_WIDE[kind])] = (
-                att_grads(1 - c, row, kind).astype(BF)
-            )
-
-        for side in range(2):
-            send(
-                dyf.at[:, pl.ds(side * AW + ATT_LO[kind], ATT_WIDE[kind])],
-                arecv.at[pl.ds(side * HALF, HALF), att_lanes[kind]],
-                g_ss.at[2 * kind - 3 + side],
-                g_rs.at[2 * kind - 3 + side],
-                sibling,
-            )
-    for kind in (3, 4):
-        for side in range(2):
-            arrived(arecv.at[pl.ds(0, HALF), att_lanes[kind]], g_rs.at[2 * kind - 3 + side])
-
-        @pl.loop(0, 4)
-        def _(row):
-            rows = many(row * 256, 256)
-            arecv[rows, att_lanes[kind]] = (
-                att_grads(c, row, kind) + arecv[rows, att_lanes[kind]].astype(F32)
-            ).astype(BF)
-
-        start(kind)
+    att_grads_swap(3)
+    att_grads_own(3)
+    start(GQ)
+    join(GO, 0)
+    join(GO, 1)
+    finish(F1)
+    collect_wait(inbox.at[0], co_rs.at[YY])
+    act_o[...] = (hid[...] + inbox_sum(inbox.at[0])).astype(BF)
     collect_wait(inbox.at[1], co_rs.at[DT])
     dn = inbox_sum(inbox.at[1])
     xv = tok[...].astype(F32)
@@ -968,8 +1017,8 @@
             vec[half, i, 0:4, 0:64] = jnp.concatenate(
                 [gain_a[:, at : at + BR], gain_b[:, at : at + BR], qk[0:1, 0:64], qk[0:1, 64:128]], axis=0
             )
-    send(vec.at[1 - c], vecr, g_ss.at[7], g_rs.at[7], sibling)
-    arrived(vecr, g_rs.at[7])
+    send(vec.at[1 - c], vecr, g_ss.at[6], g_rs.at[6], sibling)
+    arrived(vecr, g_rs.at[6])
     vecr[...] += vec[c]
     source = shard * DZ + z
     for dz in range(DZ):
@@ -982,51 +1031,60 @@
                     pltpu.make_async_copy(src, vr.at[source], v_rs.at[source]).start()
                 else:
                     send(src, vr.at[source], v_ss.at[k], v_rs.at[source], dev(tx, c, tz, ty))
-    join(3)
-    join(4)
-    for j in range(3):
-        grads_wait(j, *kind_refs[j][1:3])
-    for j in range(3):
-        arrived(w3.at[pl.ds(0, 1024), pl.ds(j * FFS, FFS)], g_ss.at[j])
-    load = pltpu.make_async_copy(gr, w3.at[pl.ds(0, 12 * BR)], loc.at[0])
-    load.start()
-    load.wait()
-
-    def three(ref, t, lo, width):
-        lanes = pl.ds(lo, width)
-        at = t * 3 * BR
-        return (
-            ref[at : at + BR, lanes].astype(F32) + ref[at + BR : at + 2 * BR, lanes].astype(F32)
-        ) + ref[at + 2 * BR : at + 3 * BR, lanes].astype(F32)
-
+    join(GQ, 0)
+    join(GQ, 1)
+    finish(GO)
     leave = []
+    for g in (F0, F1):
+        final_wait(g)
     for j, out in enumerate((gate_o, up_o, down_o)):
         for t in range(4):
-            rows = pl.ds((j % 2) * 4 * BR + t * BR, BR)
-            if j == 2:
-                leave[t].wait()
-            dact[rows, :] = three(w3, t, j * FFS, FFS)
+            rows = pl.ds(t * BR, BR)
+            if j > 0:
+                leave[4 * (j - 1) + t].wait()
+            for first, width in CHUNKS:
+                at = 3 * first + j * width
+                stage[rows, first : first + width] = end_f[t, :, at : at + width].astype(F32)
             leave.append(
                 pltpu.make_async_copy(
-                    dact.at[rows], out.at[:, pl.ds(t * FFS, FFS)], loc.at[1 + 4 * j + t]
+                    stage.at[rows], out.at[:, pl.ds(t * FFS, FFS)], loc.at[4 * j + t]
                 )
             )
             leave[-1].start()
-    for j in (3, 4):
-        grads_wait(j, *kind_refs[j][1:3])
-    for t in range(4):
-        ga_o[t] = three(ar, t, 0, AW)
+    finish(GQ)
     for i in range(4 * DZ):
         arrived(vr.at[0], v_rs.at[i])
+    sums = jnp.sum(vr[...], axis=0)
+    for i, out in enumerate((ga_o, gf_o, gq_o, gk_o)):
+        out[...] = sums[i : i + 1, 0:64]
+    final_wait(GO)
+    for t in range(4):
+        go_o[:, 320 * t : 320 * t + 320] = end_a[t, :, 640:960].astype(F32)
+    final_wait(GQ)
+    for t in range(4):
+        gqkv_o[:, 320 * t : 320 * t + 320] = end_a[t, :, 0:320].astype(F32)
+    for lo, to in ((320, QW), (448, QW + KW)):
+        for g in range(5):
+            parts = []
+            if g < 4:
+                parts.append(end_a[g, :, lo : lo + 64].astype(F32))
+            if g > 0:
+                parts.append(end_a[g - 1, :, lo + 64 : lo + 128].astype(F32))
+            gqkv_o[:, to + 64 * g : to + 64 * g + 64] = sum(parts[1:], parts[0])
+    for copy in leave[8:]:
+        copy.wait()
+    for g in (F0, F1, GO, GQ):
+        grad_sent(g)
+    weights_sent(QKV_M)
+    weights_sent(OUT_M)
     for i in range(1, 4 * DZ):
         arrived(vr.at[0], v_ss.at[i])
-    for copy in leave[4:]:
-        copy.wait()
-    vec_o[...] = jnp.sum(vr[...], axis=0)
-    for j in (3, 4):
+    for j in range(2):
+        arrived(w3.at[pl.ds(0, 1024), chunk_lanes(j)[2]], g_ss.at[j])
+    for j in (2, 3):
         for side in range(2):
-            arrived(arecv.at[pl.ds(0, HALF), att_lanes[j]], g_ss.at[2 * j - 3 + side])
-    arrived(vecr, g_ss.at[7])
+            arrived(arecv.at[pl.ds(0, HALF), att_lanes[j]], g_ss.at[2 * j - 2 + side])
+    arrived(vecr, g_ss.at[6])
     spread_sent(small, sp_ss.at[SMALL])
     spread_sent(tok, sp_ss.at[TOK])
     spread_sent(cot, sp_ss.at[COT])
@@ -1036,9 +1094,9 @@
     collect_sent(inbox.at[1], co_ss.at[DT])
 
 
-JOIN_AFTER = {1: 0, 3: 1, 4: 2}
-ATT_LO = {3: QKV_W, 4: 0}
-ATT_WIDE = {3: AW - QKV_W, 4: QKV_W}
+JOIN_AFTER = {4: ((1, 1),)}
+ATT_LO = {2: QKV_W, 3: 0}
+ATT_WIDE = {2: AW - QKV_W, 3: QKV_W}
 
 
 def plane_plan(
@@ -1059,20 +1117,23 @@
     dma = pltpu.SemaphoreType.DMA
     vm = pltpu.VMEM
     far, close = pl.BlockSpec(memory_space=pl.ANY), pl.BlockSpec(memory_space=pltpu.VMEM)
-    act, dtok, gate, up, down, ga, vec, _ = pl.pallas_call(
+    outs = pl.pallas_call(
         layer_body,
         out_shape=[
             jax.ShapeDtypeStruct((BLK, width), BF),
             jax.ShapeDtypeStruct((BLK, width), F32),
-            jax.ShapeDtypeStruct((BR, 4 * FFS), F32),
-            jax.ShapeDtypeStruct((BR, 4 * FFS), F32),
-            jax.ShapeDtypeStruct((BR, 4 * FFS), F32),
-            jax.ShapeDtypeStruct((4, BR, AW), F32),
-            jax.ShapeDtypeStruct((8, BLK), F32),
-            jax.ShapeDtypeStruct((12 * BR, 3 * FFS), BF),
+            jax.ShapeDtypeStruct((1, BR), F32),
+            jax.ShapeDtypeStruct(w_qkv.shape, F32),
+            jax.ShapeDtypeStruct(w_out.shape, F32),
+            jax.ShapeDtypeStruct((1, BR), F32),
+            jax.ShapeDtypeStruct(w_gate.shape, F32),
+            jax.ShapeDtypeStruct(w_up.shape, F32),
+            jax.ShapeDtypeStruct(w_down.shape, F32),
+            jax.ShapeDtypeStruct((1, HD), F32),
+            jax.ShapeDtypeStruct((1, HD), F32),
         ],
         in_specs=[close] * 5 + [far] * 3,
-        out_specs=[close] * 2 + [far] * 3 + [close] * 2 + [far],
+        out_specs=[close] * 6 + [far] * 3 + [close] * 2,
         scratch_shapes=[
             vm((4, BR, AW), BF),
             vm((8, LEN4), F32),
@@ -1084,7 +1145,7 @@
             vm((LEN4, width), BF),
             vm((2, LEN4, width), BF),
             vm((2, 4, BLK, width), BF),
-            vm((LEN4, FFS), F32),
+            vm((4 * BR, FFS), F32),
             vm((LEN4, FFS), BF),
             vm((LEN4, 2 * FFS), BF),
             vm((QKV_W, LEN4), F32),
@@ -1104,24 +1165,27 @@
             vm((384, LEN4), BF),
             vm((2, 64, LEN4), F32),
             vm((2, 64, LEN4), F32),
-            vm((3, 2, 4 * BR, FFS), BF),
+            vm((2, 4 * BR, 3 * FFS), BF),
+            vm((2, 4 * BR, 3 * FFS), BF),
+            vm((4, BR, 3 * FFS), BF),
             vm((2, 4 * BR, AW), BF),
+            vm((2, 4 * BR, AW), BF),
+            vm((4, BR, AW), BF),
             vm((1024, AW), BF),
-            vm((12 * BR, AW), BF),
             vm((2, 4 * DZ, 8, BLK), F32),
             vm((4 * DZ, 8, BLK), F32),
             vm((4 * DZ, 8, BLK), F32),
             vm((8, width), F32),
             dma((5, 4)), dma((5, 4)),
             dma((4, 4)), dma((4, 4)),
-            dma((5, 12)), dma((5, 16)), dma((5, 12)),
+            dma((5, 3)), dma((5, 4)), dma((5, 10)), dma((5, 8)),
             dma((5, 2)), dma((5, 2)),
             dma((8,)), dma((8,)),
             dma((5, 4)), dma((5, 4)),
-            dma((5, 16)), dma((5, 12)),
+            dma((5, 6)), dma((5, 4)), dma((5, 3)), dma((5, 4)),
             dma((16,)), dma((16,)),
-            dma((13,)),
-            pltpu.SemaphoreType.REGULAR,
+            dma((12,)),
+            pltpu.SemaphoreType.REGULAR((2,)),
         ],
         compiler_params=pltpu.CompilerParams(
             collective_id=0, has_side_effects=True, vmem_limit_bytes=VMEM_BYTES
@@ -1129,28 +1193,11 @@
     )(
         tokens.reshape(BLK, width), cotangent.reshape(BLK, width), small, w_qkv, w_out, w_gate, w_up, w_down
     )
-    none = jnp.zeros((BR, 64), F32)
-
-    def groups(at):
-        first = jnp.concatenate([ga[t][:, at : at + 64] for t in range(4)] + [none], axis=1)
-        second = jnp.concatenate([none] + [ga[t][:, at + 64 : at + 128] for t in range(4)], axis=1)
-        return first + second
-
-    g_qkv = jnp.concatenate([ga[t][:, 0:320] for t in range(4)] + [groups(320), groups(448)], axis=1)
-    g_out = jnp.concatenate([ga[t][:, 640:960] for t in range(4)], axis=1)
-    return (
-        act.reshape(tokens.shape),
-        dtok.reshape(tokens.shape),
-        vec[0, :64],
-        g_qkv,
-        g_out,
-        vec[1, :64],
-        gate,
-        up,
-        down,
-        vec[2, :64],
-        vec[3, :64],
-    )
+    shapes = (
+        tokens.shape, tokens.shape, (BR,), w_qkv.shape, w_out.shape, (BR,), w_gate.shape, w_up.shape, w_down.shape,
+        (HD,), (HD,),
+    )
+    return tuple(out.reshape(shape) for out, shape in zip(outs, shapes))
 
 
 def solution(mesh):

time: 379 us -> 298 us (0.79); the launches traced: 374 us -> 297 us
  Pallas kernels: 354 us -> 283 us
    pallas_call x1, Pallas kernels: 354 us -> 283 us  [plane_plan(): pl.pallas_call(layer_body, out_shape=[jax.ShapeDtypeStruct((BLK, width),...]
    unnamed x15 -> x41, local copies, waits for them, and re-layouts: 5.79 us -> 12.5 us
    concatenate x6 -> x0, local copies, waits for them, and re-layouts: 4.34 us -> none  [the longest x1 2.09 us: plane_plan(): jnp.concatenate([ga[t][:, 0:320] for t in range(4)] + [groups(320), group...]
where the time goes in v3:
time: 298 us; the launch traced here: 297 us
  Pallas kernels  283 us (95%)
  local copies, waits for them, and re-layouts  13.1 us (4%)
    pallas_call x1, Pallas kernels, plane_plan(): pl.pallas_call(layer_body, out_shape=[jax.ShapeDtypeStruct((BLK, width),...  283 us
    unnamed x41, local copies, waits for them, and re-layouts  12.5 us

profile of v3, /device:TPU:1, one launch (start us, length us, event | category | flops | bytes accessed | tf_op | source)
XLA Modules:
  0.0 297.4 jit_solution(8812131528759201798)
XLA Ops:
  0.6 0.0 copy-start.10
  0.7 0.6 copy-done.10
  1.3 0.0 copy-start.6
  1.3 0.0 copy-start.7
  1.3 0.6 copy-done.6
  2.0 0.0 copy-done.7
  2.0 0.6 copy-done.8
  2.7 0.0 copy-done.9
  2.7 0.6 concatenate.3.small
  3.3 283.5 %shard_map.203 = (bf16[128,2048]{1,0:T(8,128)(2,1)}, f32[128,2048]{1,0:T(8,128)}, f32[1,64]{1,0:T(1,128)}, f32[64,1920]{1,0:T(8,128)}, f32[64,1280]{1,0:T(8,128)...) custom-call(bf16[128,2048]{1,0:T(8,128)(2,1)} %bitcast.14, ...), custom_call_target="tpu_custom_call" | custom-call | tf_op jit(solution)/shard_map/pallas_call | solution.py:1120
  286.8 0.0 copy-start
  286.8 2.0 copy.34
  288.8 0.0 copy-done
  288.8 1.0 copy.35
  289.7 0.0 copy-done.14
  289.7 0.5 copy.36
  290.3 0.0 copy-done.4
  290.3 0.8 copy.37
  291.0 0.0 copy-done.5
  291.0 0.7 copy.38
  291.8 0.0 copy-done.13
  291.8 0.5 copy.39
  292.3 0.0 copy-done.3
  292.3 0.9 copy.40
  293.2 0.6 copy-done.2
  293.8 0.9 copy.41
  294.7 0.6 copy-done.1
  295.3 0.9 copy.42
  296.2 0.0 copy-done.12
  296.2 0.5 copy.43
  296.7 0.1 copy-done.11
  296.8 0.5 copy.44
  (17 shorter events, 0.0 us)
Async XLA Ops:
  0.6 0.7 copy-start.10
  1.3 0.7 copy-start.6
  1.3 0.7 copy-start.7
  2.0 0.7 copy-start.8
  2.0 0.7 copy-start.9
  286.8 2.0 copy-start
  288.8 1.0 copy-start.14
  288.8 1.5 copy-start.4
  288.8 2.3 copy-start.5
  289.7 2.5 copy-start.3
  291.0 0.7 copy-start.13
  292.3 1.5 copy-start.2
  293.8 1.5 copy-start.1
  295.3 0.9 copy-start.12
  296.2 0.6 copy-start.11

commit v4 on v3

--- a/solution.py
+++ b/solution.py
@@ -369,27 +369,83 @@
     return lambda: pl.semaphore_wait(barrier, len(found))
 
 
-def spread_start(src, spot, ss, rs):
+def spread_small(src, spot, ss, rs):
     x, c, z, y = place()
     slot = 2 * x + c
     for k, (dx, dy) in enumerate(((1, 1), (1, 0), (0, 1))):
-        send(src, spot, ss.at[k], rs.at[slot], dev(flip(x, dx), y, z, flip(y, dy)))
+        send(src, spot, ss.at[k], rs.at[slot, 0], dev(flip(x, dx), y, z, flip(y, dy)))
 
     @pl.when(c == y)
     def _():
-        pltpu.make_async_copy(src, spot, rs.at[slot]).start()
+        pltpu.make_async_copy(src, spot, rs.at[slot, 0]).start()
 
     @pl.when(c != y)
     def _():
-        send(src, spot, ss.at[3], rs.at[slot], dev(x, y, z, y))
-
-
-def spread_wait(block, rs):
+        send(src, spot, ss.at[3], rs.at[slot, 0], dev(x, y, z, y))
+
+
+def spread_start(src, full, ss, rs):
+    x, c, z, y = place()
+    slot = 2 * x + c
+    spot = rows_of(full, slot, BLK)
+    send(src, spot, ss.at[0], rs.at[slot, 0], dev(1 - x, y, z, y))
+    send(src, spot, ss.at[1], rs.at[slot, 0], dev(x, y, z, 1 - y))
+
+    @pl.when(c == y)
+    def _():
+        pltpu.make_async_copy(src, spot, rs.at[slot, 0]).start()
+
+    @pl.when(c != y)
+    def _():
+        send(src, spot, ss.at[2], rs.at[slot, 0], dev(x, y, z, y))
+
+
+def spread_pass(full, ss, rs):
+    x, c, z, y = place()
+    for side in range(2):
+
+        @pl.when((c == y) if side == 0 else (c != y))
+        def _():
+            for k in range(2):
+                slot = 2 * ((1 - x) if side == 0 else x) + k
+                arrived(rows_of(full, slot, BLK), rs.at[slot, 0])
+                half = full.at[many(slot * BLK + side * (BLK // 2), BLK // 2)]
+                target = dev(x, c, z, 1 - y) if side == 0 else dev(1 - x, c, z, y)
+                send(half, half, ss.at[3 + k], rs.at[slot, side], target)
+
+
+def spread_wait(full, rs):
+    x, c, z, y = place()
+
+    @pl.when(c == y)
+    def _():
+        for k in range(2):
+            arrived(rows_of(full, 0, BLK), rs.at[2 * x + k, 0])
+
+    @pl.when(c != y)
+    def _():
+        for k in range(2):
+            for side in range(2):
+                arrived(rows_of(full, 0, BLK // 2), rs.at[2 * (1 - x) + k, side])
+
+
+def spread_sent(src, ss):
+    x, c, z, y = place()
+    for k in range(2):
+        arrived(src, ss.at[k])
+        arrived(src.at[pl.ds(0, BLK // 2)], ss.at[3 + k])
+
+    @pl.when(c != y)
+    def _():
+        arrived(src, ss.at[2])
+
+
+def small_wait(block, rs):
     for j in range(4):
-        arrived(block, rs.at[j])
-
-
-def spread_sent(src, ss):
+        arrived(block, rs.at[j, 0])
+
+
+def small_sent(src, ss):
     x, c, z, y = place()
     for k in range(3):
         arrived(src, ss.at[k])
@@ -408,45 +464,70 @@
     return 2 * flip(x, dx) + flip(c, dc)
 
 
-def collect_start(order, partial, inbox, ss, rs):
+def collect_halves(partial, helper, ss, hs):
     x, c, z, y = place()
-    dx, dc = BLOCK_ORDER[order]
-    src = rows_of(partial, block_at(order), BLK)
-    slot = 2 * x + y
-    spot = inbox.at[slot]
-    target = dev(flip(x, dx), flip(c, dc), z, c)
-    if dx or dc:
-        send(src, spot, ss.at[order], rs.at[slot], target)
-        return
+
+    @pl.when(c != y)
+    def _():
+        for k in range(2):
+            row = (2 * (1 - x) + k) * BLK
+            for side, target in enumerate((dev(1 - x, c, z, y), dev(x, c, z, 1 - y))):
+                half = partial.at[many(row + side * (BLK // 2), BLK // 2)]
+                send(half, helper.at[k], ss.at[2 * k + side], hs.at[k], target)
+
+
+def collect_near(partial, inbox, ss, rs):
+    x, c, z, y = place()
 
     @pl.when(c == y)
     def _():
-        pltpu.make_async_copy(src, spot, rs.at[slot]).start()
+        own = rows_of(partial, 2 * x + c, BLK)
+        other = rows_of(partial, 2 * x + 1 - c, BLK)
+        pltpu.make_async_copy(own, inbox.at[0], rs.at[0]).start()
+        send(other, inbox.at[0], ss.at[0], rs.at[0], dev(x, 1 - c, z, y))
+
+
+def collect_far(partial, helper, inbox, ss, rs, hs):
+    x, c, z, y = place()
+    for k in range(2):
+        arrived(helper.at[k], hs.at[k])
+    for side in range(2):
+
+        @pl.when((c != y) if side == 0 else (c == y))
+        def _():
+            tx = x if side == 0 else 1 - x
+            slot = 2 if side == 0 else 1
+            for k in range(2):
+                row = (2 * tx + k) * BLK
+                rows = many(row + side * (BLK // 2), BLK // 2)
+                partial[rows, :] = (partial[rows, :].astype(F32) + helper[k].astype(F32)).astype(BF)
+                send(
+                    partial.at[many(row, BLK)], inbox.at[slot], ss.at[4 + k], rs.at[slot], dev(tx, k, z, c)
+                )
+
+
+def collect_wait(inbox, rs):
+    for j in range(3):
+        arrived(inbox.at[j], rs.at[j])
+
+
+def collect_sent(inbox, helper, ss):
+    x, c, z, y = place()
+    for k in range(2):
+        arrived(inbox.at[0], ss.at[4 + k])
+
+    @pl.when(c == y)
+    def _():
+        arrived(inbox.at[0], ss.at[0])
 
     @pl.when(c != y)
     def _():
-        send(src, spot, ss.at[order], rs.at[slot], target)
-
-
-def collect_wait(inbox, rs):
-    for j in range(4):
-        arrived(inbox.at[j], rs.at[j])
-
-
-def collect_sent(inbox, ss):
-    x, c, z, y = place()
-    for k in range(3):
-        arrived(inbox.at[0], ss.at[k])
-
-    @pl.when(c != y)
-    def _():
-        arrived(inbox.at[0], ss.at[3])
+        for k in range(4):
+            arrived(helper.at[0], ss.at[k])
 
 
 def inbox_sum(inbox):
-    return (inbox[0].astype(F32) + inbox[1].astype(F32)) + (
-        inbox[2].astype(F32) + inbox[3].astype(F32)
-    )
+    return inbox[0].astype(F32) + inbox[1].astype(F32) + inbox[2].astype(F32)
 
 
 def mm(left, right):
@@ -468,11 +549,11 @@
 
 def layer_body(
     tok, cot, small, wq, wo, wg, wu, wd,
-    act_o, dtok_o, ga_o, gqkv_o, go_o, gf_o, gate_o, up_o, down_o, gq_o, gk_o,
-    wap, smallf, xf, n1, wav, w3, dyf, n2f, part, inbox, stage, active, dgu,
+    act_o, dtok_o, end_f, end_a, vr,
+    wap, smallf, xf, n1, wav, w3, dyf, n2f, part, inbox, helper, active, dgu,
     qkvt, dqkvt, dqkv, qt, kt, kk, vt, vv, lse, att, cs, grow, hid, blk, dot_s, dkt, dvt,
-    help_f, come_f, end_f, help_a, come_a, end_a, arecv, vec, vecr, vr, gp2,
-    sp_ss, sp_rs, co_ss, co_rs, w_ss, w_rs, l_ss, l_rs, c_ss, c_rs, g_ss, g_rs, h_ss, h_rs, o_ss, o_rs, p_ss, p_rs, v_ss, v_rs, loc,
+    help_f, come_f, help_a, come_a, arecv, vec, vecr, gp2,
+    sp_ss, sp_rs, co_ss, co_rs, co_hs, w_ss, w_rs, l_ss, l_rs, c_ss, c_rs, g_ss, g_rs, h_ss, h_rs, o_ss, o_rs, p_ss, p_rs, v_ss, v_rs,
     ready,
 ):
     x, c, z, y = place()
@@ -666,16 +747,24 @@
             lambda t: end_f.at[t, :, lanes],
         )
 
-    def att_grad(kind):
-        lanes = pl.ds(ATT_LO[kind], ATT_WIDE[kind])
-        return grad(
-            kind, arecv, 0, ATT_LO[kind], ATT_WIDE[kind],
-            lambda i, tx: help_a.at[i, pl.ds(tx * 2 * BR, 2 * BR), lanes],
-            lambda i, tx: come_a.at[i, pl.ds(tx * 2 * BR, 2 * BR), lanes],
-            lambda t: end_a.at[t, :, lanes],
+    GA = grad(
+        2, arecv, 0, 0, FFS,
+        lambda i, tx: help_a.at[i, pl.ds(tx * 2 * BR, 2 * BR)],
+        lambda i, tx: come_a.at[i, pl.ds(tx * 2 * BR, 2 * BR)],
+        lambda t: end_a.at[t],
+    )
+    F0, F1 = ffn_grad(0), ffn_grad(1)
+
+    def collect_step(order, side, kind):
+        if order == 1:
+            collect_halves(part.at[side], helper.at[side], co_ss.at[kind], co_hs.at[kind])
+        if order == 3:
+            collect_near(part.at[side], inbox.at[side], co_ss.at[kind], co_rs.at[kind])
+
+    def collect_last(side, kind):
+        collect_far(
+            part.at[side], helper.at[side], inbox.at[side], co_ss.at[kind], co_rs.at[kind], co_hs.at[kind]
         )
-
-    F0, F1, GO, GQ = ffn_grad(0), ffn_grad(1), att_grad(2), att_grad(3)
 
     everyone_here = greet(x, c, z, y)
     turned = jnp.transpose(small[...])
@@ -687,19 +776,19 @@
         wap[t, :, 320:448] = wq[:, QW + 64 * t : QW + 64 * t + 128]
         wap[t, :, 448:576] = wq[:, QW + KW + 64 * t : QW + KW + 64 * t + 128]
         wap[t, :, 576:640] = gains.astype(BF)
-        wap[t, :, 640:960] = wo[:, 320 * t : 320 * t + 320]
-        wap[t, :, 960:1024] = jnp.zeros((BR, 64), BF)
+        wap[t, :, 640:704] = jnp.zeros((BR, 64), BF)
+        wap[t, :, 704:1024] = wo[:, 320 * t : 320 * t + 320]
     everyone_here()
     weights_start(QKV_M)
     spot = smallf.at[:, many((2 * x + c) * BLK, BLK)]
-    spread_start(small, spot, sp_ss.at[SMALL], sp_rs.at[SMALL])
+    spread_small(small, spot, sp_ss.at[SMALL], sp_rs.at[SMALL])
     weights_start(OUT_M)
-    spread_start(tok, rows_of(xf, 2 * x + c, BLK), sp_ss.at[TOK], sp_rs.at[TOK])
+    spread_start(tok, xf, sp_ss.at[TOK], sp_rs.at[TOK])
     weights_start(F0_M)
     weights_start(F1_M)
     weights_line(QKV_M)
     weights_line(OUT_M)
-    spread_wait(spot, sp_rs.at[SMALL])
+    small_wait(spot, sp_rs.at[SMALL])
     seg_row = smallf[4:5, :]
     seg_col = jnp.transpose(smallf[...])[:, 4:5]
     key_at = lax.broadcasted_iota(jnp.int32, (LEN4, LEN4), 0)
@@ -712,13 +801,14 @@
     cs[32:64, :] = jnp.sin(angles)
     weights_pass_near(QKV_M)
     weights_pass_near(OUT_M)
+    spread_pass(xf, sp_ss.at[TOK], sp_rs.at[TOK])
+    weights_line(F0_M)
     weights_pass_far(QKV_M)
     weights_pass_far(OUT_M)
-    weights_line(F0_M)
     weights_line(F1_M)
     weights_swap(QKV_M)
-    spread_wait(rows_of(xf, 0, BLK), sp_rs.at[TOK])
-    spread_start(cot, rows_of(dyf, 2 * x + c, BLK), sp_ss.at[COT], sp_rs.at[COT])
+    spread_wait(xf, sp_rs.at[TOK])
+    spread_start(cot, dyf, sp_ss.at[COT], sp_rs.at[COT])
     weights_wait(QKV_M)
     grow[...] = jnp.transpose(wav[:, 512:640].astype(F32))[64:72, :]
 
@@ -755,7 +845,8 @@
         vt[g] = value.astype(BF)
         vv[g] = jnp.transpose(value).astype(BF)
     weights_swap(OUT_M)
-    dqkvt[QS * 64 : 384, :] = jnp.zeros((384 - QS * 64, LEN4), F32)
+    spread_pass(dyf, sp_ss.at[COT], sp_rs.at[COT])
+    dqkvt[0:64, :] = jnp.zeros((64, LEN4), F32)
     for h in range(QS):
         g = group_of(h)
         scores = jnp.where(allowed, mm(kk[g], qt[h]) * SCALE, NEG)
@@ -763,17 +854,19 @@
         weights = jnp.exp(scores - top)
         total = jnp.sum(weights, axis=0, keepdims=True)
         lse[h : h + 1, :] = top + jnp.log(total)
-        dqkvt[h * 64 : h * 64 + 64, :] = mm(vt[g], (weights / total).astype(BF))
+        dqkvt[h * 64 + 64 : h * 64 + 128, :] = mm(vt[g], (weights / total).astype(BF))
     att[...] = jnp.transpose(dqkvt[0:384, :]).astype(BF)
     weights_pass_near(F0_M)
     weights_wait(OUT_M)
     for order in range(4):
         rows = many(block_at(order) * BLK, BLK)
         part[0, rows, :] = mm_nt(att[rows, :], wav[:, QKV_W:AW]).astype(BF)
-        collect_start(order, part.at[0], inbox.at[0], co_ss.at[OUT], co_rs.at[OUT])
+        collect_step(order, 0, OUT)
+    collect_last(0, OUT)
     weights_pass_near(F1_M)
     weights_pass_far(F0_M)
     collect_wait(inbox.at[0], co_rs.at[OUT])
+    spread_sent(tok, sp_ss.at[TOK])
     hidden = tok[...].astype(F32) + inbox_sum(inbox.at[0])
     hid[...] = hidden
     blk[0] = (
@@ -781,11 +874,12 @@
         * lax.rsqrt(jnp.mean(hidden * hidden, axis=1, keepdims=True) + norm_eps)
         * grow[1:2, :]
     ).astype(BF)
-    spread_start(blk.at[0], rows_of(n2f, 2 * x + c, BLK), sp_ss.at[N2], sp_rs.at[N2])
+    spread_start(blk.at[0], n2f, sp_ss.at[N2], sp_rs.at[N2])
+    spread_pass(n2f, sp_ss.at[N2], sp_rs.at[N2])
     weights_pass_far(F1_M)
     weights_swap(F0_M)
-    spread_wait(rows_of(dyf, 0, BLK), sp_rs.at[COT])
-    spread_wait(rows_of(n2f, 0, BLK), sp_rs.at[N2])
+    spread_wait(dyf, sp_rs.at[COT])
+    spread_wait(n2f, sp_rs.at[N2])
     weights_wait(F0_M)
 
     def hidden_units(j):
@@ -855,7 +949,8 @@
 
     every = slice(0, LEN4)
     hidden_units(0)
-    collect_sent(inbox.at[0], co_ss.at[OUT])
+    collect_sent(inbox.at[0], helper.at[0], co_ss.at[OUT])
+    spread_sent(cot, sp_ss.at[COT])
 
     @pl.loop(0, 8)
     def _(j):
@@ -877,7 +972,9 @@
             wide = many(j * 512, 512)
             part[1, rows, wide] = (part[1, rows, wide].astype(F32) + dn_part(1, rows, wide)).astype(BF)
 
-        collect_start(order, part.at[1], inbox.at[1], co_ss.at[DN], co_rs.at[DN])
+        collect_step(order, 1, DN)
+
+    collect_last(1, DN)
 
     @pl.loop(0, 8)
     def _(j):
@@ -898,52 +995,45 @@
     dh = cot[...].astype(F32) + r * (a - h * (r * r * jnp.mean(a * h, axis=1, keepdims=True)))
     dtok_o[...] = dh
     blk[1] = dh.astype(BF)
-    spread_start(blk.at[1], rows_of(xf, 2 * x + c, BLK), sp_ss.at[DAB], sp_rs.at[DAB])
-    for order in range(4):
-        collect_start(order, part.at[0], inbox.at[0], co_ss.at[YY], co_rs.at[YY])
-    finish(F0)
-    join(F1, 0)
-    def att_grads(core, row, kind):
+    spread_start(blk.at[1], xf, sp_ss.at[DAB], sp_rs.at[DAB])
+    spread_pass(xf, sp_ss.at[DAB], sp_rs.at[DAB])
+    collect_step(1, 0, YY)
+    collect_step(3, 0, YY)
+    def att_grads(core, row):
         wide = many((2 * lax.div(row, 2) + core) * HALF + lax.rem(row, 2) * 256, 256)
-        if kind == 3:
-            return mm_tn(n1[:, wide], dqkv[...])
-        return mm_tn(xf[:, wide], att[...])
-
-    att_lanes = {k: pl.ds(ATT_LO[k], ATT_WIDE[k]) for k in (2, 3)}
-
-    def att_grads_swap(kind):
+        one, two = mm_tn(n1[:, wide], dqkv[...]), mm_tn(xf[:, wide], att[...])
+        return one[:, 0:512], one[:, 512:640] + two[:, 0:128], two[:, 128:384]
+
+    def att_grads_swap():
         @pl.loop(0, 4)
         def _(row):
-            side = lax.div(row, 2) * AW + ATT_LO[kind]
-            dyf[many(lax.rem(row, 2) * 256, 256), pl.ds(pl.multiple_of(side, 128), ATT_WIDE[kind])] = (
-                att_grads(1 - c, row, kind).astype(BF)
-            )
+            rows = many(lax.rem(row, 2) * 256, 256)
+            side = lax.div(row, 2) * AW
+            one, both, two = att_grads(1 - c, row)
+            dyf[rows, pl.ds(pl.multiple_of(side, 128), 512)] = one.astype(BF)
+            dyf[rows, pl.ds(pl.multiple_of(side + 512, 128), 128)] = both.astype(BF)
+            dyf[rows, pl.ds(pl.multiple_of(side + 640, 128), 256)] = two.astype(BF)
 
         for side in range(2):
             send(
-                dyf.at[:, pl.ds(side * AW + ATT_LO[kind], ATT_WIDE[kind])],
-                arecv.at[pl.ds(side * HALF, HALF), att_lanes[kind]],
-                g_ss.at[2 * kind - 2 + side],
-                g_rs.at[2 * kind - 2 + side],
-                sibling,
+                dyf.at[:, pl.ds(side * AW, FFS)], arecv.at[pl.ds(side * HALF, HALF)],
+                g_ss.at[2 + side], g_rs.at[2 + side], sibling,
             )
 
-    def att_grads_own(kind):
+    def att_grads_own():
         for side in range(2):
-            arrived(arecv.at[pl.ds(0, HALF), att_lanes[kind]], g_rs.at[2 * kind - 2 + side])
+            arrived(arecv.at[pl.ds(0, HALF)], g_rs.at[2 + side])
 
         @pl.loop(0, 4)
         def _(row):
             rows = many(row * 256, 256)
-            arecv[rows, att_lanes[kind]] = (
-                att_grads(c, row, kind) + arecv[rows, att_lanes[kind]].astype(F32)
-            ).astype(BF)
-
-    spread_wait(rows_of(xf, 0, BLK), sp_rs.at[DAB])
-    att_grads_swap(2)
+            one, both, two = att_grads(c, row)
+            arecv[rows, 0:512] = (one + arecv[rows, 0:512].astype(F32)).astype(BF)
+            arecv[rows, 512:640] = (both + arecv[rows, 512:640].astype(F32)).astype(BF)
+            arecv[rows, 640:896] = (two + arecv[rows, 640:896].astype(F32)).astype(BF)
+
+    spread_wait(xf, sp_rs.at[DAB])
     dot_s[...] = jnp.transpose(mm(xf[...], wav[:, QKV_W:AW]).astype(BF).astype(F32)).astype(BF)
-    att_grads_own(2)
-    start(GO)
     dkt[...] = jnp.zeros_like(dkt)
     dvt[...] = jnp.zeros_like(dvt)
 
@@ -962,7 +1052,7 @@
         g = group_of(h)
         scores = mm(kk[g], qt[h]) * SCALE
         p = jnp.where(allowed, jnp.exp(scores - lse[h : h + 1, :]), 0.0)
-        d_out = dot_s[h * 64 : h * 64 + 64, :]
+        d_out = dot_s[h * 64 + 64 : h * 64 + 128, :]
         dvt[g] += mm_nt(d_out, p.astype(BF))
         dp = mm(vv[g], d_out)
         ds = (p * (dp - jnp.sum(p * dp, axis=0, keepdims=True))).astype(BF)
@@ -972,7 +1062,7 @@
         dq_gain = dq_gain + more
         dqkvt[h * 64 : h * 64 + 64, :] = d
         for g_at, i in JOIN_AFTER.get(h, ()):
-            join((F0, F1, GO, GQ)[g_at], i)
+            join((F0, F1)[g_at], i)
     dk_gain = jnp.zeros((64, 1), F32)
     for g in range(2):
         base = QS * 64 + g * 64
@@ -983,20 +1073,24 @@
         dqkvt[base + 128 : base + 192, :] = dvt[g]
     dqkvt[576:640, :] = jnp.zeros((64, LEN4), F32)
     dqkv[...] = jnp.transpose(dqkvt[...]).astype(BF)
-    collect_sent(inbox.at[1], co_ss.at[DN])
+    att_grads_swap()
+    collect_sent(inbox.at[1], helper.at[1], co_ss.at[DN])
     for order in range(4):
         rows = many(block_at(order) * BLK, BLK)
         part[1, rows, :] = mm_nt(dqkv[rows, :], wav[:, 0:QKV_W]).astype(BF)
-        collect_start(order, part.at[1], inbox.at[1], co_ss.at[DT], co_rs.at[DT])
-
-    att_grads_swap(3)
-    att_grads_own(3)
-    start(GQ)
-    join(GO, 0)
-    join(GO, 1)
+        collect_step(order, 1, DT)
+
+    join(F1, 1)
+    att_grads_own()
+    start(GA)
+    finish(F0)
+    collect_last(1, DT)
+    collect_last(0, YY)
     finish(F1)
     collect_wait(inbox.at[0], co_rs.at[YY])
     act_o[...] = (hid[...] + inbox_sum(inbox.at[0])).astype(BF)
+    join(GA, 0)
+    join(GA, 1)
     collect_wait(inbox.at[1], co_rs.at[DT])
     dn = inbox_sum(inbox.at[1])
     xv = tok[...].astype(F32)
@@ -1031,37 +1125,46 @@
                     pltpu.make_async_copy(src, vr.at[source], v_rs.at[source]).start()
                 else:
                     send(src, vr.at[source], v_ss.at[k], v_rs.at[source], dev(tx, c, tz, ty))
-    join(GQ, 0)
-    join(GQ, 1)
-    finish(GO)
-    leave = []
-    for g in (F0, F1):
-        final_wait(g)
-    for j, out in enumerate((gate_o, up_o, down_o)):
-        for t in range(4):
-            rows = pl.ds(t * BR, BR)
-            if j > 0:
-                leave[4 * (j - 1) + t].wait()
-            for first, width in CHUNKS:
-                at = 3 * first + j * width
-                stage[rows, first : first + width] = end_f[t, :, at : at + width].astype(F32)
-            leave.append(
-                pltpu.make_async_copy(
-                    stage.at[rows], out.at[:, pl.ds(t * FFS, FFS)], loc.at[4 * j + t]
-                )
-            )
-            leave[-1].start()
-    finish(GQ)
+    finish(GA)
     for i in range(4 * DZ):
         arrived(vr.at[0], v_rs.at[i])
+    for g in (F0, F1, GA):
+        final_wait(g)
+    for g in (F0, F1, GA):
+        grad_sent(g)
+    weights_sent(QKV_M)
+    weights_sent(OUT_M)
+    for i in range(1, 4 * DZ):
+        arrived(vr.at[0], v_ss.at[i])
+    for j in range(2):
+        arrived(w3.at[pl.ds(0, 1024), chunk_lanes(j)[2]], g_ss.at[j])
+    for side in range(2):
+        arrived(arecv.at[pl.ds(0, HALF)], g_ss.at[2 + side])
+    arrived(vecr, g_ss.at[6])
+    small_sent(small, sp_ss.at[SMALL])
+    spread_sent(blk.at[0], sp_ss.at[N2])
+    spread_sent(blk.at[1], sp_ss.at[DAB])
+    collect_sent(inbox.at[0], helper.at[0], co_ss.at[YY])
+    collect_sent(inbox.at[1], helper.at[1], co_ss.at[DT])
+
+
+JOIN_AFTER = {1: ((1, 0),)}
+
+
+def results_body(
+    act, dtok, end_f, end_a, vr, act_o, dtok_o, ga_o, gqkv_o, go_o, gf_o, gate_o, up_o, down_o, gq_o, gk_o
+):
+    act_o[...] = act[...]
+    dtok_o[...] = dtok[...]
     sums = jnp.sum(vr[...], axis=0)
     for i, out in enumerate((ga_o, gf_o, gq_o, gk_o)):
         out[...] = sums[i : i + 1, 0:64]
-    final_wait(GO)
     for t in range(4):
-        go_o[:, 320 * t : 320 * t + 320] = end_a[t, :, 640:960].astype(F32)
-    final_wait(GQ)
-    for t in range(4):
+        for j, out in enumerate((gate_o, up_o, down_o)):
+            for first, width in CHUNKS:
+                at = 3 * first + j * width
+                out[:, t * FFS + first : t * FFS + first + width] = end_f[t, :, at : at + width].astype(F32)
+        go_o[:, 320 * t : 320 * t + 320] = end_a[t, :, 576:896].astype(F32)
         gqkv_o[:, 320 * t : 320 * t + 320] = end_a[t, :, 0:320].astype(F32)
     for lo, to in ((320, QW), (448, QW + KW)):
         for g in range(5):
@@ -1071,32 +1174,6 @@
             if g > 0:
                 parts.append(end_a[g - 1, :, lo + 64 : lo + 128].astype(F32))
             gqkv_o[:, to + 64 * g : to + 64 * g + 64] = sum(parts[1:], parts[0])
-    for copy in leave[8:]:
-        copy.wait()
-    for g in (F0, F1, GO, GQ):
-        grad_sent(g)
-    weights_sent(QKV_M)
-    weights_sent(OUT_M)
-    for i in range(1, 4 * DZ):
-        arrived(vr.at[0], v_ss.at[i])
-    for j in range(2):
-        arrived(w3.at[pl.ds(0, 1024), chunk_lanes(j)[2]], g_ss.at[j])
-    for j in (2, 3):
-        for side in range(2):
-            arrived(arecv.at[pl.ds(0, HALF), att_lanes[j]], g_ss.at[2 * j - 2 + side])
-    arrived(vecr, g_ss.at[6])
-    spread_sent(small, sp_ss.at[SMALL])
-    spread_sent(tok, sp_ss.at[TOK])
-    spread_sent(cot, sp_ss.at[COT])
-    spread_sent(blk.at[0], sp_ss.at[N2])
-    spread_sent(blk.at[1], sp_ss.at[DAB])
-    collect_sent(inbox.at[0], co_ss.at[YY])
-    collect_sent(inbox.at[1], co_ss.at[DT])
-
-
-JOIN_AFTER = {4: ((1, 1),)}
-ATT_LO = {2: QKV_W, 3: 0}
-ATT_WIDE = {2: AW - QKV_W, 3: QKV_W}
 
 
 def plane_plan(
@@ -1117,23 +1194,17 @@
     dma = pltpu.SemaphoreType.DMA
     vm = pltpu.VMEM
     far, close = pl.BlockSpec(memory_space=pl.ANY), pl.BlockSpec(memory_space=pltpu.VMEM)
-    outs = pl.pallas_call(
+    halves = pl.pallas_call(
         layer_body,
         out_shape=[
             jax.ShapeDtypeStruct((BLK, width), BF),
             jax.ShapeDtypeStruct((BLK, width), F32),
-            jax.ShapeDtypeStruct((1, BR), F32),
-            jax.ShapeDtypeStruct(w_qkv.shape, F32),
-            jax.ShapeDtypeStruct(w_out.shape, F32),
-            jax.ShapeDtypeStruct((1, BR), F32),
-            jax.ShapeDtypeStruct(w_gate.shape, F32),
-            jax.ShapeDtypeStruct(w_up.shape, F32),
-            jax.ShapeDtypeStruct(w_down.shape, F32),
-            jax.ShapeDtypeStruct((1, HD), F32),
-            jax.ShapeDtypeStruct((1, HD), F32),
+            jax.ShapeDtypeStruct((4, BR, 3 * FFS), BF),
+            jax.ShapeDtypeStruct((4, BR, FFS), BF),
+            jax.ShapeDtypeStruct((4 * DZ, 8, BLK), F32),
         ],
         in_specs=[close] * 5 + [far] * 3,
-        out_specs=[close] * 6 + [far] * 3 + [close] * 2,
+        out_specs=[close] * 2 + [far] * 3,
         scratch_shapes=[
             vm((4, BR, AW), BF),
             vm((8, LEN4), F32),
@@ -1144,8 +1215,8 @@
             vm((LEN4, width), BF),
             vm((LEN4, width), BF),
             vm((2, LEN4, width), BF),
-            vm((2, 4, BLK, width), BF),
-            vm((4 * BR, FFS), F32),
+            vm((2, 3, BLK, width), BF),
+            vm((2, 2, BLK // 2, width), BF),
             vm((LEN4, FFS), BF),
             vm((LEN4, 2 * FFS), BF),
             vm((QKV_W, LEN4), F32),
@@ -1167,24 +1238,20 @@
             vm((2, 64, LEN4), F32),
             vm((2, 4 * BR, 3 * FFS), BF),
             vm((2, 4 * BR, 3 * FFS), BF),
-            vm((4, BR, 3 * FFS), BF),
-            vm((2, 4 * BR, AW), BF),
-            vm((2, 4 * BR, AW), BF),
-            vm((4, BR, AW), BF),
-            vm((1024, AW), BF),
+            vm((2, 4 * BR, FFS), BF),
+            vm((2, 4 * BR, FFS), BF),
+            vm((1024, FFS), BF),
             vm((2, 4 * DZ, 8, BLK), F32),
             vm((4 * DZ, 8, BLK), F32),
-            vm((4 * DZ, 8, BLK), F32),
             vm((8, width), F32),
-            dma((5, 4)), dma((5, 4)),
-            dma((4, 4)), dma((4, 4)),
+            dma((5, 5)), dma((5, 4, 2)),
+            dma((4, 6)), dma((4, 3)), dma((4, 2)),
             dma((5, 3)), dma((5, 4)), dma((5, 10)), dma((5, 8)),
             dma((5, 2)), dma((5, 2)),
             dma((8,)), dma((8,)),
             dma((5, 4)), dma((5, 4)),
             dma((5, 6)), dma((5, 4)), dma((5, 3)), dma((5, 4)),
             dma((16,)), dma((16,)),
-            dma((12,)),
             pltpu.SemaphoreType.REGULAR((2,)),
         ],
         compiler_params=pltpu.CompilerParams(
@@ -1193,6 +1260,25 @@
     )(
         tokens.reshape(BLK, width), cotangent.reshape(BLK, width), small, w_qkv, w_out, w_gate, w_up, w_down
     )
+    outs = pl.pallas_call(
+        results_body,
+        out_shape=[
+            jax.ShapeDtypeStruct((BLK, width), BF),
+            jax.ShapeDtypeStruct((BLK, width), F32),
+            jax.ShapeDtypeStruct((1, BR), F32),
+            jax.ShapeDtypeStruct(w_qkv.shape, F32),
+            jax.ShapeDtypeStruct(w_out.shape, F32),
+            jax.ShapeDtypeStruct((1, BR), F32),
+            jax.ShapeDtypeStruct(w_gate.shape, F32),
+            jax.ShapeDtypeStruct(w_up.shape, F32),
+            jax.ShapeDtypeStruct(w_down.shape, F32),
+            jax.ShapeDtypeStruct((1, HD), F32),
+            jax.ShapeDtypeStruct((1, HD), F32),
+        ],
+        in_specs=[close] * 5,
+        out_specs=[close] * 11,
+        compiler_params=pltpu.CompilerParams(vmem_limit_bytes=60 * 2**20),
+    )(*halves)
     shapes = (
         tokens.shape, tokens.shape, (BR,), w_qkv.shape, w_out.shape, (BR,), w_gate.shape, w_up.shape, w_down.shape,
         (HD,), (HD,),

time: 298 us -> 287 us (0.963)
  local copies, waits for them, and re-layouts: 13.1 us -> 0.62 us
    unnamed x41 -> x0, local copies, waits for them, and re-layouts: 12.5 us -> none
    pallas_call x1, Pallas kernels: 283 us -> 279 us  [plane_plan(): pl.pallas_call(layer_body, out_shape=[jax.ShapeDtypeStruct((BLK, width),...]
    pallas_call x0 -> x1, Pallas kernels: none -> 4.51 us  [plane_plan(): pl.pallas_call(results_body, out_shape=[jax.ShapeDtypeStruct((BLK, width)...]
where the time goes in v4:
time: 287 us; the launch traced here: 286 us
  Pallas kernels  283 us (99%)
    pallas_call x1, Pallas kernels, plane_plan(): pl.pallas_call(layer_body, out_shape=[jax.ShapeDtypeStruct((BLK, width),...  279 us

profile of v4, /device:TPU:1, one launch (start us, length us, event | category | flops | bytes accessed | tf_op | source)
XLA Modules:
  0.0 286.4 jit_solution(11668011056541938023)
XLA Ops:
  0.6 0.7 convert_element_type.14
  1.3 0.7 pad_convert_fusion.2
  2.0 0.7 pad_convert_fusion
  2.7 0.6 concatenate.3.small
  3.3 278.6 %shard_map.203 = (bf16[128,2048]{1,0:T(8,128)(2,1)}, f32[128,2048]{1,0:T(8,128)}, bf16[4,64,2688]{2,1,0:T(8,128)(2,1)}, bf16[4,64,896]{2,1,0:T(8,128)(2,1)}, f32[16,8,128]{2,1,0:T(8,128)}) custom-call(bf16[128,2048]{1,0:T(8,128)(2,1)} %bitcast.12, bf16[128,2048]{1,0:T(8,128)(2,1)} %bitcast.13, f32[8,128]{1,0:T(8,128)} %concatenate.3.small, ...), custom_call_target="tpu_custom_call" | custom-call | tf_op jit(solution)/shard_map/pallas_call | solution.py:1197
  281.9 4.5 %shard_map.204 = (bf16[128,2048]{1,0:T(8,128)(2,1)}, f32[128,2048]{1,0:T(8,128)}, f32[1,64]{1,0:T(1,128)}, f32[64,1920]{1,0:T(8,128)}, f32[64,1280]{1,0:T(8,128)...) custom-call(bf16[128,2048]{1,0:T(8,128)(2,1)} %get-tuple-element.27., ...), custom_call_target="tpu_custom_call" | custom-call | tf_op jit(solution)/shard_map/pallas_call | solution.py:1263
  (3 shorter events, 0.0 us)

commit v5 on v4

--- a/solution.py
+++ b/solution.py
@@ -952,9 +952,9 @@
     collect_sent(inbox.at[0], helper.at[0], co_ss.at[OUT])
     spread_sent(cot, sp_ss.at[COT])
 
-    @pl.loop(0, 8)
+    @pl.loop(0, 4)
     def _(j):
-        wide = many(j * 256, 256)
+        wide = many(j * 512, 512)
         part[1, :, wide] = dn_part(0, every, wide).astype(BF)
         part[0, :, wide] = y_part(0, every, wide).astype(BF)
 
@@ -974,18 +974,17 @@
 
         collect_step(order, 1, DN)
 
+
+    @pl.loop(0, 4)
+    def _(j):
+        wide = many(j * 512, 512)
+        part[0, :, wide] = (part[0, :, wide].astype(F32) + y_part(1, every, wide)).astype(BF)
+
     collect_last(1, DN)
 
-    @pl.loop(0, 8)
-    def _(j):
-        wide = many(j * 256, 256)
-        part[0, :, wide] = (part[0, :, wide].astype(F32) + y_part(1, every, wide)).astype(BF)
-
     grads_swap(1)
-    join(F0, 0)
     grads_own(1)
     start(F1)
-    join(F0, 1)
     collect_wait(inbox.at[1], co_rs.at[DN])
     dn = inbox_sum(inbox.at[1])
     h = hid[...]
@@ -999,6 +998,8 @@
     spread_pass(xf, sp_ss.at[DAB], sp_rs.at[DAB])
     collect_step(1, 0, YY)
     collect_step(3, 0, YY)
+    join(F0, 0)
+    join(F0, 1)
     def att_grads(core, row):
         wide = many((2 * lax.div(row, 2) + core) * HALF + lax.rem(row, 2) * 256, 256)
         one, two = mm_tn(n1[:, wide], dqkv[...]), mm_tn(xf[:, wide], att[...])
@@ -1083,14 +1084,14 @@
     join(F1, 1)
     att_grads_own()
     start(GA)
+    collect_last(1, DT)
     finish(F0)
-    collect_last(1, DT)
     collect_last(0, YY)
-    finish(F1)
     collect_wait(inbox.at[0], co_rs.at[YY])
     act_o[...] = (hid[...] + inbox_sum(inbox.at[0])).astype(BF)
     join(GA, 0)
     join(GA, 1)
+    finish(F1)
     collect_wait(inbox.at[1], co_rs.at[DT])
     dn = inbox_sum(inbox.at[1])
     xv = tok[...].astype(F32)

time: 287 us -> 283 us (0.986)
  Pallas kernels: 283 us -> 279 us
    pallas_call x1, Pallas kernels: 279 us -> 275 us  [plane_plan(): pl.pallas_call(layer_body, out_shape=[jax.ShapeDtypeStruct((BLK, width),...]
where the time goes in v5:
time: 283 us
  Pallas kernels  279 us (99%)
    pallas_call x1, Pallas kernels, plane_plan(): pl.pallas_call(layer_body, out_shape=[jax.ShapeDtypeStruct((BLK, width),...  275 us

profile of v5, /device:TPU:1, one launch (start us, length us, event | category | flops | bytes accessed | tf_op | source)
XLA Modules:
  0.0 282.8 jit_solution(3934176426819887798)
XLA Ops:
  0.6 0.7 convert_element_type.14
  1.3 0.7 pad_convert_fusion.2
  2.0 0.7 pad_convert_fusion
  2.7 0.6 concatenate.3.small
  3.3 274.9 %shard_map.203 = (bf16[128,2048]{1,0:T(8,128)(2,1)}, f32[128,2048]{1,0:T(8,128)}, bf16[4,64,2688]{2,1,0:T(8,128)(2,1)}, bf16[4,64,896]{2,1,0:T(8,128)(2,1)}, f32[16,8,128]{2,1,0:T(8,128)}) custom-call(bf16[128,2048]{1,0:T(8,128)(2,1)} %bitcast.12, bf16[128,2048]{1,0:T(8,128)(2,1)} %bitcast.13, f32[8,128]{1,0:T(8,128)} %concatenate.3.small, ...), custom_call_target="tpu_custom_call" | custom-call | tf_op jit(solution)/shard_map/pallas_call | solution.py:1198
  278.2 4.5 %shard_map.204 = (bf16[128,2048]{1,0:T(8,128)(2,1)}, f32[128,2048]{1,0:T(8,128)}, f32[1,64]{1,0:T(1,128)}, f32[64,1920]{1,0:T(8,128)}, f32[64,1280]{1,0:T(8,128)...) custom-call(bf16[128,2048]{1,0:T(8,128)(2,1)} %get-tuple-element.27., ...), custom_call_target="tpu_custom_call" | custom-call | tf_op jit(solution)/shard_map/pallas_call | solution.py:1264
  (3 shorter events, 0.0 us)
